TPU v7x, 32 devices: a whole 2x2x4 slice. The times are simulated.
32 devices in a mesh: dp: 4 (over y, x), fsdp: 8 (over z, core).
Axes of the slice: x: 2, y: 2, z: 4, core: 2. Of those that a mesh axis runs over, the one named last changes fastest.
Arguments:
- tokens: bfloat16 [8, 1280, 1536], P('fsdp', 'dp'), may hold values from -6 to 6
- cotangent: bfloat16 [8, 1280, 1536], P('fsdp', 'dp'), may hold values from -12 to 12
- lengths: int32 [8], P('fsdp'), may hold values from 320 to 1280, as said below
- qkv_weight: float32 [1536, 2048], P('dp', 'fsdp'), may hold values from -0.109375 to 0.109375
- qkv_first: float32 [1536, 2048], P('dp', 'fsdp'), may hold values from -0.001953125 to 0.001953125
- qkv_second: float32 [1536, 2048], P('dp', 'fsdp'), may hold values from 1.0684257e-08 to 1.7094811e-07
- out_weight: float32 [1536, 1536], P('dp', 'fsdp'), may hold values from -0.66340347 to 0.66340347
- out_first: float32 [1536, 1536], P('dp', 'fsdp'), may hold values from -0.001953125 to 0.001953125
- out_second: float32 [1536, 1536], P('dp', 'fsdp'), may hold values from 1.0684257e-08 to 1.7094811e-07
- mlp_in_weight: float32 [1536, 17920], P('dp', 'fsdp'), may hold values from -0.15625 to 0.15625
- mlp_in_first: float32 [1536, 17920], P('dp', 'fsdp'), may hold values from -0.001953125 to 0.001953125
- mlp_in_second: float32 [1536, 17920], P('dp', 'fsdp'), may hold values from 1.0684257e-08 to 1.7094811e-07
- down_weight: float32 [8960, 1536], P('dp', 'fsdp'), may hold values from -0.091910525 to 0.091910525
- down_first: float32 [8960, 1536], P('dp', 'fsdp'), may hold values from -0.001953125 to 0.001953125
- down_second: float32 [8960, 1536], P('dp', 'fsdp'), may hold values from 1.0684257e-08 to 1.7094811e-07
- small_params: float32 [8, 640], P('dp', 'fsdp'), may hold values from -2 to 3.5, as said below
- small_first: float32 [8, 640], P('dp', 'fsdp'), may hold values from -0.001953125 to 0.001953125
- small_second: float32 [8, 640], P('dp', 'fsdp'), may hold values from 1.0684257e-08 to 1.7094811e-07
Outputs:
- mixed: bfloat16 [8, 1280, 1536], P('fsdp', 'dp')
- input_grad: bfloat16 [8, 1280, 1536], P('fsdp', 'dp')
- grad_norm: float32 [], replicated
- qkv_new: float32 [1536, 2048], P('dp', 'fsdp')
- qkv_first_new: float32 [1536, 2048], P('dp', 'fsdp')
- qkv_second_new: float32 [1536, 2048], P('dp', 'fsdp')
- qkv_copy: bfloat16 [1536, 2048], P('dp', 'fsdp')
- out_new: float32 [1536, 1536], P('dp', 'fsdp')
- out_first_new: float32 [1536, 1536], P('dp', 'fsdp')
- out_second_new: float32 [1536, 1536], P('dp', 'fsdp')
- out_copy: bfloat16 [1536, 1536], P('dp', 'fsdp')
- mlp_in_new: float32 [1536, 17920], P('dp', 'fsdp')
- mlp_in_first_new: float32 [1536, 17920], P('dp', 'fsdp')
- mlp_in_second_new: float32 [1536, 17920], P('dp', 'fsdp')
- mlp_in_copy: bfloat16 [1536, 17920], P('dp', 'fsdp')
- down_new: float32 [8960, 1536], P('dp', 'fsdp')
- down_first_new: float32 [8960, 1536], P('dp', 'fsdp')
- down_second_new: float32 [8960, 1536], P('dp', 'fsdp')
- down_copy: bfloat16 [8960, 1536], P('dp', 'fsdp')
- small_new: float32 [8, 640], P('dp', 'fsdp')
- small_first_new: float32 [8, 640], P('dp', 'fsdp')
- small_second_new: float32 [8, 640], P('dp', 'fsdp')
- small_copy: bfloat16 [8, 640], P('dp', 'fsdp')
Inputs may be any that keep to these rules, and one draw needn't show every extreme that they name: `lengths`: each row's valid tokens come first; in every draw at least one row is valid over all 1280 tokens. `small_params`: the two gains are positive, the bias has both signs.
All inputs are finite; a program needn't handle non-finite values.
Results may differ from a plain program's by a relative error of at most 0.035.
Values may be sent and summed in bfloat16 or wider, within the bound.
No kernel may reach another device: no remote copies, remote signals or barrier semaphores. Data moves between devices by JAX's collectives and lax.ppermute only.
A program may use at most 512 MiB of HBM per device.

v0:
```python
import jax
import jax.numpy as jnp
from jax import lax
from jax.sharding import PartitionSpec as P

D = 1536
HEADS = 12
KV_HEADS = 2
HEAD = 128
FF = 8960
STEP = 5
GROUP = 6
SMALL = 5120


NORM_EPS = 1e-06
ROPE_BASE = 1000000.0
BETA_FIRST = 0.5
BETA_SECOND = 0.5
ADAM_EPS = 1e-08
MATRIX_RATE = 0.03
SMALL_RATE = 0.3
MATRIX_DECAY = 0.1
CLIP_NORM = 1.0
MASKED = -1e30


def shortened(array):

    def short(part):
        return part.astype(jnp.bfloat16) if part.dtype == jnp.float32 else part

    return jax.tree.map(short, array)


def unpack_small(small_vec):
    grouped = small_vec.reshape(KV_HEADS * HEAD, 3 * GROUP + 2)
    gain_attn = grouped[:, :GROUP].reshape(-1)
    gain_mlp = grouped[:, GROUP : 2 * GROUP].reshape(-1)
    biases = jnp.concatenate(
        [
            grouped[:, 2 * GROUP : 3 * GROUP].reshape(-1),
            grouped[:, 3 * GROUP],
            grouped[:, 3 * GROUP + 1],
        ]
    )
    return (gain_attn, gain_mlp, biases)


def group_small(gain_attn, gain_mlp, biases):
    count = KV_HEADS * HEAD
    pieces = [
        gain_attn.reshape(count, GROUP),
        gain_mlp.reshape(count, GROUP),
        biases[:D].reshape(count, GROUP),
        biases[D : D + count][:, None],
        biases[D + count :][:, None],
    ]
    return jnp.concatenate(pieces, axis=1).reshape(8, SMALL // 8)


def rotate_half(values):
    half_width = HEAD // 2
    return jnp.concatenate([-values[..., half_width:], values[..., :half_width]], axis=-1)


def rope_tables(positions):
    pair_index = jnp.arange(HEAD // 2, dtype=jnp.float32)
    inverse = jnp.power(jnp.float32(ROPE_BASE), -2.0 * pair_index / HEAD)
    angles = positions[:, None] * inverse[None, :]
    angles = jnp.concatenate([angles, angles], axis=-1)
    return (jnp.cos(angles), jnp.sin(angles))


def rms_scale(values):
    return lax.rsqrt(jnp.mean(values * values, axis=-1, keepdims=True) + NORM_EPS)


def contract_first(left, right):
    return lax.dot_general(
        left, right, (((0,), (0,)), ((), ())), preferred_element_type=jnp.float32
    )


def contract_last(left, right):
    return lax.dot_general(
        left, right, (((1,), (1,)), ((), ())), preferred_element_type=jnp.float32
    )


def gather_all(shards):
    lengthened = jax.tree.map(
        lambda part, own: part.astype(own.dtype),
        lax.all_gather(shortened(shards), "dp", axis=0, tiled=True),
        shards,
    )
    return jax.tree.map(
        lambda part, own: part.astype(own.dtype),
        lax.all_gather(shortened(lengthened), "fsdp", axis=1, tiled=True),
        lengthened,
    )


def reduce_all(terms):
    narrowed = jax.tree.map(
        lambda part: part.astype(jnp.float32),
        lax.psum_scatter(shortened(terms), "fsdp", scatter_dimension=1, tiled=True),
    )
    return jax.tree.map(
        lambda part: part.astype(jnp.float32),
        lax.psum_scatter(shortened(narrowed), "dp", scatter_dimension=0, tiled=True),
    )


def update(weight, first, second, gradient, clip_factor, rate, decay):
    step_grad = gradient * clip_factor
    first_new = BETA_FIRST * first + (1.0 - BETA_FIRST) * step_grad
    second_new = BETA_SECOND * second + (1.0 - BETA_SECOND) * step_grad * step_grad
    first_fix = 1.0 - BETA_FIRST**STEP
    second_fix = 1.0 - BETA_SECOND**STEP
    weight_new = weight - rate * (
        first_new / first_fix / (jnp.sqrt(second_new / second_fix) + ADAM_EPS) + decay * weight
    )
    return (weight_new, first_new, second_new, weight_new.astype(jnp.bfloat16))


def sharded_pass(tokens, cotangent, lengths, half_qkv, half_out, half_in, half_down, half_small):
    local_rows = tokens.shape[1]
    seq_len = local_rows * lax.axis_size("dp")
    kv_width = KV_HEADS * HEAD
    score_scale = HEAD ** (-0.5)
    qkv_full, out_full, small_full = gather_all((half_qkv, half_out, half_small))
    small_vec = small_full.reshape(-1).astype(jnp.float32)
    gain_attn, gain_mlp, biases = unpack_small(small_vec)
    inputs = tokens[0].astype(jnp.float32)
    query_places = lax.axis_index("dp") * local_rows + jnp.arange(local_rows, dtype=jnp.int32)
    key_places = jnp.arange(seq_len, dtype=jnp.int32)
    row_length = lengths[0]
    cosine, sine_table = rope_tables(query_places.astype(jnp.float32))
    cosine = cosine[:, None, :]
    sine_table = sine_table[:, None, :]
    first_scale = rms_scale(inputs)
    first_normed = inputs * first_scale
    normed = (first_normed * gain_attn).astype(jnp.bfloat16)
    projected = jnp.dot(normed, qkv_full, preferred_element_type=jnp.float32) + biases
    queries = projected[:, :D].reshape(local_rows, HEADS, HEAD)
    key_rows = projected[:, D : D + kv_width].reshape(local_rows, KV_HEADS, HEAD)
    queries = (queries * cosine + rotate_half(queries) * sine_table).astype(jnp.bfloat16)
    queries = queries.reshape(local_rows, KV_HEADS, GROUP, HEAD)
    key_rows = (
        (key_rows * cosine + rotate_half(key_rows) * sine_table)
        .astype(jnp.bfloat16)
        .reshape(local_rows, kv_width)
    )
    value_rows = projected[:, D + kv_width :].astype(jnp.bfloat16)
    kv_all = lax.all_gather(
        jnp.concatenate([key_rows, value_rows], axis=1), "dp", axis=0, tiled=True
    )
    all_keys = kv_all[:, :kv_width].reshape(seq_len, KV_HEADS, HEAD)
    all_values = kv_all[:, kv_width:].reshape(seq_len, KV_HEADS, HEAD)
    allowed = (key_places[None, :] <= query_places[:, None]) & (key_places[None, :] < row_length)

    def score_block():
        raw_scores = (
            jnp.einsum("tkhd,skd->khts", queries, all_keys, preferred_element_type=jnp.float32)
            * score_scale
        )
        return jnp.where(allowed[None, None], raw_scores, MASKED)

    scores = score_block()
    row_peak = jnp.max(scores, axis=-1, keepdims=True)
    exponent = jnp.exp(scores - row_peak)
    row_total = jnp.sum(exponent, axis=-1, keepdims=True)
    log_total = row_peak + jnp.log(row_total)
    probs_low = (exponent / row_total).astype(jnp.bfloat16)
    attended = jnp.einsum(
        "khts,skd->tkhd", probs_low, all_values, preferred_element_type=jnp.float32
    )
    attended = attended.reshape(local_rows, D).astype(jnp.bfloat16)
    middle = inputs + jnp.dot(attended, out_full, preferred_element_type=jnp.float32)
    second_scale = rms_scale(middle)
    second_normed = middle * second_scale
    normed_again = (second_normed * gain_mlp).astype(jnp.bfloat16)
    in_full, down_full = gather_all((half_in, half_down))
    gate_up = jnp.dot(normed_again, in_full, preferred_element_type=jnp.float32)
    gate_part = gate_up[:, :FF]
    up_part = gate_up[:, FF:]
    sigmoid_gate = jax.nn.sigmoid(gate_part)
    activated = gate_part * sigmoid_gate
    hidden = (activated * up_part).astype(jnp.bfloat16)
    mixed = (middle + jnp.dot(hidden, down_full, preferred_element_type=jnp.float32)).astype(
        jnp.bfloat16
    )
    valid = (query_places < row_length).astype(jnp.float32)
    out_cot = cotangent[0].astype(jnp.float32) * valid[:, None]
    out_cot_low = out_cot.astype(jnp.bfloat16)
    in_full, down_full = gather_all((half_in, half_down))
    (down_grad,) = reduce_all((contract_first(hidden, out_cot_low),))
    hidden_cot = contract_last(out_cot_low, down_full)
    gate_cot = hidden_cot * up_part * sigmoid_gate * (1.0 + gate_part * (1.0 - sigmoid_gate))
    up_cot = hidden_cot * activated
    gate_up_cot = jnp.concatenate([gate_cot, up_cot], axis=1).astype(jnp.bfloat16)
    (in_grad,) = reduce_all((contract_first(normed_again, gate_up_cot),))
    normed_again_cot = contract_last(gate_up_cot, in_full)
    gain_mlp_grad = jnp.sum(normed_again_cot * second_normed, axis=0)
    scaled_second = normed_again_cot * gain_mlp
    middle_cot = out_cot + second_scale * (
        scaled_second
        - second_normed * jnp.mean(scaled_second * second_normed, axis=-1, keepdims=True)
    )
    qkv_full, out_full = gather_all((half_qkv, half_out))
    middle_low = middle_cot.astype(jnp.bfloat16)
    out_grad_term = contract_first(attended, middle_low)
    attended_cot = (
        contract_last(middle_low, out_full)
        .astype(jnp.bfloat16)
        .reshape(local_rows, KV_HEADS, GROUP, HEAD)
    )
    scores = score_block()
    probs = jnp.exp(scores - log_total)
    probs_again = probs.astype(jnp.bfloat16)
    probs_cot = jnp.einsum(
        "tkhd,skd->khts", attended_cot, all_values, preferred_element_type=jnp.float32
    )
    row_dot = jnp.sum(probs * probs_cot, axis=-1, keepdims=True)
    scores_cot = (probs * (probs_cot - row_dot)).astype(jnp.bfloat16)
    query_cot = jnp.einsum(
        "khts,skd->tkhd", scores_cot, all_keys, preferred_element_type=jnp.float32
    )
    query_cot = query_cot.reshape(local_rows, HEADS, HEAD) * score_scale
    key_cot = jnp.einsum("khts,tkhd->skd", scores_cot, queries, preferred_element_type=jnp.float32)
    key_cot = key_cot.reshape(seq_len, kv_width) * score_scale
    value_cot = jnp.einsum(
        "khts,tkhd->skd", probs_again, attended_cot, preferred_element_type=jnp.float32
    )
    value_cot = value_cot.reshape(seq_len, kv_width)
    kv_cot = lax.psum_scatter(
        jnp.concatenate([key_cot, value_cot], axis=1).astype(jnp.bfloat16),
        "dp",
        scatter_dimension=0,
        tiled=True,
    ).astype(jnp.float32)
    query_back = query_cot * cosine - rotate_half(query_cot * sine_table)
    key_local = kv_cot[:, :kv_width].reshape(local_rows, KV_HEADS, HEAD)
    key_back = key_local * cosine - rotate_half(key_local * sine_table)
    projected_cot = jnp.concatenate(
        [
            query_back.reshape(local_rows, D),
            key_back.reshape(local_rows, kv_width),
            kv_cot[:, kv_width:],
        ],
        axis=1,
    )
    bias_grad = jnp.sum(projected_cot, axis=0)
    projected_low = projected_cot.astype(jnp.bfloat16)
    qkv_grad_term = contract_first(normed, projected_low)
    normed_cot = contract_last(projected_low, qkv_full)
    gain_attn_grad = jnp.sum(normed_cot * first_normed, axis=0)
    scaled_first = normed_cot * gain_attn
    input_cot = middle_cot + first_scale * (
        scaled_first - first_normed * jnp.mean(scaled_first * first_normed, axis=-1, keepdims=True)
    )
    small_term = group_small(gain_attn_grad, gain_mlp_grad, bias_grad)
    qkv_grad, out_grad, small_grad = reduce_all((qkv_grad_term, out_grad_term, small_term))
    return (mixed, input_cot, qkv_grad, out_grad, in_grad, down_grad, small_grad)


def per_device(
    tokens,
    cotangent,
    lengths,
    qkv_weight,
    qkv_first,
    qkv_second,
    out_weight,
    out_first,
    out_second,
    mlp_in_weight,
    mlp_in_first,
    mlp_in_second,
    down_weight,
    down_first,
    down_second,
    small_params,
    small_first,
    small_second,
):
    half_qkv = qkv_weight.astype(jnp.bfloat16)
    half_out = out_weight.astype(jnp.bfloat16)
    half_in = mlp_in_weight.astype(jnp.bfloat16)
    half_down = down_weight.astype(jnp.bfloat16)
    half_small = small_params.astype(jnp.bfloat16)
    results = sharded_pass(
        tokens, cotangent, lengths, half_qkv, half_out, half_in, half_down, half_small
    )
    mixed, input_cot, qkv_grad, out_grad, in_grad, down_grad, small_grad = results
    local_squares = sum(
        (jnp.sum(piece * piece) for piece in (qkv_grad, out_grad, in_grad, down_grad, small_grad))
    )
    total_squares = lax.psum(local_squares, ("dp", "fsdp"))
    grad_norm = jnp.sqrt(total_squares)
    clip_factor = CLIP_NORM / jnp.maximum(grad_norm, CLIP_NORM)
    qkv_out = update(
        qkv_weight, qkv_first, qkv_second, qkv_grad, clip_factor, MATRIX_RATE, MATRIX_DECAY
    )
    out_out = update(
        out_weight, out_first, out_second, out_grad, clip_factor, MATRIX_RATE, MATRIX_DECAY
    )
    mlp_out = update(
        mlp_in_weight, mlp_in_first, mlp_in_second, in_grad, clip_factor, MATRIX_RATE, MATRIX_DECAY
    )
    down_out = update(
        down_weight, down_first, down_second, down_grad, clip_factor, MATRIX_RATE, MATRIX_DECAY
    )
    small_out = update(
        small_params, small_first, small_second, small_grad, clip_factor, SMALL_RATE, 0.0
    )
    return (
        mixed[None],
        input_cot.astype(jnp.bfloat16)[None],
        grad_norm,
        qkv_out[0],
        qkv_out[1],
        qkv_out[2],
        qkv_out[3],
        out_out[0],
        out_out[1],
        out_out[2],
        out_out[3],
        mlp_out[0],
        mlp_out[1],
        mlp_out[2],
        mlp_out[3],
        down_out[0],
        down_out[1],
        down_out[2],
        down_out[3],
        small_out[0],
        small_out[1],
        small_out[2],
        small_out[3],
    )


def solution(mesh):
    in_specs = (
        P("fsdp", "dp", None),
        P("fsdp", "dp", None),
        P("fsdp"),
        P("dp", "fsdp"),
        P("dp", "fsdp"),
        P("dp", "fsdp"),
        P("dp", "fsdp"),
        P("dp", "fsdp"),
        P("dp", "fsdp"),
        P("dp", "fsdp"),
        P("dp", "fsdp"),
        P("dp", "fsdp"),
        P("dp", "fsdp"),
        P("dp", "fsdp"),
        P("dp", "fsdp"),
        P("dp", "fsdp"),
        P("dp", "fsdp"),
        P("dp", "fsdp"),
    )
    out_specs = (
        P("fsdp", "dp", None),
        P("fsdp", "dp", None),
        P(),
        P("dp", "fsdp"),
        P("dp", "fsdp"),
        P("dp", "fsdp"),
        P("dp", "fsdp"),
        P("dp", "fsdp"),
        P("dp", "fsdp"),
        P("dp", "fsdp"),
        P("dp", "fsdp"),
        P("dp", "fsdp"),
        P("dp", "fsdp"),
        P("dp", "fsdp"),
        P("dp", "fsdp"),
        P("dp", "fsdp"),
        P("dp", "fsdp"),
        P("dp", "fsdp"),
        P("dp", "fsdp"),
        P("dp", "fsdp"),
        P("dp", "fsdp"),
        P("dp", "fsdp"),
        P("dp", "fsdp"),
    )
    return jax.shard_map(
        per_device, mesh=mesh, in_specs=in_specs, out_specs=out_specs, check_vma=False
    )
```

profile of v0, /device:TPU:0, one launch (start us, length us, event | category | flops | bytes accessed | tf_op | source)
XLA Modules:
  0.0 2382.0 jit_solution(15834429713471065050)
XLA Ops:
  8.3 14.2 all_gather.43
  34.3 15.4 all-gather.1
  53.4 34.8 %all-gather.11.cloned.1.call-done = bf16[1536,2048]{1,0:T(8,128)(2,1)} async-done(((bf16[1536,256]{1,0:T(8,128)(2,1)}), bf16[1536,2048]{1,0:T(8,128)(2,1)}) %all-gather.11.cloned.1.call-update) | async-done | bytes 6291472 | tf_op jit(solution)/shard_map/all_gather | solution.py:99
  98.6 20.7 all_gather.46
  119.4 49.1 %all-gather.17.cloned.1.call-done = bf16[1536,2240]{0,1:T(8,128)(2,1)} async-done(((bf16[384,2240]{0,1:T(8,128)(2,1)}), bf16[1536,2240]{0,1:T(8,128)(2,1)}) %all-gather.17.cloned.1.call-update) | async-done | bytes 6881296 | tf_op jit(solution)/shard_map/all_gather | solution.py:94
  168.6 49.6 %all-gather.23.cloned.1.call-done = bf16[4,2240,192]{1,2,0:T(8,128)(2,1)} async-done(((bf16[1,2240,192]{1,2,0:T(8,128)(2,1)}), bf16[4,2240,192]{1,2,0:T(8,128)(2,1)}) %all-gather.23.cloned.1.call-update) | async-done | bytes 3440656 | tf_op jit(solution)/shard_map/all_gather | solution.py:94
  235.2 14.2 all-gather.13.cloned.1.call-done
  272.7 29.8 %all-gather.15.cloned.1.call-done = bf16[1536,1536]{0,1:T(8,128)(2,1)} async-done(((bf16[1536,192]{0,1:T(8,128)(2,1)}), bf16[1536,1536]{0,1:T(8,128)(2,1)}) %all-gather.15.cloned.1.call-update) | async-done | bytes 4718608 | tf_op jit(solution)/shard_map/all_gather | solution.py:99
  308.1 460.5 %all-gather.19.cloned.1.call-done = bf16[1536,17920]{0,1:T(8,128)(2,1)} async-done(((bf16[1536,2240]{0,1:T(8,128)(2,1)}), bf16[1536,17920]{0,1:T(8,128)(2,1)}) %all-gather.19.cloned.1.call-update) | async-done | bytes 55050256 | tf_op jit(solution)/shard_map/all_gather | solution.py:99
  768.6 34.4 %fusion.75 = f32[320,17920]{1,0:T(8,128)} fusion(bf16[1536,17920]{0,1:T(8,128)(2,1)} %all-gather.19.cloned.1.call-done, f32[320,1536]{1,0:T(8,128)S(1)} %get-tuple-element.76, f32[1536]{0:T(1024)S(1)} %mul.448, f32[320]{0:T(512)S(1)} %add_rsqrt_fusion), kind=kOutput, calls=%fused_computation.156 | convolution fusion | flops 17617551360 | bytes 79961344 | tf_op jit(solution)/shard_map/dot_general | solution.py:185
  803.1 205.2 %all-gather.21.cloned.1.call-done = bf16[8960,1536]{0,1:T(8,128)(2,1)} async-done(((bf16[8960,192]{0,1:T(8,128)(2,1)}), bf16[8960,1536]{0,1:T(8,128)(2,1)}) %all-gather.21.cloned.1.call-update) | async-done | bytes 27525136 | tf_op jit(solution)/shard_map/all_gather | solution.py:99
  1008.3 27.4 %multiply_convert_fusion.1 = (bf16[320,8960]{1,0:T(8,128)(2,1)}, bf16[320,8960]{1,0:T(8,128)(2,1)}, bf16[320,8960]{1,0:T(8,128)(2,1)}) fusion(f32[320,17920]{1,0:T(8,128)} %fusion.75, bf16[8960,1536]{0,1:T(8,128)(2,1)} %all-gather.21.cloned.1.call-done, bf16[1,320,1536]{2,1,0:T(8,128)(2,1)S(1)} %copy-done.31, f32[320]{0:T(512)S(1)} %compare_convert_fusion), kind=kOutput, calls=%fused_computation.15 | convolution fusion | flops 8852520960 | bytes 68650240 | tf_op jit(solution)/shard_map/dot_general | solution.py:86
  1035.6 34.3 %multiply_reduce_fusion = (bf16[1536]{0:T(1024)(128)(2,1)}, f32[320]{0:T(512)S(1)}, f32[320,1536]{1,0:T(8,128)}) fusion(f32[320,1536]{1,0:T(8,128)S(1)} %get-tuple-element.76, f32[320]{0:T(512)S(1)} %add_rsqrt_fusion, f32[1536]{0:T(1024)S(1)} %mul.448, bf16[1536,17920]{0,1:T(8,128)(2,1)} %all-gather.19.cloned.1.call-done, ...), kind=kOutput, calls=%fused_computation.73 | convolution fusion | flops 17641961472 | bytes 70462976 | tf_op jit(solution)/shard_map/dot_general | solution.py:86
  1168.9 21.6 convolution_convert_fusion.1
  1190.5 36.9 %convolution_convert_fusion = bf16[1536,17920]{0,1:T(8,128)(2,1)} fusion(bf16[320,8960]{1,0:T(8,128)(2,1)} %get-tuple-element.50, bf16[320,8960]{1,0:T(8,128)(2,1)} %get-tuple-element.49, f32[320,1536]{1,0:T(8,128)} %copy-done.20, f32[1536]{0:T(1024)S(1)} %mul.448, f32[320]{0:T(512)S(1)} %add_rsqrt_fusion), kind=kOutput, calls=%fused_computation | convolution fusion | flops 17668014080 | bytes 68492544 | tf_op jit(solution)/shard_map/dot_general | solution.py:80
  1241.0 39.9 %reduce-scatter.23.cloned.1.call-done = bf16[1536,256]{1,0:T(8,128)(2,1)} async-done(((bf16[1536,2048]{1,0:T(8,128)(2,1)}), bf16[1536,256]{1,0:T(8,128)(2,1)}) %reduce-scatter.23.cloned.1.call-update) | async-done | bytes 786448 | tf_op jit(solution)/shard_map/reduce_scatter | solution.py:107
  1281.0 270.0 %reduce-scatter.29.cloned.1.call-done = bf16[8960,192]{0,1:T(8,128)(2,1)} async-done(((bf16[8960,1536]{0,1:T(8,128)(2,1)}), bf16[8960,192]{0,1:T(8,128)(2,1)}) %reduce-scatter.29.cloned.1.call-update) | async-done | bytes 3440656 | tf_op jit(solution)/shard_map/reduce_scatter | solution.py:107
  1557.3 521.9 %reduce-scatter.39.cloned.1.call-done = bf16[1536,2240]{0,1:T(8,128)(2,1)} async-done(((bf16[1536,17920]{0,1:T(8,128)(2,1)}), bf16[1536,2240]{0,1:T(8,128)(2,1)}) %reduce-scatter.39.cloned.1.call-update) | async-done | bytes 6881296
  2091.0 16.1 fusion.26
  2122.0 16.5 reduce-scatter.31.cloned.1.call-done
  2140.3 27.4 %reduce-scatter.25.cloned.1.call-done = bf16[384,256]{1,0:T(8,128)(2,1)} async-done(((bf16[1536,256]{1,0:T(8,128)(2,1)}), bf16[384,256]{1,0:T(8,128)(2,1)}) %reduce-scatter.25.cloned.1.call-update) | async-done | bytes 196624 | tf_op jit(solution)/shard_map/reduce_scatter | solution.py:111
  2170.6 56.3 %reduce-scatter.35.cloned.1.call-done = bf16[2240,192]{1,0:T(8,128)(2,1)} async-done(((bf16[8960,192]{1,0:T(8,128)(2,1)}), bf16[2240,192]{1,0:T(8,128)(2,1)}) %reduce-scatter.35.cloned.1.call-update) | async-done | bytes 860176
  2229.6 77.3 %reduce-scatter.33.cloned.1.call-done = bf16[384,2240]{1,0:T(8,128)(2,1)} async-done(((bf16[1536,2240]{1,0:T(8,128)(2,1)}), bf16[384,2240]{1,0:T(8,128)(2,1)}) %reduce-scatter.33.cloned.1.call-update) | async-done | bytes 1720336
  2317.1 39.3 %psum.7 = f32[]{:T(128)} all-reduce(f32[]{:T(128)S(6)} %add.203), channel_id=1, replica_groups=mesh['dp'=4,'fsdp'=8] {'dp','fsdp'}, use_global_device_ids=true, to_apply=%region_26.27 | all-reduce | flops 1 | bytes 8 | tf_op jit(solution)/shard_map/psum | solution.py:300
  (249 shorter events, 247.5 us)
Async XLA Ops:
  7.2 81.0 %all-gather.11.cloned.1.call-start = ((), (), s32[]{:S(2)}) async-start(), calls=%async_computation.10 | async-start | bytes 7077888 | tf_op jit(solution)/shard_map/all_gather | solution.py:99
  22.5 146.0 %all-gather.17.cloned.1.call-start = ((), (), s32[]{:S(2)}) async-start(), calls=%async_computation.13 | async-start | bytes 8601600 | tf_op jit(solution)/shard_map/all_gather | solution.py:94
  26.0 192.2 %all-gather.23.cloned.1.call-start = ((), (), s32[]{:S(2)}) async-start(), calls=%async_computation.21 | async-start | bytes 4423680 | tf_op jit(solution)/shard_map/all_gather | solution.py:94
  27.1 222.2 %all-gather.13.cloned.1.call-start = ((), (), s32[]{:S(2)}) async-start(), calls=%async_computation.11 | async-start | bytes 1638400 | tf_op jit(solution)/shard_map/all_gather | solution.py:156
  98.5 204.0 %all-gather.15.cloned.1.call-start = ((), (), s32[]{:S(2)}) async-start(), calls=%async_computation.12 | async-start | bytes 5308416 | tf_op jit(solution)/shard_map/all_gather | solution.py:99
  119.4 649.3 %all-gather.19.cloned.1.call-start = ((), (), s32[]{:S(2)}) async-start(), calls=%async_computation.14 | async-start | bytes 61931520 | tf_op jit(solution)/shard_map/all_gather | solution.py:99
  168.5 839.8 %all-gather.21.cloned.1.call-start = ((), (), s32[]{:S(2)}) async-start(), calls=%async_computation.15 | async-start | bytes 30965760 | tf_op jit(solution)/shard_map/all_gather | solution.py:99
  227.4 925.9 %reduce-scatter.21.cloned.1.call-start = ((), (), s32[]{:S(2)}) async-start(), calls=%async_computation.16 | async-start | bytes 1638400 | tf_op jit(solution)/shard_map/reduce_scatter | solution.py:237
  307.4 728.2 %copy-start.20 = (f32[320,1536]{1,0:T(8,128)}, f32[320,1536]{1,0:T(8,128)S(1)}, u32[]{:S(2)}) copy-start(f32[320,1536]{1,0:T(8,128)S(1)} %get-tuple-element.76) | copy-start | bytes 5898244
  768.6 239.6 %copy-start.31 = (bf16[1,320,1536]{2,1,0:T(8,128)(2,1)S(1)}, bf16[1,320,1536]{2,1,0:T(8,128)(2,1)}, u32[]{:S(2)}) copy-start(bf16[1,320,1536]{2,1,0:T(8,128)(2,1)} %param.19) | copy-start | bytes 2949124
  1073.0 52.6 %copy-start.4 = (f32[320,1536]{1,0:T(8,128)}, f32[320,1536]{1,0:T(8,128)S(1)}, u32[]{:S(2)}) copy-start(f32[320,1536]{1,0:T(8,128)S(1)} %fusion.39) | copy-start | bytes 5898244
  1125.6 113.1 %reduce-scatter.27.cloned.1.call-start = ((), (), s32[]{:S(2)}) async-start(), calls=%async_computation.19 | async-start | bytes 5308416 | tf_op jit(solution)/shard_map/reduce_scatter | solution.py:107
  1131.3 149.6 %reduce-scatter.23.cloned.1.call-start = ((), (), s32[]{:S(2)}) async-start(), calls=%async_computation.17 | async-start | bytes 7077888 | tf_op jit(solution)/shard_map/reduce_scatter | solution.py:107
  1168.8 382.2 %reduce-scatter.29.cloned.1.call-start = ((), (), s32[]{:S(2)}) async-start(), calls=%async_computation.20 | async-start | bytes 30965760 | tf_op jit(solution)/shard_map/reduce_scatter | solution.py:107
  1190.5 888.7 %reduce-scatter.39.cloned.1.call-start = ((), (), s32[]{:S(2)}) async-start(), calls=%async_computation.26 | async-start | bytes 61931520
  1227.4 883.3 %reduce-scatter.37.cloned.1.call-start = ((), (), s32[]{:S(2)}) async-start(), calls=%async_computation.25 | async-start | bytes 184320
  1238.6 900.0 %reduce-scatter.31.cloned.1.call-start = ((), (), s32[]{:S(2)}) async-start(), calls=%async_computation.22 | async-start | bytes 983040
  1240.9 926.7 %reduce-scatter.25.cloned.1.call-start = ((), (), s32[]{:S(2)}) async-start(), calls=%async_computation.18 | async-start | bytes 983040 | tf_op jit(solution)/shard_map/reduce_scatter | solution.py:111
  1280.9 946.0 %reduce-scatter.35.cloned.1.call-start = ((), (), s32[]{:S(2)}) async-start(), calls=%async_computation.24 | async-start | bytes 5734400
  1557.2 749.7 %reduce-scatter.33.cloned.1.call-start = ((), (), s32[]{:S(2)}) async-start(), calls=%async_computation.23 | async-start | bytes 8847360
  2313.1 44.0 %copy-start.46 = (f32[2,80]{1,0:T(2,128)S(1)}, f32[2,80]{1,0:T(2,128)}, u32[]{:S(2)}) copy-start(f32[2,80]{1,0:T(2,128)} %param.33) | copy-start | bytes 1924
  2313.1 44.0 %copy-start.47 = (f32[2,80]{1,0:T(2,128)S(1)}, f32[2,80]{1,0:T(2,128)}, u32[]{:S(2)}) copy-start(f32[2,80]{1,0:T(2,128)} %param.34) | copy-start | bytes 1924
  2313.1 44.6 %copy-start.30 = (f32[384,192]{0,1:T(8,128)S(1)}, f32[384,192]{0,1:T(8,128)}, u32[]{:S(2)}) copy-start(f32[384,192]{0,1:T(8,128)} %param.24) | copy-start | bytes 884740
  2313.1 44.6 %copy-start.39 = (f32[384,192]{0,1:T(8,128)S(1)}, f32[384,192]{0,1:T(8,128)}, u32[]{:S(2)}) copy-start(f32[384,192]{0,1:T(8,128)} %param.25) | copy-start | bytes 884740
  (43 other events, 460.6 us)
Sparse Core Ops, SparseCore 0:
  22.6 65.5 all-gather.10
  90.6 77.8 all-gather.16
  170.9 47.2 all-gather.22
  220.5 28.8 all-gather.12
  250.8 51.6 all-gather.14
  304.1 464.5 all-gather.18
  770.8 237.3 all-gather.20
  1125.7 27.5 reduce-scatter.20
  1155.6 54.9 reduce-scatter.26
  1212.7 68.1 reduce-scatter.22
  1283.3 267.6 reduce-scatter.28
  1553.4 525.7 reduce-scatter.38
  2082.0 28.6 reduce-scatter.36
  2114.3 24.2 reduce-scatter.30
  2141.6 26.0 reduce-scatter.24
  2170.9 55.9 reduce-scatter.34
  2230.1 76.7 reduce-scatter.32
where the time goes:
time: 2390 us; the launch traced here: 2380 us
  waiting for transfers between devices  1860 us (78%)
  matrix products  248 us (10%)
  blocking collectives  107 us (4%)
  local copies, waits for them, and re-layouts  74 us (3%)
  other arithmetic  67.1 us (3%)
    all_gather x4, waiting for transfers between devices, gather_all(): lax.all_gather(shortened(lengthened), 'fsdp', axis=1, tiled=True)  730 us
    unnamed x22, waiting for transfers between devices  676 us
    reduce_scatter x3, waiting for transfers between devices, reduce_all(): lax.psum_scatter(shortened(terms), 'fsdp', scatter_dimension=1, tiled=True)  310 us
    all_gather x2, waiting for transfers between devices, gather_all(): lax.all_gather(shortened(shards), 'dp', axis=0, tiled=True)  98.7 us
    dot_general x4, matrix products, contract_last(): lax.dot_general(left, right, (((1,), (1,)), ((), ())), preferred_element_...  74.5 us
    dot_general x4, matrix products, contract_first(): lax.dot_general(left, right, (((0,), (0,)), ((), ())), preferred_element_...  70.9 us
  transfers between devices with their start and end apart: 17, of which 16 were waited for; matrix products, arithmetic and copies ran while one was open for 10% of the time, Pallas kernels for 0%

commit v1 on v0

v1 whole, which is shorter than its diff:
```python
import jax
import jax.numpy as jnp
from jax import lax
from jax.sharding import PartitionSpec as P

D = 1536
HEADS = 12
KV_HEADS = 2
HEAD = 128
FF = 8960
STEP = 5
GROUP = 6
SMALL = 5120
QKV = 2048
KV_WIDTH = KV_HEADS * HEAD


NORM_EPS = 1e-06
ROPE_BASE = 1000000.0
BETA_FIRST = 0.5
BETA_SECOND = 0.5
ADAM_EPS = 1e-08
MATRIX_RATE = 0.03
SMALL_RATE = 0.3
MATRIX_DECAY = 0.1
CLIP_NORM = 1.0
MASKED = -1e30
SCALE = HEAD ** (-0.5)
CHUNKS = (768, 768, 704)


def unpack_small(small_vec):
    grouped = small_vec.reshape(KV_HEADS * HEAD, 3 * GROUP + 2)
    gain_attn = grouped[:, :GROUP].reshape(-1)
    gain_mlp = grouped[:, GROUP : 2 * GROUP].reshape(-1)
    biases = jnp.concatenate(
        [
            grouped[:, 2 * GROUP : 3 * GROUP].reshape(-1),
            grouped[:, 3 * GROUP],
            grouped[:, 3 * GROUP + 1],
        ]
    )
    return (gain_attn, gain_mlp, biases)


def group_small(gain_attn, gain_mlp, biases):
    count = KV_HEADS * HEAD
    pieces = [
        gain_attn.reshape(count, GROUP),
        gain_mlp.reshape(count, GROUP),
        biases[:D].reshape(count, GROUP),
        biases[D : D + count][:, None],
        biases[D + count :][:, None],
    ]
    return jnp.concatenate(pieces, axis=1).reshape(8, SMALL // 8)


def rotate_half(values):
    half_width = HEAD // 2
    return jnp.concatenate([-values[..., half_width:], values[..., :half_width]], axis=-1)


def rope_tables(positions):
    pair_index = jnp.arange(HEAD // 2, dtype=jnp.float32)
    inverse = jnp.power(jnp.float32(ROPE_BASE), -2.0 * pair_index / HEAD)
    angles = positions[:, None] * inverse[None, :]
    angles = jnp.concatenate([angles, angles], axis=-1)
    return (jnp.cos(angles), jnp.sin(angles))


def rms_scale(values):
    return lax.rsqrt(jnp.mean(values * values, axis=-1, keepdims=True) + NORM_EPS)


def dot_nn(left, right):
    return jnp.dot(left, right, preferred_element_type=jnp.float32)


def dot_nt(left, right):
    return lax.dot_general(
        left, right, (((1,), (1,)), ((), ())), preferred_element_type=jnp.float32
    )


def dot_tn(left, right):
    return lax.dot_general(
        left, right, (((0,), (0,)), ((), ())), preferred_element_type=jnp.float32
    )


def update(weight, first, second, gradient, clip_factor, rate, decay):
    step_grad = gradient * clip_factor
    first_new = BETA_FIRST * first + (1.0 - BETA_FIRST) * step_grad
    second_new = BETA_SECOND * second + (1.0 - BETA_SECOND) * step_grad * step_grad
    first_fix = 1.0 - BETA_FIRST**STEP
    second_fix = 1.0 - BETA_SECOND**STEP
    weight_new = weight - rate * (
        first_new / first_fix / (jnp.sqrt(second_new / second_fix) + ADAM_EPS) + decay * weight
    )
    return (weight_new, first_new, second_new, weight_new.astype(jnp.bfloat16))


def dp_send(block, k):
    count = lax.axis_size("dp")
    return lax.ppermute(block, "dp", [(i, i ^ k) for i in range(count)])


def core_swap(block):
    count = lax.axis_size("fsdp")
    return lax.ppermute(block, "fsdp", [(i, i ^ 1) for i in range(count)])


def dp_gather(block):
    return [block] + [dp_send(block, k) for k in range(1, lax.axis_size("dp"))]


def dp_own(array, k):
    return lax.dynamic_index_in_dim(array, lax.axis_index("dp") ^ k, 0, keepdims=False)


def dp_exchange(array):
    count = lax.axis_size("dp")
    place = lax.axis_index("dp")
    got = jnp.stack([dp_own(array, 0)] + [dp_send(dp_own(array, k), k) for k in range(1, count)])
    return jnp.stack(
        [lax.dynamic_index_in_dim(got, place ^ a, 0, keepdims=False) for a in range(count)]
    )


def dp_columns(array, k, width):
    return lax.dynamic_slice_in_dim(array, (lax.axis_index("dp") ^ k) * width, width, 1)


def dp_order(blocks):
    place = lax.axis_index("dp")
    stacked = jnp.stack(blocks)
    return jnp.concatenate(
        [
            lax.dynamic_index_in_dim(stacked, place ^ a, 0, keepdims=False)
            for a in range(len(blocks))
        ],
        axis=1,
    )


def parity_groups():
    count = lax.axis_size("fsdp")
    return [[2 * i + c for i in range(count // 2)] for c in range(2)]


def is_even():
    return lax.rem(lax.axis_index("fsdp"), 2) == 0


def gather_matrix(shard):
    piece = shard.T
    along = lax.all_gather(
        piece, "fsdp", axis=0, tiled=True, axis_index_groups=parity_groups()
    )
    own = dp_gather(along)
    other = [core_swap(block) for block in own]
    return own, other


def interleave(own, other):
    slices = lax.axis_size("fsdp") // 2
    rows = own.shape[0]
    even = jnp.where(is_even(), own, other)
    odd = jnp.where(is_even(), other, own)
    both = jnp.stack([even.reshape(rows, slices, -1), odd.reshape(rows, slices, -1)], axis=2)
    return both.reshape(rows, -1)


def split_parity(array):
    slices = lax.axis_size("fsdp") // 2
    rows = array.shape[0]
    both = array.reshape(rows, slices, 2, -1)
    even = both[:, :, 0].reshape(rows, -1)
    odd = both[:, :, 1].reshape(rows, -1)
    return jnp.where(is_even(), even, odd), jnp.where(is_even(), odd, even)


def reduce_matrix(own_terms, other_terms):
    summed = [
        mine.astype(jnp.float32) + core_swap(theirs).astype(jnp.float32)
        for mine, theirs in zip(own_terms, other_terms)
    ]
    total = summed[0]
    for k in range(1, len(summed)):
        total = total + dp_send(summed[k].astype(jnp.bfloat16), k).astype(jnp.float32)
    shard = lax.psum_scatter(
        total.astype(jnp.bfloat16),
        "fsdp",
        scatter_dimension=0,
        tiled=True,
        axis_index_groups=parity_groups(),
    )
    return shard.T.astype(jnp.float32)


def bf16(array):
    return array.astype(jnp.bfloat16)


def mlp_in_pieces(shard):
    ranks = lax.axis_size("dp")
    rows, columns = shard.shape
    part = columns // ranks
    sent = shard.reshape(rows, ranks, part).transpose(1, 2, 0)
    got = dp_exchange(sent)
    return got.transpose(1, 0, 2).reshape(part, ranks * rows)


def mlp_in_back(grad):
    ranks = lax.axis_size("dp")
    part = grad.shape[0]
    rows = grad.shape[1] // ranks
    got = dp_exchange(grad.reshape(part, ranks, rows).transpose(1, 0, 2))
    return got.transpose(2, 0, 1).reshape(rows, ranks * part)


def down_pieces(shard, part):
    ranks = lax.axis_size("dp")
    units, columns = shard.shape
    slices = units // (ranks * part)
    sent = shard.reshape(slices, ranks, part, columns).transpose(1, 3, 0, 2)
    got = dp_exchange(sent)
    return got.transpose(1, 0, 2, 3).reshape(columns, ranks * slices, part)


def down_back(grad):
    ranks = lax.axis_size("dp")
    columns, all_slices, part = grad.shape
    slices = all_slices // ranks
    got = dp_exchange(grad.reshape(columns, ranks, slices, part).transpose(1, 0, 2, 3))
    return got.transpose(2, 0, 3, 1).reshape(slices * ranks * part, columns)


def sharded_pass(tokens, cotangent, lengths, half_qkv, half_out, half_in, half_down, half_small):
    ranks = lax.axis_size("dp")
    lines = lax.axis_size("fsdp")
    place = lax.axis_index("dp")
    local_rows = tokens.shape[1]
    block_rows = D // ranks

    qkv_own, qkv_other = gather_matrix(half_qkv)
    small_full = lax.all_gather(half_small, ("dp", "fsdp"), axis=0, tiled=False)
    small_rows, small_columns = half_small.shape
    small_vec = small_full.reshape(ranks, lines, small_rows, small_columns)
    small_vec = small_vec.transpose(0, 2, 1, 3).reshape(-1).astype(jnp.float32)
    gain_attn, gain_mlp, biases = unpack_small(small_vec)

    out_own, out_other = gather_matrix(half_out)
    part = half_in.shape[1] // ranks
    in_piece = mlp_in_pieces(half_in)
    down_piece = down_pieces(half_down, part)
    slices = lines // 2
    in_chunks = []
    down_chunks = []
    start = 0
    for size in CHUNKS:
        width = size // slices
        in_chunks.append(
            lax.all_gather(in_piece[start : start + width], "fsdp", axis=0, tiled=True)
        )
        down_chunks.append(
            lax.all_gather(
                down_piece[:, :, start : start + width].reshape(-1, size),
                "fsdp",
                axis=0,
                tiled=True,
            )
        )
        start += width

    inputs = tokens[0].astype(jnp.float32)
    row_length = lengths[0]
    local_places = jnp.arange(local_rows, dtype=jnp.int32)
    query_places = place * local_rows + local_places
    key_places = jnp.concatenate([(place ^ k) * local_rows + local_places for k in range(ranks)])
    valid = (query_places < row_length).astype(jnp.float32)
    out_cot = cotangent[0].astype(jnp.float32) * valid[:, None]
    out_cot_all = jnp.concatenate(dp_gather(bf16(out_cot)))

    cosine, sine_table = rope_tables(query_places.astype(jnp.float32))
    cosine = cosine[:, None, :]
    sine_table = sine_table[:, None, :]
    first_scale = rms_scale(inputs)
    first_normed = inputs * first_scale
    normed = bf16(first_normed * gain_attn)
    normed_blocks = [dp_columns(normed, k, block_rows) for k in range(ranks)]
    projected = interleave(
        sum(dot_nt(block, mat) for block, mat in zip(normed_blocks, qkv_own)),
        sum(dot_nt(block, mat) for block, mat in zip(normed_blocks, qkv_other)),
    )
    projected = projected + biases
    queries = projected[:, :D].reshape(local_rows, HEADS, HEAD)
    key_rows = projected[:, D : D + KV_WIDTH].reshape(local_rows, KV_HEADS, HEAD)
    queries = bf16(queries * cosine + rotate_half(queries) * sine_table)
    queries = queries.reshape(local_rows, KV_HEADS, GROUP, HEAD)
    key_rows = bf16(key_rows * cosine + rotate_half(key_rows) * sine_table)
    key_rows = key_rows.reshape(local_rows, KV_WIDTH)
    value_rows = bf16(projected[:, D + KV_WIDTH :])
    kv_all = jnp.concatenate(dp_gather(jnp.concatenate([key_rows, value_rows], axis=1)))
    all_keys = kv_all[:, :KV_WIDTH].reshape(-1, KV_HEADS, HEAD)
    all_values = kv_all[:, KV_WIDTH:].reshape(-1, KV_HEADS, HEAD)
    allowed = (key_places[None, :] <= query_places[:, None]) & (key_places[None, :] < row_length)

    def score_block():
        raw_scores = (
            jnp.einsum("tkhd,skd->khts", queries, all_keys, preferred_element_type=jnp.float32)
            * SCALE
        )
        return jnp.where(allowed[None, None], raw_scores, MASKED)

    scores = score_block()
    row_peak = jnp.max(scores, axis=-1, keepdims=True)
    exponent = jnp.exp(scores - row_peak)
    row_total = jnp.sum(exponent, axis=-1, keepdims=True)
    log_total = row_peak + jnp.log(row_total)
    probs_low = bf16(exponent / row_total)
    attended = jnp.einsum(
        "khts,skd->tkhd", probs_low, all_values, preferred_element_type=jnp.float32
    )
    attended = bf16(attended.reshape(local_rows, D))
    attended_blocks = [dp_columns(attended, k, block_rows) for k in range(ranks)]
    middle = inputs + interleave(
        sum(dot_nt(block, mat) for block, mat in zip(attended_blocks, out_own)),
        sum(dot_nt(block, mat) for block, mat in zip(attended_blocks, out_other)),
    )
    second_scale = rms_scale(middle)
    second_normed = middle * second_scale
    normed_again = bf16(second_normed * gain_mlp)

    normed_all = jnp.concatenate(dp_gather(normed_again))
    mixed_part = 0.0
    back_part = 0.0
    in_grads = []
    down_grads = []
    for size, in_mat, down_mat in zip(CHUNKS, in_chunks, down_chunks):
        gate_up = dot_nt(normed_all, in_mat)
        gate = gate_up[:, :size]
        up = gate_up[:, size:]
        sigmoid_gate = jax.nn.sigmoid(gate)
        activated = gate * sigmoid_gate
        hidden = bf16(activated * up)
        mixed_part = mixed_part + dot_nt(hidden, down_mat)
        hidden_cot = dot_nn(out_cot_all, down_mat)
        gate_cot = hidden_cot * up * sigmoid_gate * (1.0 + gate * (1.0 - sigmoid_gate))
        up_cot = hidden_cot * activated
        gate_up_cot = bf16(jnp.concatenate([gate_cot, up_cot], axis=1))
        back_part = back_part + dot_nn(gate_up_cot, in_mat)
        down_grads.append(
            lax.psum_scatter(
                bf16(dot_tn(out_cot_all, hidden)), "fsdp", scatter_dimension=0, tiled=True
            ).reshape(-1, slices, size // slices)
        )
        in_grads.append(
            lax.psum_scatter(
                bf16(dot_tn(gate_up_cot, normed_all)), "fsdp", scatter_dimension=0, tiled=True
            )
        )

    def token_reduce(partial):
        partial = partial.reshape(ranks, local_rows, D)
        total = partial[0]
        for k in range(1, ranks):
            total = total + dp_send(bf16(partial[k]), k).astype(jnp.float32)
        return total

    normed_again_cot = token_reduce(back_part)
    mixed = bf16(middle + token_reduce(mixed_part))
    in_grad = mlp_in_back(jnp.concatenate(in_grads)).astype(jnp.float32)
    down_grad = down_back(jnp.concatenate(down_grads, axis=2)).astype(jnp.float32)

    gain_mlp_grad = jnp.sum(normed_again_cot * second_normed, axis=0)
    scaled_second = normed_again_cot * gain_mlp
    middle_cot = out_cot + second_scale * (
        scaled_second
        - second_normed * jnp.mean(scaled_second * second_normed, axis=-1, keepdims=True)
    )
    middle_low = bf16(middle_cot)
    middle_own, middle_other = split_parity(middle_low)
    out_grad = reduce_matrix(
        [bf16(dot_tn(middle_own, block)) for block in attended_blocks],
        [bf16(dot_tn(middle_other, block)) for block in attended_blocks],
    )
    attended_cot = bf16(
        dp_order(
            [
                dot_nn(middle_own, mine) + dot_nn(middle_other, theirs)
                for mine, theirs in zip(out_own, out_other)
            ]
        )
    ).reshape(local_rows, KV_HEADS, GROUP, HEAD)
    scores = score_block()
    probs = jnp.exp(scores - log_total)
    probs_again = bf16(probs)
    probs_cot = jnp.einsum(
        "tkhd,skd->khts", attended_cot, all_values, preferred_element_type=jnp.float32
    )
    row_dot = jnp.sum(probs * probs_cot, axis=-1, keepdims=True)
    scores_cot = bf16(probs * (probs_cot - row_dot))
    query_cot = jnp.einsum(
        "khts,skd->tkhd", scores_cot, all_keys, preferred_element_type=jnp.float32
    )
    query_cot = query_cot.reshape(local_rows, HEADS, HEAD) * SCALE
    key_cot = jnp.einsum("khts,tkhd->skd", scores_cot, queries, preferred_element_type=jnp.float32)
    key_cot = key_cot.reshape(-1, KV_WIDTH) * SCALE
    value_cot = jnp.einsum(
        "khts,tkhd->skd", probs_again, attended_cot, preferred_element_type=jnp.float32
    )
    value_cot = value_cot.reshape(-1, KV_WIDTH)
    kv_cot = jnp.concatenate([key_cot, value_cot], axis=1).reshape(ranks, local_rows, -1)
    kv_total = kv_cot[0]
    for k in range(1, ranks):
        kv_total = kv_total + dp_send(bf16(kv_cot[k]), k).astype(jnp.float32)
    query_back = query_cot * cosine - rotate_half(query_cot * sine_table)
    key_local = kv_total[:, :KV_WIDTH].reshape(local_rows, KV_HEADS, HEAD)
    key_back = key_local * cosine - rotate_half(key_local * sine_table)
    projected_cot = jnp.concatenate(
        [
            query_back.reshape(local_rows, D),
            key_back.reshape(local_rows, KV_WIDTH),
            kv_total[:, KV_WIDTH:],
        ],
        axis=1,
    )
    bias_grad = jnp.sum(projected_cot, axis=0)
    projected_low = bf16(projected_cot)
    projected_own, projected_other = split_parity(projected_low)
    qkv_grad = reduce_matrix(
        [bf16(dot_tn(projected_own, block)) for block in normed_blocks],
        [bf16(dot_tn(projected_other, block)) for block in normed_blocks],
    )
    normed_cot = dp_order(
        [
            dot_nn(projected_own, mine) + dot_nn(projected_other, theirs)
            for mine, theirs in zip(qkv_own, qkv_other)
        ]
    )
    gain_attn_grad = jnp.sum(normed_cot * first_normed, axis=0)
    scaled_first = normed_cot * gain_attn
    input_cot = middle_cot + first_scale * (
        scaled_first - first_normed * jnp.mean(scaled_first * first_normed, axis=-1, keepdims=True)
    )
    small_term = group_small(gain_attn_grad, gain_mlp_grad, bias_grad)
    small_sum = lax.psum(small_term, ("dp", "fsdp"))
    small_grad = lax.dynamic_slice(
        small_sum,
        (place * small_rows, lax.axis_index("fsdp") * small_columns),
        (small_rows, small_columns),
    )
    return (mixed, input_cot, qkv_grad, out_grad, in_grad, down_grad, small_grad)


def per_device(
    tokens,
    cotangent,
    lengths,
    qkv_weight,
    qkv_first,
    qkv_second,
    out_weight,
    out_first,
    out_second,
    mlp_in_weight,
    mlp_in_first,
    mlp_in_second,
    down_weight,
    down_first,
    down_second,
    small_params,
    small_first,
    small_second,
):
    results = sharded_pass(
        tokens,
        cotangent,
        lengths,
        bf16(qkv_weight),
        bf16(out_weight),
        bf16(mlp_in_weight),
        bf16(down_weight),
        bf16(small_params),
    )
    mixed, input_cot, qkv_grad, out_grad, in_grad, down_grad, small_grad = results
    local_squares = sum(
        (jnp.sum(piece * piece) for piece in (qkv_grad, out_grad, in_grad, down_grad, small_grad))
    )
    total_squares = lax.psum(local_squares, ("dp", "fsdp"))
    grad_norm = jnp.sqrt(total_squares)
    clip_factor = CLIP_NORM / jnp.maximum(grad_norm, CLIP_NORM)
    outs = [mixed[None], bf16(input_cot)[None], grad_norm]
    for weight, first, second, gradient, rate, decay in (
        (qkv_weight, qkv_first, qkv_second, qkv_grad, MATRIX_RATE, MATRIX_DECAY),
        (out_weight, out_first, out_second, out_grad, MATRIX_RATE, MATRIX_DECAY),
        (mlp_in_weight, mlp_in_first, mlp_in_second, in_grad, MATRIX_RATE, MATRIX_DECAY),
        (down_weight, down_first, down_second, down_grad, MATRIX_RATE, MATRIX_DECAY),
        (small_params, small_first, small_second, small_grad, SMALL_RATE, 0.0),
    ):
        outs.extend(update(weight, first, second, gradient, clip_factor, rate, decay))
    return tuple(outs)


def solution(mesh):
    rows = P("fsdp", "dp", None)
    shard = P("dp", "fsdp")
    return jax.shard_map(
        per_device,
        mesh=mesh,
        in_specs=(rows, rows, P("fsdp")) + (shard,) * 15,
        out_specs=(rows, rows, P()) + (shard,) * 20,
        check_vma=False,
    )
```

time: 2390 us -> 1020 us (0.43)
  waiting for transfers between devices: 1860 us -> 259 us
  blocking collectives: 107 us -> 166 us
  starting transfers between devices: 0.88 us -> 57.3 us
  local copies, waits for them, and re-layouts: 74 us -> 121 us
  other arithmetic: 67.1 us -> 114 us
    all_gather x7 -> x6, waiting for transfers between devices: 843 us -> 0.02 us  [the longest x3 0.02 us: sharded_pass(): lax.all_gather(in_piece[start:start + width], 'fsdp', axis=0, tiled=True)]
    unnamed x22 -> x14, waiting for transfers between devices: 676 us -> 0.23 us
    reduce_scatter x5 -> x8, waiting for transfers between devices: 345 us -> 38.9 us  [the longest x3 28.4 us: sharded_pass(): lax.psum_scatter(bf16(dot_tn(gate_up_cot, normed_all)), 'fsdp', scatter_d...]
    ppermute x0 -> x58, waiting for transfers between devices: none -> 220 us  [the longest x42 220 us: dp_send(): return lax.ppermute(block, 'dp', [(i, i ^ k) for i in range(count)])]
    ppermute x0 -> x58, starting transfers between devices: none -> 55.8 us  [the longest x42 51.6 us: dp_send(): return lax.ppermute(block, 'dp', [(i, i ^ k) for i in range(count)])]
    psum x0 -> x1, blocking collectives: none -> 38.3 us  [sharded_pass(): small_sum = lax.psum(small_term, ('dp', 'fsdp'))]
    all_gather x4 -> x3, blocking collectives: 57.4 us -> 87.9 us  [the longest x2 48.5 us: gather_matrix(): lax.all_gather(piece, 'fsdp', axis=0, tiled=True, axis_index_groups=parit...]
    dot_general x12 -> x66, matrix products: 206 us -> 218 us  [the longest x22 81.8 us: dot_nn(): return jnp.dot(left, right, preferred_element_type=jnp.float32)]
  transfers between devices with their start and end apart: 17 -> 72, of which waited for: 16 -> 21; matrix products, arithmetic and copies ran while one was open for 10% -> 40% of each run, Pallas kernels for 0% -> 0%
where the time goes in v1:
time: 1020 us; the launch traced here: 1010 us
  matrix products  270 us (26%)
  waiting for transfers between devices  259 us (25%)
  blocking collectives  166 us (16%)
  local copies, waits for them, and re-layouts  121 us (12%)
  other arithmetic  114 us (11%)
  starting transfers between devices  57.3 us (6%)
  between operations  22.4 us (2%)
    ppermute x42, waiting for transfers between devices, dp_send(): return lax.ppermute(block, 'dp', [(i, i ^ k) for i in range(count)])  220 us
    dot_general x22, matrix products, dot_nn(): return jnp.dot(left, right, preferred_element_type=jnp.float32)  81.8 us
    dot_general x22, matrix products, dot_nt(): lax.dot_general(left, right, (((1,), (1,)), ((), ())), preferred_element_...  73.3 us
    dot_general x22, matrix products, dot_tn(): lax.dot_general(left, right, (((0,), (0,)), ((), ())), preferred_element_...  62.7 us
    ppermute x42, starting transfers between devices, dp_send(): return lax.ppermute(block, 'dp', [(i, i ^ k) for i in range(count)])  51.6 us
    all_gather x2, blocking collectives, gather_matrix(): lax.all_gather(piece, 'fsdp', axis=0, tiled=True, axis_index_groups=parit...  48.5 us
    psum x1, blocking collectives, per_device(): total_squares = lax.psum(local_squares, ('dp', 'fsdp'))  40 us
    all_gather x1, blocking collectives, sharded_pass(): small_full = lax.all_gather(half_small, ('dp', 'fsdp'), axis=0, tiled=False)  39.4 us
  transfers between devices with their start and end apart: 72, of which 21 were waited for; matrix products, arithmetic and copies ran while one was open for 40% of the time, Pallas kernels for 0%

profile of v1, /device:TPU:0, one launch (start us, length us, event | category | flops | bytes accessed | tf_op | source)
XLA Modules:
  0.0 1009.7 jit_solution(14196169078391409858)
XLA Ops:
  69.7 25.2 %all_gather.32 = bf16[1024,384]{0,1:T(8,128)(2,1)S(1)} all-gather(bf16[256,384]{0,1:T(8,128)(2,1)S(1)} %convert_bitcast_fusion.1), channel_id=1, replica_groups={{0,2,4,6},{1,3,5,7},{8,10,12,14},{9,11,13,15},{16,18,20,22},{17,19,21,2..., dimensions={0}, use_global_device_ids=true | all-gather | bytes 983040 | tf_op jit(solution)/shard_map/all_gather | solution.py:157
  98.4 23.3 %all_gather.33 = bf16[768,384]{1,0:T(8,128)(2,1)} all-gather(bf16[192,384]{1,0:T(8,128)(2,1)S(1)} %convert_bitcast_fusion.2), channel_id=1, replica_groups={{0,2,4,6},{1,3,5,7},{8,10,12,14},{9,11,13,15},{16,18,20,22},{17,19,21,2..., dimensions={0}, use_global_device_ids=true | all-gather | bytes 737280 | tf_op jit(solution)/shard_map/all_gather | solution.py:157
  124.1 39.4 %all-gather.1 = bf16[32,2,80]{2,1,0:T(2,128)(2,1)S(1)} all-gather(bf16[1,2,80]{2,1,0:T(2,128)(2,1)S(1)} %convert_bitcast_fusion.3), channel_id=2, replica_groups=mesh['dp'=4,'fsdp'=8] {'dp','fsdp'}, dimensions={0}, use_global_device_ids=true | all-gather | bytes 10560 | tf_op jit(solution)/shard_map/all_gather | solution.py:247
  299.4 16.6 %collective-permute-done.19 = bf16[320,1536]{1,0:T(8,128)(2,1)} collective-permute-done((bf16[320,1536]{1,0:T(8,128)(2,1)}, bf16[320,1536]{1,0:T(8,128)(2,1)}, u32[]{:S(2)}, u32[]{:S(2)}) %collective-permute-start.19) | collective-permute-done | bytes 983072 | tf_op jit(solution)/shard_map/ppermute | solution.py:105
  317.0 20.1 %collective-permute-done.18 = bf16[320,1536]{1,0:T(8,128)(2,1)} collective-permute-done((bf16[320,1536]{1,0:T(8,128)(2,1)}, bf16[320,1536]{1,0:T(8,128)(2,1)}, u32[]{:S(2)}, u32[]{:S(2)}) %collective-permute-start.18) | collective-permute-done | bytes 983072 | tf_op jit(solution)/shard_map/ppermute | solution.py:105
  337.1 12.5 %fusion.172 = f32[1280,1408]{1,0:T(8,128)} fusion(bf16[1408,1536]{1,0:T(8,128)(2,1)} %all-gather.17.cloned.1.call-done, bf16[320,1536]{1,0:T(8,128)(2,1)} %collective-permute-done.19, bf16[320,1536]{1,0:T(8,128)(2,1)} %collective-permute-done.18, bf16[320,1536]{1,0:T(8,128)(2,1)} %collective-permute-done.17, bf16[320,1536]{1,0:T(8,128)(2,1)} %multiply_convert_fusion.9), kind=kOutput, calls=%fused_computation.393 | convolution fusion | flops 5552209920 | bytes 15466496 | tf_op jit(solution)/shard_map/dot_general | solution.py:80
  358.2 20.5 %collective-permute-done.30 = bf16[320,1536]{1,0:T(8,128)(2,1)} collective-permute-done((bf16[320,1536]{1,0:T(8,128)(2,1)}, bf16[320,1536]{1,0:T(8,128)(2,1)}, u32[]{:S(2)}, u32[]{:S(2)}) %collective-permute-start.30) | collective-permute-done | bytes 983072 | tf_op jit(solution)/shard_map/ppermute | solution.py:105
  389.7 11.3 %fusion.174 = f32[1280,1536]{1,0:T(8,128)} fusion(bf16[1536,1536]{1,0:T(8,128)(2,1)} %all-gather.9.cloned.1.call-done, bf16[320,1536]{1,0:T(8,128)(2,1)} %collective-permute-done.19, bf16[320,1536]{1,0:T(8,128)(2,1)} %collective-permute-done.18, bf16[320,1536]{1,0:T(8,128)(2,1)} %collective-permute-done.17, bf16[320,1536]{1,0:T(8,128)(2,1)} %multiply_convert_fusion.9), kind=kOutput, calls=%fused_computation.395 | convolution fusion | flops 6055526400 | bytes 16515072 | tf_op jit(solution)/shard_map/dot_general | solution.py:80
  422.0 11.4 %fusion.173 = f32[1280,1536]{1,0:T(8,128)} fusion(bf16[1536,1536]{1,0:T(8,128)(2,1)} %all-gather.13.cloned.1.call-done, bf16[320,1536]{1,0:T(8,128)(2,1)} %collective-permute-done.19, bf16[320,1536]{1,0:T(8,128)(2,1)} %collective-permute-done.18, bf16[320,1536]{1,0:T(8,128)(2,1)} %collective-permute-done.17, bf16[320,1536]{1,0:T(8,128)(2,1)} %multiply_convert_fusion.9), kind=kOutput, calls=%fused_computation.394 | convolution fusion | flops 6055526400 | bytes 16515072 | tf_op jit(solution)/shard_map/dot_general | solution.py:80
  433.5 11.4 %multiply_convert_fusion.3 = (bf16[1280,768]{1,0:T(8,128)(2,1)}, bf16[1280,768]{1,0:T(8,128)(2,1)}, bf16[1280,768]{1,0:T(8,128)(2,1)}) fusion(f32[1280,1536]{1,0:T(8,128)} %fusion.173, bf16[1536,768]{1,0:T(8,128)(2,1)} %all-gather.15.cloned.1.call-done, bf16[320,1536]{1,0:T(8,128)(2,1)} %collective-permute-done.31, ...), kind=kOutput, calls=%fused_computation.32 | convolution fusion | flops 3050373120 | bytes 20054016 | tf_op jit(solution)/shard_map/dot_general | solution.py:76
  493.0 20.1 %collective-permute-done.33 = bf16[320,1536]{1,0:T(8,128)(2,1)} collective-permute-done((bf16[320,1536]{1,0:T(8,128)(2,1)}, bf16[320,1536]{1,0:T(8,128)(2,1)}, u32[]{:S(2)}, u32[]{:S(2)}) %collective-permute-start.33) | collective-permute-done | bytes 983072 | tf_op jit(solution)/shard_map/ppermute | solution.py:105
  516.7 17.4 %collective-permute-done.28 = bf16[320,1536]{1,0:T(8,128)(2,1)S(1)} collective-permute-done((bf16[320,1536]{1,0:T(8,128)(2,1)S(1)}, bf16[320,1536]{1,0:T(8,128)(2,1)S(1)}, u32[]{:S(2)}, u32[]{:S(2)}) %collective-permute-start.28) | collective-permute-done | bytes 983072 | tf_op jit(solution)/shard_map/ppermute | solution.py:105
  534.0 20.1 %collective-permute-done.27 = bf16[320,1536]{1,0:T(8,128)(2,1)S(1)} collective-permute-done((bf16[320,1536]{1,0:T(8,128)(2,1)S(1)}, bf16[320,1536]{1,0:T(8,128)(2,1)S(1)}, u32[]{:S(2)}, u32[]{:S(2)}) %collective-permute-start.27) | collective-permute-done | bytes 983072 | tf_op jit(solution)/shard_map/ppermute | solution.py:105
  568.9 11.9 %collective-permute-done.51 = bf16[768,384]{1,0:T(8,128)(2,1)S(1)} collective-permute-done((bf16[768,384]{1,0:T(8,128)(2,1)S(1)}, bf16[768,384]{1,0:T(8,128)(2,1)S(1)}, u32[]{:S(2)}, u32[]{:S(2)}) %collective-permute-start.51) | collective-permute-done | bytes 589856 | tf_op jit(solution)/shard_map/ppermute | solution.py:105
  580.8 11.7 %collective-permute-done.49 = bf16[768,384]{1,0:T(8,128)(2,1)S(1)} collective-permute-done((bf16[768,384]{1,0:T(8,128)(2,1)S(1)}, bf16[768,384]{1,0:T(8,128)(2,1)S(1)}, u32[]{:S(2)}, u32[]{:S(2)}) %collective-permute-start.49) | collective-permute-done | bytes 589856 | tf_op jit(solution)/shard_map/ppermute | solution.py:105
  618.7 11.4 %convolution_convert_fusion = bf16[1408,1536]{1,0:T(8,128)(2,1)} fusion(bf16[1280,704]{1,0:T(8,128)(2,1)} %get-tuple-element.241, bf16[1280,704]{1,0:T(8,128)(2,1)S(1)} %copy-done.100, bf16[320,1536]{1,0:T(8,128)(2,1)} %collective-permute-done.19, bf16[320,1536]{1,0:T(8,128)(2,1)} %collective-permute-done.18, ...), kind=kOutput, calls=%fused_computation.18 | convolution fusion | flops 5561581568 | bytes 11862016 | tf_op jit(solution)/shard_map/dot_general | solution.py:86
  670.5 16.9 %fusion = (f32[2,6,320]{2,1,0:T(8,128)S(1)}, f32[2,1280,320,6]{1,2,3,0:T(8,128)}) fusion(f32[2,6,320,1280]{3,2,1,0:T(8,128)} %get-tuple-element.331, f32[2,6,320]{2,1,0:T(8,128)S(1)} %log_add_fusion, bf16[1280,2,128,1]{0,2,3,1:T(8,128)(2,1)S(1)} %bitcast.471, bf16[320,2,6,128]{0,3,2,1:T(8,128)(2,1)S(1)} %bitcast.452), kind=kOutput, calls=%fused_computation.2 | convolution fusion | flops 1273032960 | bytes 40990720 | tf_op jit(solution)/shard_map/tkhd,skd->khts/dot_general | solution.py:399
  687.3 13.7 %fusion.2 = bf16[2,6,320,1280]{3,2,1,0:T(8,128)(2,1)S(1)} fusion(f32[2,1280,320,6]{1,2,3,0:T(8,128)} %get-tuple-element.337, f32[2,6,320,1280]{3,2,1,0:T(8,128)} %get-tuple-element.331, f32[2,6,320]{2,1,0:T(8,128)S(1)} %get-tuple-element.336, f32[2,6,320]{2,1,0:T(8,128)S(1)} %log_add_fusion), kind=kLoop, calls=%fused_computation.4 | loop fusion | flops 19660800 | bytes 49182720 | tf_op jit(solution)/shard_map/convert_element_type | solution.py:202
  705.2 12.1 %fusion.5 = f32[2,128,1280,1]{2,1,3,0:T(8,128)} fusion(bf16[320,2,6,128]{0,3,2,1:T(8,128)(2,1)} %bitcast.453, f32[2,6,320,1280]{3,2,1,0:T(8,128)} %get-tuple-element.331, f32[2,6,320]{2,1,0:T(8,128)S(1)} %log_add_fusion), kind=kOutput, calls=%fused_computation.11 | convolution fusion | flops 1268121600 | bytes 21969920 | tf_op jit(solution)/shard_map/khts,tkhd->skd/dot_general | solution.py:410
  777.1 12.4 %collective-permute-done.44 = bf16[1024,384]{1,0:T(8,128)(2,1)S(1)} collective-permute-done((bf16[1024,384]{1,0:T(8,128)(2,1)S(1)}, bf16[1024,384]{1,0:T(8,128)(2,1)S(1)}, u32[]{:S(2)}, u32[]{:S(2)}) %collective-permute-start.44) | collective-permute-done | bytes 786464 | tf_op jit(solution)/shard_map/ppermute | solution.py:105
  789.5 15.9 %collective-permute-done.42 = bf16[1024,384]{1,0:T(8,128)(2,1)S(1)} collective-permute-done((bf16[1024,384]{1,0:T(8,128)(2,1)S(1)}, bf16[1024,384]{1,0:T(8,128)(2,1)S(1)}, u32[]{:S(2)}, u32[]{:S(2)}) %collective-permute-start.42) | collective-permute-done | bytes 786464 | tf_op jit(solution)/shard_map/ppermute | solution.py:105
  812.9 38.3 %psum.14 = f32[8,640]{1,0:T(8,128)S(1)} all-reduce(f32[8,640]{1,0:T(8,128)S(1)} %reshape.435), channel_id=1, replica_groups=mesh['dp'=4,'fsdp'=8] {'dp','fsdp'}, use_global_device_ids=true, to_apply=%region_22.23 | all-reduce | flops 5120 | bytes 40960 | tf_op jit(solution)/shard_map/psum | solution.py:448
  862.7 28.4 %reduce-scatter.13.cloned.1.call-done = bf16[192,1536]{1,0:T(8,128)(2,1)} async-done(((bf16[1536,1536]{1,0:T(8,128)(2,1)}), bf16[192,1536]{1,0:T(8,128)(2,1)}) %reduce-scatter.13.cloned.1.call-update) | async-done | bytes 589840 | tf_op jit(solution)/shard_map/reduce_scatter | solution.py:359
  930.5 40.0 %psum.15 = f32[]{:T(128)} all-reduce(f32[]{:T(128)S(6)} %add.525), channel_id=1, replica_groups=mesh['dp'=4,'fsdp'=8] {'dp','fsdp'}, use_global_device_ids=true, to_apply=%region_24.25 | all-reduce | flops 1 | bytes 8 | tf_op jit(solution)/shard_map/psum | solution.py:491
  (607 shorter events, 525.4 us)
Async XLA Ops:
  7.2 329.9 %all-gather.17.cloned.1.call-start = ((), (), s32[]{:S(2)}) async-start(), calls=%async_computation.12 | async-start | bytes 4866048 | tf_op jit(solution)/shard_map/all_gather | solution.py:264
  34.8 343.9 %all-gather.19.cloned.1.call-start = ((), (), s32[]{:S(2)}) async-start(), calls=%async_computation.13 | async-start | bytes 2654208 | tf_op jit(solution)/shard_map/all_gather | solution.py:267
  64.0 325.6 %all-gather.9.cloned.1.call-start = ((), (), s32[]{:S(2)}) async-start(), calls=%async_computation.8 | async-start | bytes 5308416 | tf_op jit(solution)/shard_map/all_gather | solution.py:264
  65.9 335.1 %all-gather.11.cloned.1.call-start = ((), (), s32[]{:S(2)}) async-start(), calls=%async_computation.9 | async-start | bytes 2654208 | tf_op jit(solution)/shard_map/all_gather | solution.py:267
  69.7 352.4 %all-gather.13.cloned.1.call-start = ((), (), s32[]{:S(2)}) async-start(), calls=%async_computation.10 | async-start | bytes 5308416 | tf_op jit(solution)/shard_map/all_gather | solution.py:264
  94.9 77.0 %collective-permute-start.2 = (bf16[1024,384]{0,1:T(8,128)(2,1)S(1)}, bf16[1024,384]{0,1:T(8,128)(2,1)}, u32[]{:S(2)}, u32[]{:S(2)}) collective-permute-start(bf16[1024,384]{0,1:T(8,128)(2,1)S(1)} %all_gather.32), channel_id=1, source_target_pairs={{0,24},{8,16},{16,8},{24,0},{1,25},{9,17},{17,9},{25,1},{2,26},{10... | collective-permute-start | bytes 2359304 | tf_op jit(solution)/shard_map/ppermute | solution.py:105
  97.3 74.8 %collective-permute-start = (bf16[1024,384]{0,1:T(8,128)(2,1)S(1)}, bf16[1024,384]{0,1:T(8,128)(2,1)}, u32[]{:S(2)}, u32[]{:S(2)}) collective-permute-start(bf16[1024,384]{0,1:T(8,128)(2,1)S(1)} %all_gather.32), channel_id=1, source_target_pairs={{0,8},{8,0},{16,24},{24,16},{1,9},{9,1},{17,25},{25,17},{2,10},{10... | collective-permute-start | bytes 2359304 | tf_op jit(solution)/shard_map/ppermute | solution.py:105
  97.9 78.3 %collective-permute-start.1 = (bf16[1024,384]{0,1:T(8,128)(2,1)S(1)}, bf16[1024,384]{0,1:T(8,128)(2,1)}, u32[]{:S(2)}, u32[]{:S(2)}) collective-permute-start(bf16[1024,384]{0,1:T(8,128)(2,1)S(1)} %all_gather.32), channel_id=1, source_target_pairs={{0,16},{8,24},{16,0},{24,8},{1,17},{9,25},{17,1},{25,9},{2,18},{10... | collective-permute-start | bytes 2359304 | tf_op jit(solution)/shard_map/ppermute | solution.py:105
  98.4 79.7 %collective-permute-start.3 = (bf16[1024,384]{0,1:T(8,128)(2,1)S(1)}, bf16[1024,384]{0,1:T(8,128)(2,1)}, u32[]{:S(2)}, u32[]{:S(2)}) collective-permute-start(bf16[1024,384]{0,1:T(8,128)(2,1)S(1)} %all_gather.32), channel_id=1, source_target_pairs={{0,1},{1,0},{2,3},{3,2},{4,5},{5,4},{6,7},{7,6},{8,9},{9,8},{10,11... | collective-permute-start | bytes 2359304 | tf_op jit(solution)/shard_map/ppermute | solution.py:110
  121.8 91.2 %collective-permute-start.12 = (bf16[768,384]{1,0:T(8,128)(2,1)}, bf16[768,384]{1,0:T(8,128)(2,1)}, u32[]{:S(2)}, u32[]{:S(2)}) collective-permute-start(bf16[768,384]{1,0:T(8,128)(2,1)} %all_gather.33), channel_id=1, source_target_pairs={{0,24},{8,16},{16,8},{24,0},{1,25},{9,17},{17,9},{25,1},{2,26},{10... | collective-permute-start | bytes 1769480 | tf_op jit(solution)/shard_map/ppermute | solution.py:105
  171.9 261.6 %all-gather.15.cloned.1.call-start = ((), (), s32[]{:S(2)}) async-start(), calls=%async_computation.11 | async-start | bytes 2654208 | tf_op jit(solution)/shard_map/all_gather | solution.py:267
  294.9 63.3 %collective-permute-start.31 = (bf16[320,1536]{1,0:T(8,128)(2,1)}, bf16[320,1536]{1,0:T(8,128)(2,1)}, u32[]{:S(2)}, u32[]{:S(2)}) collective-permute-start(bf16[320,1536]{1,0:T(8,128)(2,1)} %fusion.47), channel_id=1, source_target_pairs={{0,24},{8,16},{16,8},{24,0},{1,25},{9,17},{17,9},{25,1},{2,26},{10... | collective-permute-start | bytes 2949128 | tf_op jit(solution)/shard_map/ppermute | solution.py:105
  296.6 82.1 %collective-permute-start.30 = (bf16[320,1536]{1,0:T(8,128)(2,1)}, bf16[320,1536]{1,0:T(8,128)(2,1)}, u32[]{:S(2)}, u32[]{:S(2)}) collective-permute-start(bf16[320,1536]{1,0:T(8,128)(2,1)} %fusion.47), channel_id=1, source_target_pairs={{0,16},{8,24},{16,0},{24,8},{1,17},{9,25},{17,1},{25,9},{2,18},{10... | collective-permute-start | bytes 2949128 | tf_op jit(solution)/shard_map/ppermute | solution.py:105
  299.3 552.6 %reduce-scatter.11.cloned.1.call-start = ((), (), s32[]{:S(2)}) async-start(), calls=%async_computation.15 | async-start | bytes 737280 | tf_op jit(solution)/shard_map/reduce_scatter | solution.py:191
  316.0 62.7 %collective-permute-start.29 = (bf16[320,1536]{1,0:T(8,128)(2,1)}, bf16[320,1536]{1,0:T(8,128)(2,1)}, u32[]{:S(2)}, u32[]{:S(2)}) collective-permute-start(bf16[320,1536]{1,0:T(8,128)(2,1)} %fusion.47), channel_id=1, source_target_pairs={{0,8},{8,0},{16,24},{24,16},{1,9},{9,1},{17,25},{25,17},{2,10},{10... | collective-permute-start | bytes 2949128 | tf_op jit(solution)/shard_map/ppermute | solution.py:105
  484.0 70.1 %collective-permute-start.27 = (bf16[320,1536]{1,0:T(8,128)(2,1)S(1)}, bf16[320,1536]{1,0:T(8,128)(2,1)S(1)}, u32[]{:S(2)}, u32[]{:S(2)}) collective-permute-start(bf16[320,1536]{1,0:T(8,128)(2,1)S(1)} %get-tuple-element.250), channel_id=1, source_target_pairs={{0,16},{8,24},{16,0},{24,8},{1,17},{9,25},{17,1},{25,9},{2,18},{10... | collective-permute-start | bytes 2949128 | tf_op jit(solution)/shard_map/ppermute | solution.py:105
  491.9 62.1 %collective-permute-start.26 = (bf16[320,1536]{1,0:T(8,128)(2,1)S(1)}, bf16[320,1536]{1,0:T(8,128)(2,1)S(1)}, u32[]{:S(2)}, u32[]{:S(2)}) collective-permute-start(bf16[320,1536]{1,0:T(8,128)(2,1)S(1)} %get-tuple-element.248), channel_id=1, source_target_pairs={{0,8},{8,0},{16,24},{24,16},{1,9},{9,1},{17,25},{25,17},{2,10},{10... | collective-permute-start | bytes 2949128 | tf_op jit(solution)/shard_map/ppermute | solution.py:105
  593.6 259.9 %reduce-scatter.23.cloned.1.call-start = ((), (), s32[]{:S(2)}) async-start(), calls=%async_computation.21 | async-start | bytes 2654208 | tf_op jit(solution)/shard_map/reduce_scatter | solution.py:354
  600.5 254.4 %reduce-scatter.21.cloned.1.call-start = ((), (), s32[]{:S(2)}) async-start(), calls=%async_computation.20 | async-start | bytes 2654208 | tf_op jit(solution)/shard_map/reduce_scatter | solution.py:354
  608.9 247.4 %reduce-scatter.19.cloned.1.call-start = ((), (), s32[]{:S(2)}) async-start(), calls=%async_computation.19 | async-start | bytes 2654208 | tf_op jit(solution)/shard_map/reduce_scatter | solution.py:354
  617.2 245.5 %reduce-scatter.17.cloned.1.call-start = ((), (), s32[]{:S(2)}) async-start(), calls=%async_computation.18 | async-start | bytes 4866048 | tf_op jit(solution)/shard_map/reduce_scatter | solution.py:359
  630.1 232.6 %reduce-scatter.15.cloned.1.call-start = ((), (), s32[]{:S(2)}) async-start(), calls=%async_computation.17 | async-start | bytes 5308416 | tf_op jit(solution)/shard_map/reduce_scatter | solution.py:359
  642.0 249.2 %reduce-scatter.13.cloned.1.call-start = ((), (), s32[]{:S(2)}) async-start(), calls=%async_computation.16 | async-start | bytes 5308416 | tf_op jit(solution)/shard_map/reduce_scatter | solution.py:359
  656.7 259.0 %reduce-scatter.9.cloned.1.call-start = ((), (), s32[]{:S(2)}) async-start(), calls=%async_computation.14 | async-start | bytes 983040 | tf_op jit(solution)/shard_map/reduce_scatter | solution.py:191
  (155 other events, 2066.7 us)
Sparse Core Ops, SparseCore 0:
  35.0 56.9 all-gather.16
  94.2 38.0 all-gather.18
  134.5 51.5 all-gather.8
  188.1 30.9 all-gather.10
  221.2 50.3 all-gather.12
  299.5 28.7 all-gather.14
  593.8 19.3 reduce-scatter.10
  616.0 34.6 reduce-scatter.22
  653.6 35.3 reduce-scatter.20
  691.2 35.4 reduce-scatter.18
  729.0 50.5 reduce-scatter.16
  781.8 53.5 reduce-scatter.14
  837.8 53.3 reduce-scatter.12
  894.0 21.6 reduce-scatter.8

commit v2 on v1

v2 whole, which is shorter than its diff:
```python
import functools
import math

import jax
import jax.numpy as jnp
from jax import lax
from jax.experimental import pallas as pl
from jax.experimental.pallas import tpu as pltpu
from jax.sharding import PartitionSpec as P

D = 1536
HEADS = 12
KV_HEADS = 2
HEAD = 128
FF = 8960
STEP = 5
GROUP = 6
SMALL = 5120
QKV = 2048
KV_WIDTH = KV_HEADS * HEAD


NORM_EPS = 1e-06
ROPE_BASE = 1000000.0
BETA_FIRST = 0.5
BETA_SECOND = 0.5
ADAM_EPS = 1e-08
MATRIX_RATE = 0.03
SMALL_RATE = 0.3
MATRIX_DECAY = 0.1
CLIP_NORM = 1.0
MASKED = -1e30
SCALE = HEAD ** (-0.5)
CHUNKS = (1024, 1216)
UNIT_TILE = 512
TOKEN_TILE = 640
GRAD_TILE = 512
TURN_TILE = 256
VMEM_LIMIT = 60 * 2**20


def unpack_small(small_vec):
    grouped = small_vec.reshape(KV_HEADS * HEAD, 3 * GROUP + 2)
    gain_attn = grouped[:, :GROUP].reshape(-1)
    gain_mlp = grouped[:, GROUP : 2 * GROUP].reshape(-1)
    biases = jnp.concatenate(
        [
            grouped[:, 2 * GROUP : 3 * GROUP].reshape(-1),
            grouped[:, 3 * GROUP],
            grouped[:, 3 * GROUP + 1],
        ]
    )
    return (gain_attn, gain_mlp, biases)


def group_small(gain_attn, gain_mlp, biases):
    count = KV_HEADS * HEAD
    pieces = [
        gain_attn.reshape(count, GROUP),
        gain_mlp.reshape(count, GROUP),
        biases[:D].reshape(count, GROUP),
        biases[D : D + count][:, None],
        biases[D + count :][:, None],
    ]
    return jnp.concatenate(pieces, axis=1).reshape(8, SMALL // 8)


def rope_tables(positions):
    pair_index = jnp.arange(HEAD // 2, dtype=jnp.float32)
    inverse = jnp.power(jnp.float32(ROPE_BASE), -2.0 * pair_index / HEAD)
    angles = positions[:, None] * inverse[None, :]
    angles = jnp.concatenate([angles, angles], axis=-1)
    return (jnp.cos(angles), jnp.sin(angles))


def bf16(array):
    return array.astype(jnp.bfloat16)


def dot_nn(left, right):
    return jnp.dot(left, right, preferred_element_type=jnp.float32)


def dot_nt(left, right):
    return lax.dot_general(
        left, right, (((1,), (1,)), ((), ())), preferred_element_type=jnp.float32
    )


def dot_tn(left, right):
    return lax.dot_general(
        left, right, (((0,), (0,)), ((), ())), preferred_element_type=jnp.float32
    )


def update(weight, first, second, gradient, clip_factor, rate, decay):
    step_grad = gradient * clip_factor
    first_new = BETA_FIRST * first + (1.0 - BETA_FIRST) * step_grad
    second_new = BETA_SECOND * second + (1.0 - BETA_SECOND) * step_grad * step_grad
    first_fix = 1.0 - BETA_FIRST**STEP
    second_fix = 1.0 - BETA_SECOND**STEP
    weight_new = weight - rate * (
        first_new / first_fix / (jnp.sqrt(second_new / second_fix) + ADAM_EPS) + decay * weight
    )
    return (weight_new, first_new, second_new, weight_new.astype(jnp.bfloat16))


def dp_send(block, k):
    count = lax.axis_size("dp")
    return lax.ppermute(block, "dp", [(i, i ^ k) for i in range(count)])


def core_swap(block):
    count = lax.axis_size("fsdp")
    return lax.ppermute(block, "fsdp", [(i, i ^ 1) for i in range(count)])


def dp_gather(block):
    return [block] + [dp_send(block, k) for k in range(1, lax.axis_size("dp"))]


def dp_own(array, k):
    return lax.dynamic_index_in_dim(array, lax.axis_index("dp") ^ k, 0, keepdims=False)


def dp_exchange(array):
    count = lax.axis_size("dp")
    place = lax.axis_index("dp")
    got = jnp.stack([dp_own(array, 0)] + [dp_send(dp_own(array, k), k) for k in range(1, count)])
    return jnp.stack(
        [lax.dynamic_index_in_dim(got, place ^ a, 0, keepdims=False) for a in range(count)]
    )


def line_send(block, r):
    count = lax.axis_size("fsdp")
    return lax.ppermute(block, "fsdp", [(i, i ^ (2 * r)) for i in range(count)])


def line_gather(block):
    count = lax.axis_size("fsdp") // 2
    place = lax.axis_index("fsdp") // 2
    got = jnp.stack([block] + [line_send(block, r) for r in range(1, count)])
    return jnp.stack(
        [lax.dynamic_index_in_dim(got, place ^ a, 0, keepdims=False) for a in range(count)]
    )


def sum_everywhere(term):
    term = term + core_swap(term)
    lines = [line_send(term, r) for r in range(1, lax.axis_size("fsdp") // 2)]
    term = term + sum(lines)
    return term + sum(dp_send(term, k) for k in range(1, lax.axis_size("dp")))


def is_even():
    return lax.rem(lax.axis_index("fsdp"), 2) == 0


def gather_line(piece):
    return line_gather(piece).reshape(-1, piece.shape[1])


def gather_rest(along):
    own = dp_gather(along)
    return own, [core_swap(block) for block in own]


def reduce_matrix(own_terms, other_terms):
    summed = [
        mine.astype(jnp.float32) + core_swap(theirs).astype(jnp.float32)
        for mine, theirs in zip(own_terms, other_terms)
    ]
    total = summed[0]
    for k in range(1, len(summed)):
        total = total + dp_send(summed[k].astype(jnp.bfloat16), k).astype(jnp.float32)
    count = lax.axis_size("fsdp") // 2
    place = lax.axis_index("fsdp") // 2
    parts = total.reshape(count, -1, total.shape[1])
    shard = lax.dynamic_index_in_dim(parts, place, 0, keepdims=False)
    for r in range(1, count):
        part = lax.dynamic_index_in_dim(parts, place ^ r, 0, keepdims=False)
        shard = shard + line_send(bf16(part), r).astype(jnp.float32)
    return shard.T


def exchange_weights(half_in, half_down):
    ranks = lax.axis_size("dp")
    rows, columns = half_in.shape
    part = columns // ranks
    width = half_down.shape[1]
    slices = half_down.shape[0] // (ranks * part)
    in_sent = half_in.reshape(rows, ranks, part).transpose(1, 2, 0)
    down_sent = half_down.reshape(slices, ranks, part, width).transpose(1, 2, 0, 3)
    sent = jnp.concatenate([in_sent, down_sent.reshape(ranks, part, slices * width)], axis=2)
    got = yield sent
    in_piece = got[:, :, :rows].transpose(1, 0, 2).reshape(part, ranks * rows)
    down_piece = got[:, :, rows:].reshape(ranks, part, slices, width).transpose(3, 0, 2, 1)
    yield in_piece, down_piece.reshape(width, ranks * slices, part)


def exchange_gradients(in_grad, down_grad, columns):
    ranks = lax.axis_size("dp")
    part = in_grad.shape[0]
    rows = in_grad.shape[1] // ranks
    slices = down_grad.shape[1] // ranks
    in_sent = in_grad.reshape(part, ranks, rows).transpose(1, 0, 2)
    down_sent = down_grad.reshape(columns, ranks, slices, part).transpose(1, 3, 2, 0)
    sent = jnp.concatenate([in_sent, down_sent.reshape(ranks, part, slices * columns)], axis=2)
    got = dp_exchange(sent)
    return got[:, :, :rows], got[:, :, rows:].reshape(ranks, part, slices, columns)


def column_slices(own, other, first, target, width, slices):
    for j in range(slices):
        mine = own(j)
        theirs = other(j)
        target[:, pl.ds(2 * j * width, width)] = jnp.where(first, mine, theirs)
        target[:, pl.ds((2 * j + 1) * width, width)] = jnp.where(first, theirs, mine)


def block_columns(ref, place, k, width):
    return ref[:, pl.ds(pl.multiple_of((place ^ k) * width, 128), width)]


def project_kernel(ranks, slices, *refs):
    info, tokens, gain, bias, cosine, sine = refs[:6]
    own = refs[6 : 6 + ranks]
    other = refs[6 + ranks : 6 + 2 * ranks]
    normed, queries, kv, proj = refs[6 + 2 * ranks :]
    place = info[0]
    first = info[1] == 0
    width = own[0].shape[1]
    step = own[0].shape[0] // slices
    part = QKV // (2 * slices)
    x = tokens[...].astype(jnp.float32)
    scale = lax.rsqrt(jnp.mean(x * x, axis=-1, keepdims=True) + NORM_EPS)
    normed[...] = bf16(x * scale * gain[...])

    def product(mats, j):
        return sum(
            dot_nt(block_columns(normed, place, k, width), mats[k][pl.ds(j * step, part), :])
            for k in range(ranks)
        )

    column_slices(
        lambda j: product(own, j), lambda j: product(other, j), first, proj, part, slices
    )
    for h in range(HEADS + KV_HEADS):
        cols = pl.ds(h * HEAD, HEAD)
        u = proj[:, cols] + bias[:, cols]
        turned = bf16(u * cosine[...] + pltpu.roll(u, HEAD // 2, 1) * sine[...])
        if h < HEADS:
            queries[:, cols] = turned
        else:
            kv[:, pl.ds((h - HEADS) * HEAD, HEAD)] = turned
    cols = pl.ds(D + KV_WIDTH, KV_WIDTH)
    kv[:, pl.ds(KV_WIDTH, KV_WIDTH)] = bf16(proj[:, cols] + bias[:, cols])


def score_bias(info, rows, ranks, target):
    place = info[0]
    length = info[2]
    query = place * rows + lax.broadcasted_iota(jnp.int32, (rows, rows), 1)
    for k in range(ranks):
        key = (place ^ k) * rows + lax.broadcasted_iota(jnp.int32, (rows, rows), 0)
        seen = (key <= query) & (key < length)
        target[pl.ds(k * rows, rows), :] = jnp.where(seen, 0.0, MASKED)


def attend_kernel(ranks, slices, *refs):
    info, tokens, gain, queries = refs[:4]
    kv = refs[4 : 4 + ranks]
    own = refs[4 + ranks : 4 + 2 * ranks]
    other = refs[4 + 2 * ranks : 4 + 3 * ranks]
    attended, totals, middle, normed_again, bias, keys, values, values_t = refs[4 + 3 * ranks :]
    place = info[0]
    first = info[1] == 0
    rows = tokens.shape[0]
    width = own[0].shape[1]
    part = own[0].shape[0] // slices
    score_bias(info, rows, ranks, bias)
    for k in range(ranks):
        keys[pl.ds(k * rows, rows), :] = kv[k][:, pl.ds(0, KV_WIDTH)]
        values[pl.ds(k * rows, rows), :] = kv[k][:, pl.ds(KV_WIDTH, KV_WIDTH)]
    values_t[...] = values[...].T

    @pl.loop(0, HEADS)
    def _(h):
        cols = pl.ds(pl.multiple_of(h * HEAD, HEAD), HEAD)
        kv_cols = pl.ds(pl.multiple_of((h // GROUP) * HEAD, HEAD), HEAD)
        scores = dot_nt(keys[:, kv_cols], queries[:, cols]) * SCALE + bias[...]
        peak = jnp.max(scores, axis=0, keepdims=True)
        exponent = jnp.exp(scores - peak)
        total = jnp.sum(exponent, axis=0, keepdims=True)
        totals[pl.ds(h, 1), :] = peak + jnp.log(total)
        probs = bf16(exponent * (1.0 / total))
        attended[:, cols] = bf16(dot_nn(values_t[kv_cols, :], probs).T)

    def product(mats, j):
        return sum(
            dot_nt(block_columns(attended, place, k, width), mats[k][pl.ds(j * part, part), :])
            for k in range(ranks)
        )

    column_slices(
        lambda j: product(own, j), lambda j: product(other, j), first, middle, part, slices
    )
    total = middle[...] + tokens[...].astype(jnp.float32)
    middle[...] = total
    scale = lax.rsqrt(jnp.mean(total * total, axis=-1, keepdims=True) + NORM_EPS)
    normed_again[...] = bf16(total * scale * gain[...])


def attend_back_kernel(ranks, slices, *refs):
    info, middle, cotangent, gain, queries, totals = refs[:6]
    got = refs[6 : 6 + ranks]
    kv = refs[6 + ranks : 6 + 2 * ranks]
    own = refs[6 + 2 * ranks : 6 + 3 * ranks]
    other = refs[6 + 3 * ranks : 6 + 4 * ranks]
    refs = refs[6 + 4 * ranks :]
    middle_cot, middle_low, gain_grad, query_cot = refs[:4]
    kv_cot = refs[4 : 4 + ranks]
    bias, keys, values, keys_t, attended_cot, key_sum, value_sum, low_own, low_other = refs[
        4 + ranks :
    ]
    place = info[0]
    first = info[1] == 0
    rows = middle.shape[0]
    width = own[0].shape[1]
    part = own[0].shape[0] // slices
    position = place * rows + lax.broadcasted_iota(jnp.int32, (rows, 1), 0)
    valid = jnp.where(position < info[2], 1.0, 0.0)
    cot = got[0][...].astype(jnp.float32)
    for k in range(1, ranks):
        cot = cot + got[k][...].astype(jnp.float32)
    v = middle[...]
    scale = lax.rsqrt(jnp.mean(v * v, axis=-1, keepdims=True) + NORM_EPS)
    n = v * scale
    gain_grad[...] = jnp.sum(cot * n, axis=0, keepdims=True)
    scaled = cot * gain[...]
    back = scale * (scaled - n * jnp.mean(scaled * n, axis=-1, keepdims=True))
    back = back + cotangent[...].astype(jnp.float32) * valid
    middle_cot[...] = back
    middle_low[...] = bf16(back)
    for j in range(slices):
        even = middle_low[:, pl.ds(2 * j * part, part)]
        odd = middle_low[:, pl.ds((2 * j + 1) * part, part)]
        low_own[:, pl.ds(j * part, part)] = jnp.where(first, even, odd)
        low_other[:, pl.ds(j * part, part)] = jnp.where(first, odd, even)
    for k in range(ranks):
        cols = pl.ds(pl.multiple_of((place ^ k) * width, 128), width)
        attended_cot[:, cols] = bf16(
            dot_nn(low_own[...], own[k][...]) + dot_nn(low_other[...], other[k][...])
        )
    score_bias(info, rows, ranks, bias)
    for k in range(ranks):
        keys[pl.ds(k * rows, rows), :] = kv[k][:, pl.ds(0, KV_WIDTH)]
        values[pl.ds(k * rows, rows), :] = kv[k][:, pl.ds(KV_WIDTH, KV_WIDTH)]
    keys_t[...] = keys[...].T
    key_sum[...] = jnp.zeros_like(key_sum)
    value_sum[...] = jnp.zeros_like(value_sum)

    @pl.loop(0, HEADS)
    def _(h):
        cols = pl.ds(pl.multiple_of(h * HEAD, HEAD), HEAD)
        kv_cols = pl.ds(pl.multiple_of((h // GROUP) * HEAD, HEAD), HEAD)
        query = queries[:, cols]
        out_cot = attended_cot[:, cols]
        scores = dot_nt(keys[:, kv_cols], query) * SCALE + bias[...]
        probs = jnp.exp(scores - totals[pl.ds(h, 1), :])
        probs_cot = dot_nt(values[:, kv_cols], out_cot)
        row_dot = jnp.sum(probs * probs_cot, axis=0, keepdims=True)
        scores_cot = bf16(probs * (probs_cot - row_dot))
        value_sum[:, kv_cols] += dot_nn(bf16(probs), out_cot)
        key_sum[:, kv_cols] += dot_nn(scores_cot, query)
        query_cot[:, cols] = dot_nn(keys_t[kv_cols, :], scores_cot).T * SCALE

    for k in range(ranks):
        at = pl.ds(k * rows, rows)
        kv_cot[k][:, pl.ds(0, KV_WIDTH)] = bf16(key_sum[at, :] * SCALE)
        kv_cot[k][:, pl.ds(KV_WIDTH, KV_WIDTH)] = bf16(value_sum[at, :])


def outer_kernel(ranks, slices, *refs):
    info, left, right = refs[:3]
    own = refs[3 : 3 + ranks]
    other = refs[3 + ranks : 3 + 2 * ranks]
    (turned,) = refs[3 + 2 * ranks :]
    place = info[0]
    parity = info[1]
    width = own[0].shape[1]
    part = own[0].shape[0] // slices
    turned[...] = right[...].T
    for k in range(ranks):
        block = block_columns(left, place, k, width)
        for j in range(slices):
            at = pl.ds(j * part, part)
            mine = pl.ds(pl.multiple_of((2 * j + parity) * part, 16), part)
            theirs = pl.ds(pl.multiple_of((2 * j + 1 - parity) * part, 16), part)
            own[k][at, :] = bf16(dot_nn(turned[mine, :], block))
            other[k][at, :] = bf16(dot_nn(turned[theirs, :], block))


def project_back_kernel(ranks, *refs):
    info, query_cot, cosine, sine = refs[:4]
    got = refs[4 : 4 + ranks]
    projected_low, bias_grad = refs[4 + ranks :]
    kv_cot = got[0][...].astype(jnp.float32)
    for k in range(1, ranks):
        kv_cot = kv_cot + got[k][...].astype(jnp.float32)
    for h in range(HEADS + 2 * KV_HEADS):
        cols = pl.ds(h * HEAD, HEAD)
        if h < HEADS:
            u = query_cot[:, cols]
        else:
            u = kv_cot[:, (h - HEADS) * HEAD : (h - HEADS + 1) * HEAD]
        if h < HEADS + KV_HEADS:
            u = u * cosine[...] + pltpu.roll(u * sine[...], HEAD // 2, 1)
        bias_grad[:, cols] = jnp.sum(u, axis=0, keepdims=True)
        projected_low[:, cols] = bf16(u)


def input_back_kernel(ranks, slices, *refs):
    info, projected_low, tokens, gain, middle_cot = refs[:5]
    own = refs[5 : 5 + ranks]
    other = refs[5 + ranks : 5 + 2 * ranks]
    input_grad, gain_grad, low_own, low_other, normed_cot = refs[5 + 2 * ranks :]
    place = info[0]
    first = info[1] == 0
    width = own[0].shape[1]
    step = own[0].shape[0] // slices
    part = QKV // (2 * slices)
    for j in range(slices):
        even = projected_low[:, pl.ds(2 * j * part, part)]
        odd = projected_low[:, pl.ds((2 * j + 1) * part, part)]
        low_own[:, pl.ds(j * part, part)] = jnp.where(first, even, odd)
        low_other[:, pl.ds(j * part, part)] = jnp.where(first, odd, even)
    for k in range(ranks):
        cols = pl.ds(pl.multiple_of((place ^ k) * width, 128), width)
        normed_cot[:, cols] = sum(
            dot_nn(low[:, pl.ds(j * part, part)], mats[k][pl.ds(j * step, part), :])
            for low, mats in ((low_own, own), (low_other, other))
            for j in range(slices)
        )
    x = tokens[...].astype(jnp.float32)
    scale = lax.rsqrt(jnp.mean(x * x, axis=-1, keepdims=True) + NORM_EPS)
    n = x * scale
    cot = normed_cot[...]
    gain_grad[...] = jnp.sum(cot * n, axis=0, keepdims=True)
    scaled = cot * gain[...]
    back = scale * (scaled - n * jnp.mean(scaled * n, axis=-1, keepdims=True))
    input_grad[...] = bf16(middle_cot[...] + back)


def call(kernel, args, outs, scratch, flops):
    vmem = pl.BlockSpec(memory_space=pltpu.VMEM)
    moved = sum(math.prod(a.shape) * a.dtype.itemsize for a in args)
    moved += sum(math.prod(a.shape) * a.dtype.itemsize for a in outs)
    return pl.pallas_call(
        kernel,
        out_shape=tuple(outs),
        in_specs=[pl.BlockSpec(memory_space=pltpu.SMEM)] + [vmem] * (len(args) - 1),
        out_specs=(vmem,) * len(outs),
        scratch_shapes=scratch,
        compiler_params=pltpu.CompilerParams(vmem_limit_bytes=VMEM_LIMIT),
        cost_estimate=pl.CostEstimate(flops=flops, bytes_accessed=moved, transcendentals=0),
    )(*args)


def f32_like(*shape):
    return jax.ShapeDtypeStruct(shape, jnp.float32)


def bf16_like(*shape):
    return jax.ShapeDtypeStruct(shape, jnp.bfloat16)


def fetch(source, target, sem):
    copy = pltpu.make_async_copy(source, target, sem)
    copy.start()
    return copy


def unit_blocks(units):
    return [(s, min(UNIT_TILE, units - s)) for s in range(0, units, UNIT_TILE)]


def transpose_tokens(source, target, tokens):
    @pl.loop(0, tokens // TURN_TILE)
    def _(t):
        at = pl.multiple_of(t * TURN_TILE, TURN_TILE)
        target[:, pl.ds(at, TURN_TILE)] = source[pl.ds(at, TURN_TILE), :].T


def load_chunk(units, ranks, refs, na, oc, w, d, sem, back=None, mixed=None):
    rows = refs["na"][0].shape[0]
    slot = 0
    first = []
    later = []

    def begin(source, target, into):
        nonlocal slot
        into.append(fetch(source, target, sem.at[slot]))
        slot += 1

    for k in range(ranks):
        begin(refs["na"][k], na.at[pl.ds(k * rows, rows)], first)
    for b, (s, n) in enumerate(unit_blocks(units)):
        for half in range(2):
            at = pl.ds(half * units + s, n)
            begin(refs["w"].at[at], w.at[at], later if b else first)
        if b == 0:
            for k in range(ranks):
                begin(refs["oc"][k], oc.at[pl.ds(k * rows, rows)], first)
            begin(refs["d"], d, first)
            if back is not None:
                begin(refs["back"], back, first)
                begin(refs["mixed"], mixed, first)
    for copy in first:
        copy.wait()
    return later


def unit_block(units, s, n, tokens, na, oc, w, d, back, mixed, gt, ut, ht, at_row, add, final):
    wg = w.at[pl.ds(s, n)]
    wu = w.at[pl.ds(units + s, n)]
    db = d.at[:, pl.ds(s, n)]

    @pl.loop(0, tokens // TOKEN_TILE)
    def _(t):
        at = pl.ds(pl.multiple_of(t * TOKEN_TILE, TOKEN_TILE), TOKEN_TILE)
        gate = dot_nt(na[at, :], wg[...])
        up = dot_nt(na[at, :], wu[...])
        hidden_cot = dot_nn(oc[at, :], db[...])
        sigmoid = 1.0 / (1.0 + jnp.exp(-gate))
        activated = gate * sigmoid
        hidden = bf16(activated * up)
        gate_cot = bf16(hidden_cot * up * sigmoid * (1.0 + gate * (1.0 - sigmoid)))
        up_cot = bf16(hidden_cot * activated)
        ht[pl.ds(at_row, n), at] = hidden.T
        gt[pl.ds(at_row, n), at] = gate_cot.T
        ut[pl.ds(at_row, n), at] = up_cot.T
        back_term = dot_nn(gate_cot, wg[...]) + dot_nn(up_cot, wu[...])
        mixed_term = dot_nt(hidden, db[...])
        if add:
            back_term = back_term + back[at, :]
            mixed_term = mixed_term + mixed[at, :]
        if final:
            na[at, :] = bf16(back_term)
            oc[at, :] = bf16(mixed_term)
        else:
            back[at, :] = back_term
            mixed[at, :] = mixed_term


def gradient_block(units, s, n, na, oc_t, gt, ut, ht, at_row, dw, dd):
    at = pl.ds(at_row, n)

    @pl.loop(0, D // GRAD_TILE)
    def _(j):
        cols = pl.ds(pl.multiple_of(j * GRAD_TILE, GRAD_TILE), GRAD_TILE)
        dw[pl.ds(s, n), cols] = bf16(dot_nn(gt[at, :], na[:, cols]))
        dw[pl.ds(units + s, n), cols] = bf16(dot_nn(ut[at, :], na[:, cols]))
        dd[cols, pl.ds(s, n)] = bf16(dot_nt(oc_t[cols, :], ht[at, :]))


def first_chunk_kernel(units, ranks, *refs):
    ins = {"na": refs[:ranks], "oc": refs[ranks : 2 * ranks]}
    refs = refs[2 * ranks :]
    ins["w"], ins["d"] = refs[:2]
    back_out, mixed_out, dw_out, dd_out = refs[2:6]
    na, oc, oc_t, w, d, dw, dd, back, mixed, gt, ut, ht, in_sem, out_sem = refs[6:]
    tokens = na.shape[0]
    later = load_chunk(units, ranks, ins, na, oc, w, d, in_sem)
    transpose_tokens(oc, oc_t, tokens)
    blocks = unit_blocks(units)
    outs = []
    for b, (s, n) in enumerate(blocks):
        if b:
            later[2 * b - 2].wait()
            later[2 * b - 1].wait()
        unit_block(
            units, s, n, tokens, na, oc, w, d, back, mixed, gt, ut, ht, 0, bool(b), False
        )
        if b == len(blocks) - 1:
            outs.append(fetch(back, back_out, out_sem.at[0]))
            outs.append(fetch(mixed, mixed_out, out_sem.at[1]))
        gradient_block(units, s, n, na, oc_t, gt, ut, ht, 0, dw, dd)
        for half in range(2):
            at = pl.ds(half * units + s, n)
            outs.append(fetch(dw.at[at], dw_out.at[at], out_sem.at[3 + 2 * b + half]))
    outs.append(fetch(dd, dd_out, out_sem.at[2]))
    for copy in outs:
        copy.wait()


def last_chunk_kernel(units, ranks, carried, *refs):
    ins = {"na": refs[:ranks], "oc": refs[ranks : 2 * ranks]}
    refs = refs[2 * ranks :]
    ins["w"], ins["d"] = refs[:2]
    refs = refs[2:]
    if carried:
        ins["back"], ins["mixed"] = refs[:2]
        refs = refs[2:]
    back_out = refs[:ranks]
    mixed_out = refs[ranks : 2 * ranks]
    gt_out, ut_out, ht_out = refs[2 * ranks : 2 * ranks + 3]
    na, oc, w, d, back, mixed, gt, ut, ht, in_sem, out_sem = refs[2 * ranks + 3 :]
    tokens = na.shape[0]
    rows = tokens // ranks
    if carried:
        later = load_chunk(units, ranks, ins, na, oc, w, d, in_sem, back, mixed)
    else:
        later = load_chunk(units, ranks, ins, na, oc, w, d, in_sem)
    blocks = unit_blocks(units)
    outs = []
    for b, (s, n) in enumerate(blocks):
        if b:
            later[2 * b - 2].wait()
            later[2 * b - 1].wait()
        unit_block(
            units,
            s,
            n,
            tokens,
            na,
            oc,
            w,
            d,
            back,
            mixed,
            gt,
            ut,
            ht,
            s,
            carried or bool(b),
            b == len(blocks) - 1,
        )
        for i, (kept, target) in enumerate(((gt, gt_out), (ut, ut_out), (ht, ht_out))):
            at = pl.ds(s, n)
            outs.append(fetch(kept.at[at], target.at[at], out_sem.at[2 * ranks + 3 * b + i]))
    for k in range(ranks):
        at = pl.ds(k * rows, rows)
        outs.append(fetch(na.at[at], back_out[k], out_sem.at[k]))
        outs.append(fetch(oc.at[at], mixed_out[k], out_sem.at[ranks + k]))
    for copy in outs:
        copy.wait()


def gradient_kernel(units, ranks, *refs):
    na_in = refs[:ranks]
    oc_in = refs[ranks : 2 * ranks]
    gt_in, ut_in, ht_in, dw_out, dd_out = refs[2 * ranks : 2 * ranks + 5]
    na, oc, oc_t, gt, ut, ht, dw, dd, in_sem, out_sem = refs[2 * ranks + 5 :]
    tokens = na.shape[0]
    rows = tokens // ranks
    copies = []
    for k in range(ranks):
        at = pl.ds(k * rows, rows)
        copies.append(fetch(oc_in[k], oc.at[at], in_sem.at[k]))
    for k in range(ranks):
        at = pl.ds(k * rows, rows)
        copies.append(fetch(na_in[k], na.at[at], in_sem.at[ranks + k]))
    for i, (source, kept) in enumerate(((gt_in, gt), (ut_in, ut), (ht_in, ht))):
        copies.append(fetch(source, kept, in_sem.at[2 * ranks + i]))
    for copy in copies[:ranks]:
        copy.wait()
    transpose_tokens(oc, oc_t, tokens)
    for copy in copies[ranks:]:
        copy.wait()
    outs = []
    for b, (s, n) in enumerate(unit_blocks(units)):
        gradient_block(units, s, n, na, oc_t, gt, ut, ht, s, dw, dd)
        for half in range(2):
            at = pl.ds(half * units + s, n)
            outs.append(fetch(dw.at[at], dw_out.at[at], out_sem.at[1 + 2 * b + half]))
    outs.append(fetch(dd, dd_out, out_sem.at[0]))
    for copy in outs:
        copy.wait()


def hbm_call(kernel, args, outs, scratch, flops):
    moved = sum(math.prod(a.shape) * a.dtype.itemsize for a in args)
    moved += sum(math.prod(a.shape) * a.dtype.itemsize for a in outs)
    anywhere = pl.BlockSpec(memory_space=pl.ANY)
    return pl.pallas_call(
        kernel,
        out_shape=tuple(outs),
        in_specs=[anywhere] * len(args),
        out_specs=(anywhere,) * len(outs),
        scratch_shapes=scratch,
        compiler_params=pltpu.CompilerParams(vmem_limit_bytes=VMEM_LIMIT),
        cost_estimate=pl.CostEstimate(flops=flops, bytes_accessed=moved, transcendentals=0),
    )(*args)


def vmem_bf16(*shape):
    return pltpu.VMEM(shape, jnp.bfloat16)


def vmem_f32(*shape):
    return pltpu.VMEM(shape, jnp.float32)


def first_chunk(na, oc, w, d):
    ranks = len(na)
    tokens = ranks * na[0].shape[0]
    units = d.shape[1]
    blocks = len(unit_blocks(units))
    scratch = [
        vmem_bf16(tokens, D),
        vmem_bf16(tokens, D),
        vmem_bf16(D, tokens),
        vmem_bf16(2 * units, D),
        vmem_bf16(D, units),
        vmem_bf16(2 * units, D),
        vmem_bf16(D, units),
        vmem_f32(tokens, D),
        vmem_f32(tokens, D),
        vmem_bf16(UNIT_TILE, tokens),
        vmem_bf16(UNIT_TILE, tokens),
        vmem_bf16(UNIT_TILE, tokens),
        pltpu.SemaphoreType.DMA((2 * ranks + 1 + 2 * blocks,)),
        pltpu.SemaphoreType.DMA((3 + 2 * blocks,)),
    ]
    outs = [
        f32_like(tokens, D),
        f32_like(tokens, D),
        bf16_like(2 * units, D),
        bf16_like(D, units),
    ]
    kernel = functools.partial(first_chunk_kernel, units, ranks)
    return hbm_call(kernel, [*na, *oc, w, d], outs, scratch, 18 * tokens * D * units)


def last_chunk(na, oc, w, d, carry):
    ranks = len(na)
    rows = na[0].shape[0]
    tokens = ranks * rows
    units = d.shape[1]
    blocks = len(unit_blocks(units))
    scratch = [
        vmem_bf16(tokens, D),
        vmem_bf16(tokens, D),
        vmem_bf16(2 * units, D),
        vmem_bf16(D, units),
        vmem_f32(tokens, D),
        vmem_f32(tokens, D),
        vmem_bf16(units, tokens),
        vmem_bf16(units, tokens),
        vmem_bf16(units, tokens),
        pltpu.SemaphoreType.DMA((2 * ranks + 3 + 2 * blocks,)),
        pltpu.SemaphoreType.DMA((2 * ranks + 3 * blocks,)),
    ]
    outs = [bf16_like(rows, D)] * (2 * ranks) + [bf16_like(units, tokens)] * 3
    kernel = functools.partial(last_chunk_kernel, units, ranks, bool(carry))
    got = hbm_call(kernel, [*na, *oc, w, d, *carry], outs, scratch, 12 * tokens * D * units)
    return got[:ranks], got[ranks : 2 * ranks], got[2 * ranks :]


def chunk_gradients(na, oc, kept):
    ranks = len(na)
    tokens = ranks * na[0].shape[0]
    units = kept[0].shape[0]
    blocks = len(unit_blocks(units))
    scratch = [
        vmem_bf16(tokens, D),
        vmem_bf16(tokens, D),
        vmem_bf16(D, tokens),
        vmem_bf16(units, tokens),
        vmem_bf16(units, tokens),
        vmem_bf16(units, tokens),
        vmem_bf16(2 * units, D),
        vmem_bf16(D, units),
        pltpu.SemaphoreType.DMA((2 * ranks + 3,)),
        pltpu.SemaphoreType.DMA((1 + 2 * blocks,)),
    ]
    outs = [bf16_like(2 * units, D), bf16_like(D, units)]
    kernel = functools.partial(gradient_kernel, units, ranks)
    return hbm_call(kernel, [*na, *oc, *kept], outs, scratch, 6 * tokens * D * units)


def sharded_pass(tokens, cotangent, lengths, half_qkv, half_out, half_in, half_down, half_small):
    ranks = lax.axis_size("dp")
    lines = lax.axis_size("fsdp")
    place = lax.axis_index("dp")
    rows = tokens.shape[1]
    slices = lines // 2
    block = D // ranks
    inputs = tokens[0]
    info = jnp.stack([place, lax.rem(lax.axis_index("fsdp"), 2), lengths[0]])

    small_rows, small_columns = half_small.shape
    small_size = small_rows * small_columns
    columns = half_qkv.shape[1]
    small_part = jnp.pad(half_small.reshape(1, small_size), ((0, 15), (0, block - small_size)))
    qkv_along = gather_line(jnp.concatenate([half_qkv.T, small_part]))
    exchange = exchange_weights(half_in, half_down)
    sent = next(exchange)
    sent, qkv_along = lax.optimization_barrier((sent, qkv_along))
    got = dp_exchange(sent)
    qkv_own, qkv_other = gather_rest(qkv_along)
    half_out, qkv_own[1] = lax.optimization_barrier((half_out, qkv_own[1]))
    out_along = gather_line(half_out.T)
    out_along, qkv_own[ranks - 1] = lax.optimization_barrier((out_along, qkv_own[ranks - 1]))
    out_own, out_other = gather_rest(out_along)

    small_pairs = []
    for mine, theirs in zip(qkv_own, qkv_other):
        mine, theirs = (
            part.reshape(slices, columns + 16, block)[:, columns, :small_size]
            for part in (mine, theirs)
        )
        even = jnp.where(is_even(), mine, theirs)
        odd = jnp.where(is_even(), theirs, mine)
        small_pairs.append(jnp.stack([even, odd], axis=1))
    small_stack = jnp.stack(small_pairs)
    small_vec = jnp.stack(
        [
            lax.dynamic_index_in_dim(small_stack, place ^ a, 0, keepdims=False)
            for a in range(ranks)
        ]
    )
    small_vec = small_vec.reshape(ranks, lines, small_rows, small_columns)
    small_vec = small_vec.transpose(0, 2, 1, 3).reshape(-1).astype(jnp.float32)
    gain_attn, gain_mlp, biases = unpack_small(small_vec)
    gain_attn = gain_attn[None]
    gain_mlp = gain_mlp[None]

    in_piece, down_piece = exchange.send(got)
    in_chunks = []
    down_chunks = []
    start = 0
    for size in CHUNKS:
        width = size // slices
        down_chunks.append(
            lax.all_gather(
                down_piece[:, :, start : start + width].reshape(-1, size),
                "fsdp",
                axis=0,
                tiled=True,
            )
        )
        in_chunks.append(
            lax.all_gather(in_piece[start : start + width], "fsdp", axis=0, tiled=True)
        )
        start += width

    query_places = place * rows + jnp.arange(rows, dtype=jnp.int32)
    cosine, sine = rope_tables(query_places.astype(jnp.float32))
    sine = jnp.where(jnp.arange(HEAD) < HEAD // 2, -sine, sine)
    normed, queries, kv = call(
        functools.partial(project_kernel, ranks, slices),
        [info, inputs, gain_attn, biases[None], cosine, sine, *qkv_own, *qkv_other],
        [bf16_like(rows, D), bf16_like(rows, D), bf16_like(rows, 2 * KV_WIDTH)],
        [vmem_f32(rows, QKV)],
        2 * rows * D * QKV,
    )
    kv_blocks = dp_gather(kv)

    valid = query_places < lengths[0]
    out_cot = jnp.where(valid[:, None], cotangent[0], jnp.zeros_like(cotangent[0]))
    out_cot, *kv_blocks = lax.optimization_barrier((out_cot, *kv_blocks))
    cot_blocks = dp_gather(out_cot)

    attended, totals, middle, normed_again = call(
        functools.partial(attend_kernel, ranks, slices),
        [info, inputs, gain_mlp, queries, *kv_blocks, *out_own, *out_other],
        [bf16_like(rows, D), f32_like(16, rows), f32_like(rows, D), bf16_like(rows, D)],
        [
            vmem_f32(ranks * rows, rows),
            vmem_bf16(ranks * rows, KV_WIDTH),
            vmem_bf16(ranks * rows, KV_WIDTH),
            vmem_bf16(KV_WIDTH, ranks * rows),
        ],
        2 * rows * D * D + 4 * rows * D * ranks * rows,
    )
    normed_blocks = dp_gather(normed_again)

    carry = ()
    in_terms = []
    down_terms = []
    for index, size in enumerate(CHUNKS):
        in_mat = in_chunks[index]
        down_mat = down_chunks[index]
        if index < len(CHUNKS) - 1:
            back, mixed, in_term, down_term = first_chunk(
                normed_blocks, cot_blocks, in_mat, down_mat
            )
            carry = (back, mixed)
        else:
            back_blocks, mixed_blocks, kept = last_chunk(
                normed_blocks, cot_blocks, in_mat, down_mat, carry
            )
            back_got = [dp_send(back_blocks[k], k) for k in range(1, ranks)]
            in_term, down_term = chunk_gradients(normed_blocks, cot_blocks, kept)
        in_terms.append(in_term)
        down_terms.append(down_term)
    in_terms[-1], down_terms[-1], back_blocks, back_got, mixed_blocks = lax.optimization_barrier(
        (in_terms[-1], down_terms[-1], back_blocks, back_got, mixed_blocks)
    )
    mixed = middle + mixed_blocks[0].astype(jnp.float32)
    for k in range(1, ranks):
        mixed = mixed + dp_send(mixed_blocks[k], k).astype(jnp.float32)
    in_parts = []
    down_parts = []
    for in_term, down_term, size in zip(in_terms, down_terms, CHUNKS):
        down_sum = lax.psum_scatter(down_term, "fsdp", scatter_dimension=0, tiled=True)
        in_sum = lax.psum_scatter(in_term, "fsdp", scatter_dimension=0, tiled=True)
        down_sum = down_sum.reshape(-1, slices, size // slices)
        in_part, down_part = exchange_gradients(in_sum, down_sum, half_down.shape[1])
        in_parts.append(in_part)
        down_parts.append(down_part)
    in_grad = jnp.concatenate(in_parts, axis=1)
    in_grad = in_grad.transpose(2, 0, 1).reshape(half_in.shape).astype(jnp.float32)
    down_grad = jnp.concatenate(down_parts, axis=1)
    down_grad = down_grad.transpose(2, 0, 1, 3).reshape(half_down.shape).astype(jnp.float32)

    middle_cot, middle_low, gain_mlp_grad, query_cot, *kv_cot = call(
        functools.partial(attend_back_kernel, ranks, slices),
        [
            info,
            middle,
            out_cot,
            gain_mlp,
            queries,
            totals,
            back_blocks[0],
            *back_got,
            *kv_blocks,
            *out_own,
            *out_other,
        ],
        [f32_like(rows, D), bf16_like(rows, D), f32_like(1, D), f32_like(rows, D)]
        + [bf16_like(rows, 2 * KV_WIDTH)] * ranks,
        [
            vmem_f32(ranks * rows, rows),
            vmem_bf16(ranks * rows, KV_WIDTH),
            vmem_bf16(ranks * rows, KV_WIDTH),
            vmem_bf16(KV_WIDTH, ranks * rows),
            vmem_bf16(rows, D),
            vmem_f32(ranks * rows, KV_WIDTH),
            vmem_f32(ranks * rows, KV_WIDTH),
            vmem_bf16(rows, D // 2),
            vmem_bf16(rows, D // 2),
        ],
        2 * rows * D * D + 10 * rows * D * ranks * rows,
    )
    kv_got = [dp_send(kv_cot[k], k) for k in range(1, ranks)]

    def outer(left, right):
        columns = right.shape[1]
        terms = call(
            functools.partial(outer_kernel, ranks, slices),
            [info, left, right],
            [bf16_like(columns // 2, block)] * (2 * ranks),
            [vmem_bf16(columns, rows)],
            2 * rows * D * columns,
        )
        return reduce_matrix(terms[:ranks], terms[ranks:])

    out_grad = outer(attended, middle_low)
    projected_low, bias_grad = call(
        functools.partial(project_back_kernel, ranks),
        [info, query_cot, cosine, sine, kv_cot[0], *kv_got],
        [bf16_like(rows, QKV), f32_like(1, QKV)],
        [],
        0,
    )
    qkv_grad = outer(normed, projected_low)
    input_grad, gain_attn_grad = call(
        functools.partial(input_back_kernel, ranks, slices),
        [info, projected_low, inputs, gain_attn, middle_cot, *qkv_own, *qkv_other],
        [bf16_like(rows, D), f32_like(1, D)],
        [vmem_bf16(rows, QKV // 2), vmem_bf16(rows, QKV // 2), vmem_f32(rows, D)],
        2 * rows * D * QKV,
    )
    small_term = group_small(gain_attn_grad[0], gain_mlp_grad[0], bias_grad[0])
    small_sum = sum_everywhere(small_term)
    small_grad = lax.dynamic_slice(
        small_sum,
        (place * small_rows, lax.axis_index("fsdp") * small_columns),
        (small_rows, small_columns),
    )
    return (bf16(mixed), input_grad, qkv_grad, out_grad, in_grad, down_grad, small_sum, small_grad)


def per_device(
    tokens,
    cotangent,
    lengths,
    qkv_weight,
    qkv_first,
    qkv_second,
    out_weight,
    out_first,
    out_second,
    mlp_in_weight,
    mlp_in_first,
    mlp_in_second,
    down_weight,
    down_first,
    down_second,
    small_params,
    small_first,
    small_second,
):
    results = sharded_pass(
        tokens,
        cotangent,
        lengths,
        bf16(qkv_weight),
        bf16(out_weight),
        bf16(mlp_in_weight),
        bf16(down_weight),
        bf16(small_params),
    )
    mixed, input_cot, qkv_grad, out_grad, in_grad, down_grad, small_sum, small_grad = results
    local_squares = sum(
        (jnp.sum(piece * piece) for piece in (qkv_grad, out_grad, in_grad, down_grad))
    )
    total_squares = sum_everywhere(local_squares) + jnp.sum(small_sum * small_sum)
    grad_norm = jnp.sqrt(total_squares)
    clip_factor = CLIP_NORM / jnp.maximum(grad_norm, CLIP_NORM)
    outs = [mixed[None], input_cot[None], grad_norm]
    for weight, first, second, gradient, rate, decay in (
        (qkv_weight, qkv_first, qkv_second, qkv_grad, MATRIX_RATE, MATRIX_DECAY),
        (out_weight, out_first, out_second, out_grad, MATRIX_RATE, MATRIX_DECAY),
        (mlp_in_weight, mlp_in_first, mlp_in_second, in_grad, MATRIX_RATE, MATRIX_DECAY),
        (down_weight, down_first, down_second, down_grad, MATRIX_RATE, MATRIX_DECAY),
        (small_params, small_first, small_second, small_grad, SMALL_RATE, 0.0),
    ):
        outs.extend(update(weight, first, second, gradient, clip_factor, rate, decay))
    return tuple(outs)


def solution(mesh):
    rows = P("fsdp", "dp", None)
    shard = P("dp", "fsdp")
    return jax.shard_map(
        per_device,
        mesh=mesh,
        in_specs=(rows, rows, P("fsdp")) + (shard,) * 15,
        out_specs=(rows, rows, P()) + (shard,) * 20,
        check_vma=False,
    )
```

time: 1020 us -> 755 us (0.74)
  matrix products: 270 us -> 0 us
  Pallas kernels: 0 us -> 215 us
  blocking collectives: 166 us -> 0 us
  local copies, waits for them, and re-layouts: 121 us -> 37.2 us
  other arithmetic: 114 us -> 56.9 us
  waiting for transfers between devices: 259 us -> 314 us
  starting transfers between devices: 57.3 us -> 101 us
    dot_general x72 -> x0, matrix products: 270 us -> none  [the longest x22 81.8 us: dot_nn(): return jnp.dot(left, right, preferred_element_type=jnp.float32)]
    pallas_call x0 -> x10, Pallas kernels: none -> 215 us  [the longest x3 124 us: hbm_call(): pl.pallas_call(kernel, out_shape=tuple(outs), in_specs=[anywhere] * len(a...]
    all_gather x3 -> x0, blocking collectives: 87.9 us -> none  [the longest x2 48.5 us: gather_matrix(): lax.all_gather(piece, 'fsdp', axis=0, tiled=True, axis_index_groups=parit...]
    psum x2 -> x0, blocking collectives: 78.3 us -> none  [the longest x1 40 us: per_device(): total_squares = lax.psum(local_squares, ('dp', 'fsdp'))]
    ppermute x42 -> x45, waiting for transfers between devices: 220 us -> 286 us  [dp_send(): return lax.ppermute(block, 'dp', [(i, i ^ k) for i in range(count)])]
    ppermute x0 -> x18, starting transfers between devices: none -> 44.5 us  [line_send(): return lax.ppermute(block, 'fsdp', [(i, i ^ 2 * r) for i in range(count)])]
    reduce_scatter x8 -> x4, waiting for transfers between devices: 38.9 us -> 0.06 us  [the longest x2 0.04 us: sharded_pass(): in_sum = lax.psum_scatter(in_term, 'fsdp', scatter_dimension=0, tiled=True)]
    ppermute x0 -> x18, waiting for transfers between devices: none -> 23.8 us  [line_send(): return lax.ppermute(block, 'fsdp', [(i, i ^ 2 * r) for i in range(count)])]
  transfers between devices with their start and end apart: 72 -> 89, of which waited for: 21 -> 37; matrix products, arithmetic and copies ran while one was open for 40% -> 6% of each run, Pallas kernels for 0% -> 29%
where the time goes in v2:
time: 755 us; the launch traced here: 749 us
  waiting for transfers between devices  314 us (42%)
  Pallas kernels  215 us (28%)
  starting transfers between devices  101 us (13%)
  other arithmetic  56.9 us (8%)
  local copies, waits for them, and re-layouts  37.2 us (5%)
  between operations  24.8 us (3%)
    ppermute x45, waiting for transfers between devices, dp_send(): return lax.ppermute(block, 'dp', [(i, i ^ k) for i in range(count)])  286 us
    pallas_call x3, Pallas kernels, hbm_call(): pl.pallas_call(kernel, out_shape=tuple(outs), in_specs=[anywhere] * len(a...  124 us
    pallas_call x7, Pallas kernels, call(): pl.pallas_call(kernel, out_shape=tuple(outs), in_specs=[pl.BlockSpec(memo...  91.8 us
    ppermute x45, starting transfers between devices, dp_send(): return lax.ppermute(block, 'dp', [(i, i ^ k) for i in range(count)])  52.7 us
    ppermute x18, starting transfers between devices, line_send(): return lax.ppermute(block, 'fsdp', [(i, i ^ 2 * r) for i in range(count)])  44.5 us
    ppermute x18, waiting for transfers between devices, line_send(): return lax.ppermute(block, 'fsdp', [(i, i ^ 2 * r) for i in range(count)])  23.8 us
    convert_element_type x5, other arithmetic, update(): return (weight_new, first_new, second_new, weight_new.astype(jnp.bfloat16))  16.6 us
  transfers between devices with their start and end apart: 89, of which 37 were waited for; matrix products, arithmetic and copies ran while one was open for 6% of the time, Pallas kernels for 29%

profile of v2, /device:TPU:0, one launch (start us, length us, event | category | flops | bytes accessed | tf_op | source)
XLA Modules:
  0.0 749.2 jit_solution(5211849537677866864)
XLA Ops:
  44.3 16.4 %collective-permute-done.31 = bf16[560,576]{1,0:T(8,128)(2,1)S(1)} collective-permute-done((bf16[560,576]{1,0:T(8,128)(2,1)S(1)}, bf16[560,576]{1,0:T(8,128)(2,1)S(1)}, u32[]{:S(2)}, u32[]{:S(2)}) %collective-permute-start.31) | collective-permute-done | bytes 645152 | tf_op jit(solution)/shard_map/ppermute | solution.py:110
  60.7 13.2 %collective-permute-done.30 = bf16[560,576]{1,0:T(8,128)(2,1)S(1)} collective-permute-done((bf16[560,576]{1,0:T(8,128)(2,1)S(1)}, bf16[560,576]{1,0:T(8,128)(2,1)S(1)}, u32[]{:S(2)}, u32[]{:S(2)}) %collective-permute-start.30) | collective-permute-done | bytes 645152 | tf_op jit(solution)/shard_map/ppermute | solution.py:110
  87.0 16.8 %collective-permute-done.4.refs_7_.refs_6_ = bf16[1088,384]{1,0:T(8,128)(2,1)S(1)} collective-permute-done((bf16[1088,384]{1,0:T(8,128)(2,1)S(1)}, bf16[1088,384]{1,0:T(8,128)(2,1)S(1)}, u32[]{:S(2)}, u32[]{:S(2)}) %collective-permute-start.4) | collective-permute-done | bytes 835616 | tf_op jit(solution)/shard_map/ppermute | solution.py:110
  103.9 8.8 %collective-permute-start.9 = (bf16[192,384]{1,0:T(8,128)(2,1)S(1)}, bf16[192,384]{1,0:T(8,128)(2,1)}, u32[]{:S(2)}, u32[]{:S(2)}) collective-permute-start(bf16[192,384]{1,0:T(8,128)(2,1)S(1)} %bitcast.201), channel_id=1, source_target_pairs={{0,4},{1,5},{2,6},{3,7},{4,0},{5,1},{6,2},{7,3},{8,12},{9,13},{10,... | collective-permute-start | bytes 442376 | tf_op jit(solution)/shard_map/ppermute | solution.py:137
  112.7 9.1 %collective-permute-done.11.refs_9_.refs_8_ = bf16[1088,384]{1,0:T(8,128)(2,1)S(1)} collective-permute-done((bf16[1088,384]{1,0:T(8,128)(2,1)S(1)}, bf16[1088,384]{1,0:T(8,128)(2,1)S(1)}, u32[]{:S(2)}, u32[]{:S(2)}) %collective-permute-start.11) | collective-permute-done | bytes 835616 | tf_op jit(solution)/shard_map/ppermute | solution.py:110
  137.2 8.8 %collective-permute-done.10 = bf16[192,384]{1,0:T(8,128)(2,1)S(1)} collective-permute-done((bf16[192,384]{1,0:T(8,128)(2,1)S(1)}, bf16[192,384]{1,0:T(8,128)(2,1)S(1)}, u32[]{:S(2)}, u32[]{:S(2)}) %collective-permute-start.10) | collective-permute-done | bytes 147488 | tf_op jit(solution)/shard_map/ppermute | solution.py:137
  171.8 29.9 %collective-permute-done.14.refs_6_.refs_12_ = bf16[320,512]{1,0:T(8,128)(2,1)S(1)} collective-permute-done((bf16[320,512]{1,0:T(8,128)(2,1)}, bf16[320,512]{1,0:T(8,128)(2,1)S(1)}, u32[]{:S(2)}, u32[]{:S(2)}) %collective-permute-start.14) | collective-permute-done | bytes 327712 | tf_op jit(solution)/shard_map/ppermute | solution.py:110
  208.8 24.1 %shard_map.354 = (bf16[320,1536]{1,0:T(8,128)(2,1)}, f32[16,320]{1,0:T(8,128)}, f32[320,1536]{1,0:T(8,128)}, bf16[320,1536]{1,0:T(8,128)(2,1)}) custom-call(s32[3]{0:T(128)} %pad_add_fusion.refs_0_, bf16[320,1536]{1,0:T(8,128)(2,1)} %bitcast.182, f32[1,1536]{1,0:T(1,128)} %broadcast_in_dim_reshape.6.refs_2_.refs_3_, ...), custom_call_target="tpu_custom_call" | custom-call | flops 4026531840 | bytes 11954188 | tf_op jit(solution)/shard_map/pallas_call | solution.py:460
  236.5 12.6 %collective-permute-done.27.refs_6_ = bf16[320,1536]{1,0:T(8,128)(2,1)S(1)} collective-permute-done((bf16[320,1536]{1,0:T(8,128)(2,1)S(1)}, bf16[320,1536]{1,0:T(8,128)(2,1)S(1)}, u32[]{:S(2)}, u32[]{:S(2)}) %collective-permute-start.27) | collective-permute-done | bytes 983072 | tf_op jit(solution)/shard_map/ppermute | solution.py:110
  250.0 20.1 %collective-permute-done.25.refs_3_ = bf16[320,1536]{1,0:T(8,128)(2,1)S(1)} collective-permute-done((bf16[320,1536]{1,0:T(8,128)(2,1)}, bf16[320,1536]{1,0:T(8,128)(2,1)S(1)}, u32[]{:S(2)}, u32[]{:S(2)}) %collective-permute-start.25) | collective-permute-done | bytes 983072 | tf_op jit(solution)/shard_map/ppermute | solution.py:110
  271.0 19.1 %collective-permute-done.24.refs_2_ = bf16[320,1536]{1,0:T(8,128)(2,1)S(1)} collective-permute-done((bf16[320,1536]{1,0:T(8,128)(2,1)}, bf16[320,1536]{1,0:T(8,128)(2,1)S(1)}, u32[]{:S(2)}, u32[]{:S(2)}) %collective-permute-start.24) | collective-permute-done | bytes 983072 | tf_op jit(solution)/shard_map/ppermute | solution.py:110
  291.1 49.0 %shard_map.355 = (f32[1280,1536]{1,0:T(8,128)}, f32[1280,1536]{1,0:T(8,128)}, bf16[2048,1536]{1,0:T(8,128)(2,1)}, bf16[1536,1024]{1,0:T(8,128)(2,1)}) custom-call(bf16[320,1536]{1,0:T(8,128)(2,1)} %get-tuple-element.108.refs_0_, bf16[320,1536]{1,0:T(8,128)(2,1)} %collective-permute-done.23.refs_1_, bf16[320,1536]{1,0:T(8,128)(2,1)} %copy-done.46, ...), custom_call_target="tpu_custom_call" | custom-call | flops 36238786560 | bytes 42467328 | tf_op jit(solution)/shard_map/pallas_call | solution.py:687
  340.8 49.9 %shard_map.356 = (bf16[320,1536]{1,0:T(8,128)(2,1)}, bf16[320,1536]{1,0:T(8,128)(2,1)}, bf16[320,1536]{1,0:T(8,128)(2,1)}, bf16[320,1536]{1,0:T(8,128)(2,1)}, bf...) custom-call(bf16[320,1536]{1,0:T(8,128)(2,1)} %get-tuple-element.108, ...), custom_call_target="tpu_custom_call" | custom-call | flops 28689039360 | bytes 52002816 | tf_op jit(solution)/shard_map/pallas_call | solution.py:687
  394.3 24.7 %shard_map.357 = (bf16[2432,1536]{1,0:T(8,128)(2,1)}, bf16[1536,1216]{1,0:T(8,128)(2,1)}) custom-call(bf16[320,1536]{1,0:T(8,128)(2,1)} %get-tuple-element.108.refs_0_, bf16[320,1536]{1,0:T(8,128)(2,1)} %collective-permute-done.23.refs_1_, bf16[320,1536]{1,0:T(8,128)(2,1)} %copy-done.46, bf16[320,1536]{1,0:T(8,128)(2,1)} %copy-done.45, ...), custom_call_target="tpu_custom_call" | custom-call | flops 14344519680 | bytes 28409856 | tf_op jit(solution)/shard_map/pallas_call | solution.py:687
  419.0 17.1 %collective-permute-done.33.refs_8_ = bf16[320,1536]{1,0:T(8,128)(2,1)S(1)} collective-permute-done((bf16[320,1536]{1,0:T(8,128)(2,1)}, bf16[320,1536]{1,0:T(8,128)(2,1)S(1)}, u32[]{:S(2)}, u32[]{:S(2)}) %collective-permute-start.33) | collective-permute-done | bytes 983072 | tf_op jit(solution)/shard_map/ppermute | solution.py:110
  438.1 31.5 %shard_map.358 = (f32[320,1536]{1,0:T(8,128)}, bf16[320,1536]{1,0:T(8,128)(2,1)}, f32[1,1536]{1,0:T(1,128)}, f32[320,1536]{1,0:T(8,128)}, bf16[320,512]{1,0:T(8,...) custom-call(s32[3]{0:T(128)} %pad_add_fusion.refs_0_, ...), custom_call_target="tpu_custom_call" | custom-call | flops 7801405440 | bytes 20152332 | tf_op jit(solution)/shard_map/pallas_call | solution.py:460
  491.9 8.9 %shard_map.360 = (bf16[320,1536]{1,0:T(8,128)(2,1)}, f32[1,1536]{1,0:T(1,128)}) custom-call(s32[3]{0:T(128)} %pad_add_fusion.refs_0_, bf16[320,2048]{1,0:T(8,128)(2,1)} %get-tuple-element.140.refs_1_.refs_2_, bf16[320,1536]{1,0:T(8,128)(2,1)} %bitcast.183, f32[1,1536]{1,0:T(1,128)} %broadcast_in_dim_reshape.7.refs_2_.refs_3_, ...), custom_call_target="tpu_custom_call" | custom-call | flops 2013265920 | bytes 11939852 | tf_op jit(solution)/shard_map/pallas_call | solution.py:460
  516.7 8.6 %shard_map.361 = (bf16[1024,384]{1,0:T(8,128)(2,1)}, bf16[1024,384]{1,0:T(8,128)(2,1)}, bf16[1024,384]{1,0:T(8,128)(2,1)}, bf16[1024,384]{1,0:T(8,128)(2,1)}, bf...) custom-call(s32[3]{0:T(128)} %pad_add_fusion.refs_0_, ...), custom_call_target="tpu_custom_call" | custom-call | flops 2013265920 | bytes 8585228 | tf_op jit(solution)/shard_map/pallas_call | solution.py:460
  539.6 17.7 %collective-permute-done.35 = bf16[320,1536]{1,0:T(8,128)(2,1)S(1)} collective-permute-done((bf16[320,1536]{1,0:T(8,128)(2,1)}, bf16[320,1536]{1,0:T(8,128)(2,1)S(1)}, u32[]{:S(2)}, u32[]{:S(2)}) %collective-permute-start.35) | collective-permute-done | bytes 983072 | tf_op jit(solution)/shard_map/ppermute | solution.py:110
  557.3 22.2 %collective-permute-done.36 = bf16[320,1536]{1,0:T(8,128)(2,1)S(1)} collective-permute-done((bf16[320,1536]{1,0:T(8,128)(2,1)S(1)}, bf16[320,1536]{1,0:T(8,128)(2,1)S(1)}, u32[]{:S(2)}, u32[]{:S(2)}) %collective-permute-start.36) | collective-permute-done | bytes 983072 | tf_op jit(solution)/shard_map/ppermute | solution.py:110
  581.4 9.6 %collective-permute-done.53 = bf16[768,384]{1,0:T(8,128)(2,1)S(1)} collective-permute-done((bf16[768,384]{1,0:T(8,128)(2,1)S(1)}, bf16[768,384]{1,0:T(8,128)(2,1)S(1)}, u32[]{:S(2)}, u32[]{:S(2)}) %collective-permute-start.53) | collective-permute-done | bytes 589856 | tf_op jit(solution)/shard_map/ppermute | solution.py:110
  592.0 12.3 %collective-permute-done.55 = bf16[768,384]{1,0:T(8,128)(2,1)S(1)} collective-permute-done((bf16[768,384]{1,0:T(8,128)(2,1)S(1)}, bf16[768,384]{1,0:T(8,128)(2,1)S(1)}, u32[]{:S(2)}, u32[]{:S(2)}) %collective-permute-start.55) | collective-permute-done | bytes 589856 | tf_op jit(solution)/shard_map/ppermute | solution.py:110
  609.7 10.9 %collective-permute-done.43 = bf16[1024,384]{1,0:T(8,128)(2,1)S(1)} collective-permute-done((bf16[1024,384]{1,0:T(8,128)(2,1)S(1)}, bf16[1024,384]{1,0:T(8,128)(2,1)S(1)}, u32[]{:S(2)}, u32[]{:S(2)}) %collective-permute-start.43) | collective-permute-done | bytes 786464 | tf_op jit(solution)/shard_map/ppermute | solution.py:110
  620.7 17.0 %collective-permute-done.45 = bf16[1024,384]{1,0:T(8,128)(2,1)S(1)} collective-permute-done((bf16[1024,384]{1,0:T(8,128)(2,1)S(1)}, bf16[1024,384]{1,0:T(8,128)(2,1)S(1)}, u32[]{:S(2)}, u32[]{:S(2)}) %collective-permute-start.45) | collective-permute-done | bytes 786464 | tf_op jit(solution)/shard_map/ppermute | solution.py:110
  (396 shorter events, 265.9 us)
Async XLA Ops:
  7.2 283.9 %all-gather.11.cloned.1.call-start = ((), (), s32[]{:S(2)}) async-start(), calls=%async_computation.7 | async-start | bytes 3538944 | tf_op jit(solution)/shard_map/all_gather | solution.py:838
  77.3 213.8 %all-gather.9.cloned.1.call-start = ((), (), s32[]{:S(2)}) async-start(), calls=%async_computation.6 | async-start | bytes 7077888 | tf_op jit(solution)/shard_map/all_gather | solution.py:846
  79.2 261.6 %all-gather.7.cloned.1.call-start = ((), (), s32[]{:S(2)}) async-start(), calls=%async_computation.5 | async-start | bytes 4423680 | tf_op jit(solution)/shard_map/all_gather | solution.py:838
  80.5 260.3 %all-gather.5.cloned.1.call-start = ((), (), s32[]{:S(2)}) async-start(), calls=%async_computation.4 | async-start | bytes 8404992 | tf_op jit(solution)/shard_map/all_gather | solution.py:846
  81.7 565.9 %reduce-scatter.7.cloned.1.call-start = ((), (), s32[]{:S(2)}) async-start(), calls=%async_computation.9 | async-start | bytes 3538944 | tf_op jit(solution)/shard_map/reduce_scatter | solution.py:909
  85.9 46.8 %collective-permute-start.3 = (bf16[1088,384]{1,0:T(8,128)(2,1)S(1)}, bf16[1088,384]{1,0:T(8,128)(2,1)}, u32[]{:S(2)}, u32[]{:S(2)}) collective-permute-start(bf16[1088,384]{1,0:T(8,128)(2,1)S(1)} %bitcast.175), channel_id=1, source_target_pairs={{0,1},{1,0},{2,3},{3,2},{4,5},{5,4},{6,7},{7,6},{8,9},{9,8},{10,11... | collective-permute-start | bytes 2506760 | tf_op jit(solution)/shard_map/ppermute | solution.py:115
  160.2 42.7 %collective-permute-start.18 = (bf16[768,384]{1,0:T(8,128)(2,1)S(1)}, bf16[768,384]{1,0:T(8,128)(2,1)}, u32[]{:S(2)}, u32[]{:S(2)}) collective-permute-start(bf16[768,384]{1,0:T(8,128)(2,1)S(1)} %bitcast.207), channel_id=1, source_target_pairs={{0,24},{8,16},{16,8},{24,0},{1,25},{9,17},{17,9},{25,1},{2,26},{10... | collective-permute-start | bytes 1769480 | tf_op jit(solution)/shard_map/ppermute | solution.py:110
  162.7 40.8 %collective-permute-start.17 = (bf16[768,384]{1,0:T(8,128)(2,1)S(1)}, bf16[768,384]{1,0:T(8,128)(2,1)}, u32[]{:S(2)}, u32[]{:S(2)}) collective-permute-start(bf16[768,384]{1,0:T(8,128)(2,1)S(1)} %bitcast.208), channel_id=1, source_target_pairs={{0,16},{8,24},{16,0},{24,8},{1,17},{9,25},{17,1},{25,9},{2,18},{10... | collective-permute-start | bytes 1769480 | tf_op jit(solution)/shard_map/ppermute | solution.py:110
  162.7 40.8 %collective-permute-start.16 = (bf16[768,384]{1,0:T(8,128)(2,1)S(1)}, bf16[768,384]{1,0:T(8,128)(2,1)}, u32[]{:S(2)}, u32[]{:S(2)}) collective-permute-start(bf16[768,384]{1,0:T(8,128)(2,1)S(1)} %bitcast.209), channel_id=1, source_target_pairs={{0,8},{8,0},{16,24},{24,16},{1,9},{9,1},{17,25},{25,17},{2,10},{10... | collective-permute-start | bytes 1769480 | tf_op jit(solution)/shard_map/ppermute | solution.py:110
  205.8 43.2 %collective-permute-start.27 = (bf16[320,1536]{1,0:T(8,128)(2,1)S(1)}, bf16[320,1536]{1,0:T(8,128)(2,1)S(1)}, u32[]{:S(2)}, u32[]{:S(2)}) collective-permute-start(bf16[320,1536]{1,0:T(8,128)(2,1)S(1)} %bitcast_select_fusion.refs_4_.refs_2_), channel_id=1, source_target_pairs={{0,16},{8,24},{16,0},{24,8},{1,17},{9,25},{17,1},{25,9},{2,18},{10... | collective-permute-start | bytes 2949128 | tf_op jit(solution)/shard_map/ppermute | solution.py:110
  206.2 42.9 %collective-permute-start.26 = (bf16[320,1536]{1,0:T(8,128)(2,1)S(1)}, bf16[320,1536]{1,0:T(8,128)(2,1)}, u32[]{:S(2)}, u32[]{:S(2)}) collective-permute-start(bf16[320,1536]{1,0:T(8,128)(2,1)S(1)} %bitcast_select_fusion.refs_4_.refs_2_), channel_id=1, source_target_pairs={{0,8},{8,0},{16,24},{24,16},{1,9},{9,1},{17,25},{25,17},{2,10},{10... | collective-permute-start | bytes 2949128 | tf_op jit(solution)/shard_map/ppermute | solution.py:110
  235.0 55.1 %collective-permute-start.24 = (bf16[320,1536]{1,0:T(8,128)(2,1)}, bf16[320,1536]{1,0:T(8,128)(2,1)S(1)}, u32[]{:S(2)}, u32[]{:S(2)}) collective-permute-start(bf16[320,1536]{1,0:T(8,128)(2,1)} %get-tuple-element.108.refs_0_), channel_id=1, source_target_pairs={{0,16},{8,24},{16,0},{24,8},{1,17},{9,25},{17,1},{25,9},{2,18},{10... | collective-permute-start | bytes 2949128 | tf_op jit(solution)/shard_map/ppermute | solution.py:110
  235.0 56.0 %collective-permute-start.23 = (bf16[320,1536]{1,0:T(8,128)(2,1)}, bf16[320,1536]{1,0:T(8,128)(2,1)}, u32[]{:S(2)}, u32[]{:S(2)}) collective-permute-start(bf16[320,1536]{1,0:T(8,128)(2,1)} %get-tuple-element.108.refs_0_), channel_id=1, source_target_pairs={{0,8},{8,0},{16,24},{24,16},{1,9},{9,1},{17,25},{25,17},{2,10},{10... | collective-permute-start | bytes 2949128 | tf_op jit(solution)/shard_map/ppermute | solution.py:110
  340.2 308.8 %reduce-scatter.5.cloned.1.call-start = ((), (), s32[]{:S(2)}) async-start(), calls=%async_computation.8 | async-start | bytes 7077888 | tf_op jit(solution)/shard_map/reduce_scatter | solution.py:910
  340.7 321.2 %reduce-scatter.11.cloned.1.call-start = ((), (), s32[]{:S(2)}) async-start(), calls=%async_computation.11 | async-start | bytes 4423680 | tf_op jit(solution)/shard_map/reduce_scatter | solution.py:909
  390.8 45.2 %collective-permute-start.33 = (bf16[320,1536]{1,0:T(8,128)(2,1)}, bf16[320,1536]{1,0:T(8,128)(2,1)S(1)}, u32[]{:S(2)}, u32[]{:S(2)}) collective-permute-start(bf16[320,1536]{1,0:T(8,128)(2,1)} %get-tuple-element.120), channel_id=1, source_target_pairs={{0,16},{8,24},{16,0},{24,8},{1,17},{9,25},{17,1},{25,9},{2,18},{10... | collective-permute-start | bytes 2949128 | tf_op jit(solution)/shard_map/ppermute | solution.py:110
  392.0 44.1 %collective-permute-start.34 = (bf16[320,1536]{1,0:T(8,128)(2,1)}, bf16[320,1536]{1,0:T(8,128)(2,1)S(1)}, u32[]{:S(2)}, u32[]{:S(2)}) collective-permute-start(bf16[320,1536]{1,0:T(8,128)(2,1)} %get-tuple-element.121), channel_id=1, source_target_pairs={{0,24},{8,16},{16,8},{24,0},{1,25},{9,17},{17,9},{25,1},{2,26},{10... | collective-permute-start | bytes 2949128 | tf_op jit(solution)/shard_map/ppermute | solution.py:110
  437.3 229.2 %reduce-scatter.9.cloned.1.call-start = ((), (), s32[]{:S(2)}) async-start(), calls=%async_computation.10 | async-start | bytes 8404992 | tf_op jit(solution)/shard_map/reduce_scatter | solution.py:910
  533.9 45.7 %collective-permute-start.36 = (bf16[320,1536]{1,0:T(8,128)(2,1)S(1)}, bf16[320,1536]{1,0:T(8,128)(2,1)S(1)}, u32[]{:S(2)}, u32[]{:S(2)}) collective-permute-start(bf16[320,1536]{1,0:T(8,128)(2,1)S(1)} %copy-done.42), channel_id=1, source_target_pairs={{0,16},{8,24},{16,0},{24,8},{1,17},{9,25},{17,1},{25,9},{2,18},{10... | collective-permute-start | bytes 2949128 | tf_op jit(solution)/shard_map/ppermute | solution.py:110
  534.3 46.2 %collective-permute-start.37 = (bf16[320,1536]{1,0:T(8,128)(2,1)S(1)}, bf16[320,1536]{1,0:T(8,128)(2,1)S(1)}, u32[]{:S(2)}, u32[]{:S(2)}) collective-permute-start(bf16[320,1536]{1,0:T(8,128)(2,1)S(1)} %copy-done.41), channel_id=1, source_target_pairs={{0,24},{8,16},{16,8},{24,0},{1,25},{9,17},{17,9},{25,1},{2,26},{10... | collective-permute-start | bytes 2949128 | tf_op jit(solution)/shard_map/ppermute | solution.py:110
  536.3 54.8 %collective-permute-start.53 = (bf16[768,384]{1,0:T(8,128)(2,1)S(1)}, bf16[768,384]{1,0:T(8,128)(2,1)S(1)}, u32[]{:S(2)}, u32[]{:S(2)}) collective-permute-start(bf16[768,384]{1,0:T(8,128)(2,1)S(1)} %add_convert_fusion.6), channel_id=1, source_target_pairs={{0,8},{8,0},{16,24},{24,16},{1,9},{9,1},{17,25},{25,17},{2,10},{10... | collective-permute-start | bytes 1769480 | tf_op jit(solution)/shard_map/ppermute | solution.py:110
  537.6 66.7 %collective-permute-start.55 = (bf16[768,384]{1,0:T(8,128)(2,1)S(1)}, bf16[768,384]{1,0:T(8,128)(2,1)S(1)}, u32[]{:S(2)}, u32[]{:S(2)}) collective-permute-start(bf16[768,384]{1,0:T(8,128)(2,1)S(1)} %add_convert_fusion.5), channel_id=1, source_target_pairs={{0,16},{8,24},{16,0},{24,8},{1,17},{9,25},{17,1},{25,9},{2,18},{10... | collective-permute-start | bytes 1769480 | tf_op jit(solution)/shard_map/ppermute | solution.py:110
  557.3 49.8 %collective-permute-start.41 = (bf16[1024,384]{1,0:T(8,128)(2,1)S(1)}, bf16[1024,384]{1,0:T(8,128)(2,1)S(1)}, u32[]{:S(2)}, u32[]{:S(2)}) collective-permute-start(bf16[1024,384]{1,0:T(8,128)(2,1)S(1)} %copy-done.50), channel_id=1, source_target_pairs={{0,1},{1,0},{2,3},{3,2},{4,5},{5,4},{6,7},{7,6},{8,9},{9,8},{10,11... | collective-permute-start | bytes 2359304 | tf_op jit(solution)/shard_map/ppermute | solution.py:115
  591.1 46.7 %collective-permute-start.45 = (bf16[1024,384]{1,0:T(8,128)(2,1)S(1)}, bf16[1024,384]{1,0:T(8,128)(2,1)S(1)}, u32[]{:S(2)}, u32[]{:S(2)}) collective-permute-start(bf16[1024,384]{1,0:T(8,128)(2,1)S(1)} %add_convert_fusion.2), channel_id=1, source_target_pairs={{0,16},{8,24},{16,0},{24,8},{1,17},{9,25},{17,1},{25,9},{2,18},{10... | collective-permute-start | bytes 2359304 | tf_op jit(solution)/shard_map/ppermute | solution.py:110
  (119 other events, 1765.2 us)
Sparse Core Ops, SparseCore 0:
  77.4 50.2 all-gather.10
  129.9 66.1 all-gather.8
  198.3 42.8 all-gather.6
  243.3 73.2 all-gather.4
  340.3 38.3 reduce-scatter.6
  380.9 68.8 reduce-scatter.4
  452.1 45.8 reduce-scatter.10
  500.3 80.5 reduce-scatter.8

commit v3 on v2

--- a/solution.py
+++ b/solution.py
@@ -31,12 +31,13 @@
 CLIP_NORM = 1.0
 MASKED = -1e30
 SCALE = HEAD ** (-0.5)
-CHUNKS = (1024, 1216)
+CHUNKS = (1536, 704)
 UNIT_TILE = 512
 TOKEN_TILE = 640
 GRAD_TILE = 512
 TURN_TILE = 256
 VMEM_LIMIT = 60 * 2**20
+FLOPS_PER_MICRO = 1_150_000_000
 
 
 def unpack_small(small_vec):
@@ -77,6 +78,11 @@
     return array.astype(jnp.bfloat16)
 
 
+def scoped(name, function, *args):
+    with jax.named_scope(name):
+        return function(*args)
+
+
 def dot_nn(left, right):
     return jnp.dot(left, right, preferred_element_type=jnp.float32)
 
@@ -115,8 +121,18 @@
     return lax.ppermute(block, "fsdp", [(i, i ^ 1) for i in range(count)])
 
 
+def gather_near(block):
+    return [block, dp_send(block, 1), dp_send(block, 2)]
+
+
+def gather_far(near):
+    _, one, two = near
+    half = one.shape[0] // 2
+    return [*near, jnp.concatenate([dp_send(one[:half], 2), dp_send(two[half:], 1)])]
+
+
 def dp_gather(block):
-    return [block] + [dp_send(block, k) for k in range(1, lax.axis_size("dp"))]
+    return gather_far(gather_near(block))
 
 
 def dp_own(array, k):
@@ -146,42 +162,53 @@
     )
 
 
+def sum_of_squares(array):
+    array = array.astype(jnp.float32)
+    return jnp.sum(array * array)
+
+
+def sum_over_core(term):
+    return term + core_swap(term)
+
+
+def sum_over_line(term):
+    return term + sum(line_send(term, r) for r in range(1, lax.axis_size("fsdp") // 2))
+
+
+def sum_over_dp(term):
+    return term + sum(dp_send(term, k) for k in range(1, lax.axis_size("dp")))
+
+
 def sum_everywhere(term):
-    term = term + core_swap(term)
-    lines = [line_send(term, r) for r in range(1, lax.axis_size("fsdp") // 2)]
-    term = term + sum(lines)
-    return term + sum(dp_send(term, k) for k in range(1, lax.axis_size("dp")))
+    return sum_over_dp(sum_over_line(sum_over_core(term)))
 
 
 def is_even():
     return lax.rem(lax.axis_index("fsdp"), 2) == 0
 
 
-def gather_line(piece):
-    return line_gather(piece).reshape(-1, piece.shape[1])
-
-
-def gather_rest(along):
-    own = dp_gather(along)
-    return own, [core_swap(block) for block in own]
-
-
-def reduce_matrix(own_terms, other_terms):
-    summed = [
-        mine.astype(jnp.float32) + core_swap(theirs).astype(jnp.float32)
-        for mine, theirs in zip(own_terms, other_terms)
-    ]
-    total = summed[0]
-    for k in range(1, len(summed)):
-        total = total + dp_send(summed[k].astype(jnp.bfloat16), k).astype(jnp.float32)
+def sum_blocks(own, got):
+    return [own[k].astype(jnp.float32) + got[k].astype(jnp.float32) for k in range(own.shape[0])]
+
+
+def reduce_over_dp(summed):
+    return [summed[0]] + [dp_send(bf16(summed[k]), k) for k in range(1, len(summed))]
+
+
+def reduce_over_line(got):
+    total = sum(block.astype(jnp.float32) for block in got)
     count = lax.axis_size("fsdp") // 2
     place = lax.axis_index("fsdp") // 2
     parts = total.reshape(count, -1, total.shape[1])
-    shard = lax.dynamic_index_in_dim(parts, place, 0, keepdims=False)
+    shard = [lax.dynamic_index_in_dim(parts, place, 0, keepdims=False)]
     for r in range(1, count):
         part = lax.dynamic_index_in_dim(parts, place ^ r, 0, keepdims=False)
-        shard = shard + line_send(bf16(part), r).astype(jnp.float32)
-    return shard.T
+        shard.append(line_send(bf16(part), r))
+    return shard
+
+
+def total_shard(shard):
+    return sum(block.astype(jnp.float32) for block in shard).T
 
 
 def exchange_weights(half_in, half_down):
@@ -199,16 +226,20 @@
     yield in_piece, down_piece.reshape(width, ranks * slices, part)
 
 
-def exchange_gradients(in_grad, down_grad, columns):
+def pack_gradients(in_grad, down_grad):
     ranks = lax.axis_size("dp")
     part = in_grad.shape[0]
+    columns = down_grad.shape[0]
     rows = in_grad.shape[1] // ranks
     slices = down_grad.shape[1] // ranks
     in_sent = in_grad.reshape(part, ranks, rows).transpose(1, 0, 2)
     down_sent = down_grad.reshape(columns, ranks, slices, part).transpose(1, 3, 2, 0)
-    sent = jnp.concatenate([in_sent, down_sent.reshape(ranks, part, slices * columns)], axis=2)
-    got = dp_exchange(sent)
-    return got[:, :, :rows], got[:, :, rows:].reshape(ranks, part, slices, columns)
+    return jnp.concatenate([in_sent, down_sent.reshape(ranks, part, slices * columns)], axis=2)
+
+
+def unpack_gradients(got, rows, columns):
+    ranks, part, width = got.shape
+    return got[:, :, :rows], got[:, :, rows:].reshape(ranks, part, -1, columns)
 
 
 def column_slices(own, other, first, target, width, slices):
@@ -272,8 +303,8 @@
     info, tokens, gain, queries = refs[:4]
     kv = refs[4 : 4 + ranks]
     own = refs[4 + ranks : 4 + 2 * ranks]
-    other = refs[4 + 2 * ranks : 4 + 3 * ranks]
-    attended, totals, middle, normed_again, bias, keys, values, values_t = refs[4 + 3 * ranks :]
+    other = [refs[4 + 2 * ranks].at[k] for k in range(ranks)]
+    attended, totals, middle, normed_again, bias, keys, values, values_t = refs[5 + 2 * ranks :]
     place = info[0]
     first = info[1] == 0
     rows = tokens.shape[0]
@@ -317,8 +348,8 @@
     got = refs[6 : 6 + ranks]
     kv = refs[6 + ranks : 6 + 2 * ranks]
     own = refs[6 + 2 * ranks : 6 + 3 * ranks]
-    other = refs[6 + 3 * ranks : 6 + 4 * ranks]
-    refs = refs[6 + 4 * ranks :]
+    other = [refs[6 + 3 * ranks].at[k] for k in range(ranks)]
+    refs = refs[7 + 3 * ranks :]
     middle_cot, middle_low, gain_grad, query_cot = refs[:4]
     kv_cot = refs[4 : 4 + ranks]
     bias, keys, values, keys_t, attended_cot, key_sum, value_sum, low_own, low_other = refs[
@@ -383,14 +414,11 @@
 
 
 def outer_kernel(ranks, slices, *refs):
-    info, left, right = refs[:3]
-    own = refs[3 : 3 + ranks]
-    other = refs[3 + ranks : 3 + 2 * ranks]
-    (turned,) = refs[3 + 2 * ranks :]
+    info, left, right, own, other, turned = refs
     place = info[0]
     parity = info[1]
-    width = own[0].shape[1]
-    part = own[0].shape[0] // slices
+    width = own.shape[2]
+    part = own.shape[1] // slices
     turned[...] = right[...].T
     for k in range(ranks):
         block = block_columns(left, place, k, width)
@@ -398,8 +426,8 @@
             at = pl.ds(j * part, part)
             mine = pl.ds(pl.multiple_of((2 * j + parity) * part, 16), part)
             theirs = pl.ds(pl.multiple_of((2 * j + 1 - parity) * part, 16), part)
-            own[k][at, :] = bf16(dot_nn(turned[mine, :], block))
-            other[k][at, :] = bf16(dot_nn(turned[theirs, :], block))
+            own[k, at, :] = bf16(dot_nn(turned[mine, :], block))
+            other[k, at, :] = bf16(dot_nn(turned[theirs, :], block))
 
 
 def project_back_kernel(ranks, *refs):
@@ -453,10 +481,11 @@
     input_grad[...] = bf16(middle_cot[...] + back)
 
 
-def call(kernel, args, outs, scratch, flops):
+def call(kernel, args, outs, scratch, micros):
     vmem = pl.BlockSpec(memory_space=pltpu.VMEM)
     moved = sum(math.prod(a.shape) * a.dtype.itemsize for a in args)
     moved += sum(math.prod(a.shape) * a.dtype.itemsize for a in outs)
+    moved *= min(micros, 1)
     return pl.pallas_call(
         kernel,
         out_shape=tuple(outs),
@@ -464,7 +493,9 @@
         out_specs=(vmem,) * len(outs),
         scratch_shapes=scratch,
         compiler_params=pltpu.CompilerParams(vmem_limit_bytes=VMEM_LIMIT),
-        cost_estimate=pl.CostEstimate(flops=flops, bytes_accessed=moved, transcendentals=0),
+        cost_estimate=pl.CostEstimate(
+            flops=micros * FLOPS_PER_MICRO, bytes_accessed=moved, transcendentals=0
+        ),
     )(*args)
 
 
@@ -476,14 +507,84 @@
     return jax.ShapeDtypeStruct(shape, jnp.bfloat16)
 
 
-def fetch(source, target, sem):
-    copy = pltpu.make_async_copy(source, target, sem)
-    copy.start()
-    return copy
-
-
-def unit_blocks(units):
-    return [(s, min(UNIT_TILE, units - s)) for s in range(0, units, UNIT_TILE)]
+class Chunk:
+    def __init__(self, size, lines):
+        self.lines = lines
+        self.slices = lines // 2
+        self.real = size // self.slices
+        self.deep = -(-self.real // 16) * 16
+        self.units = self.slices * self.deep
+        self.wide = -(-self.units // 128) * 128
+        self.columns = D // lines
+        self.folds = D // self.wide if self.columns * self.wide % (16 * D) == 0 else 1
+        self.low = self.columns // self.folds
+        self.step = self.deep + self.low
+        self.rows = lines * self.step
+        self.blocks = [
+            (s, min(UNIT_TILE, self.units - s)) for s in range(0, self.units, UNIT_TILE)
+        ]
+
+    def pack(self, in_piece, down_piece):
+        extra = self.deep - self.real
+        in_piece = jnp.pad(in_piece, ((0, extra), (0, 0)))
+        down_piece = jnp.pad(down_piece, ((0, 0), (0, 0), (0, extra)))
+        down_piece = down_piece.reshape(self.columns, self.units)
+        down_piece = jnp.pad(down_piece, ((0, 0), (0, self.wide - self.units)))
+        parts = [down_piece[i * self.low : (i + 1) * self.low] for i in range(self.folds)]
+        down_piece = jnp.concatenate(parts, axis=1)
+        down_piece = jnp.pad(down_piece, ((0, 0), (0, D - down_piece.shape[1])))
+        return jnp.concatenate([in_piece, down_piece])
+
+    def unpack(self, shard):
+        in_piece = shard[: self.real]
+        down_piece = shard[self.deep :]
+        parts = [
+            down_piece[:, i * self.wide : i * self.wide + self.units] for i in range(self.folds)
+        ]
+        down_piece = jnp.concatenate(parts)
+        down_piece = down_piece.reshape(self.columns, self.slices, self.deep)
+        return in_piece, down_piece[:, :, : self.real]
+
+    def in_parts(self, s, n, half):
+        parts = []
+        at = s
+        while at < s + n:
+            k = at // self.deep
+            count = min(s + n, (k + 1) * self.deep) - at
+            line = half * self.slices + k
+            parts.append((at - s, count, line * self.step + at - k * self.deep))
+            at += count
+        return parts
+
+    def down_parts(self, s, n):
+        width = min(self.wide, s + UNIT_TILE) - s
+        return [
+            (
+                line * self.columns + i * self.low,
+                line * self.step + self.deep,
+                i * self.wide + s,
+                width,
+            )
+            for line in range(self.lines)
+            for i in range(self.folds)
+        ]
+
+
+class Copies:
+    def __init__(self, sems):
+        self.sems = sems
+        self.used = 0
+
+    def start(self, source, target):
+        copy = pltpu.make_async_copy(source, target, self.sems.at[self.used])
+        self.used += 1
+        copy.start()
+        return copy
+
+
+def wait_all(copies):
+    for copy in copies:
+        copy.wait()
 
 
 def transpose_tokens(source, target, tokens):
@@ -493,33 +594,52 @@
         target[:, pl.ds(at, TURN_TILE)] = source[pl.ds(at, TURN_TILE), :].T
 
 
-def load_chunk(units, ranks, refs, na, oc, w, d, sem, back=None, mixed=None):
-    rows = refs["na"][0].shape[0]
-    slot = 0
-    first = []
-    later = []
-
-    def begin(source, target, into):
-        nonlocal slot
-        into.append(fetch(source, target, sem.at[slot]))
-        slot += 1
-
-    for k in range(ranks):
-        begin(refs["na"][k], na.at[pl.ds(k * rows, rows)], first)
-    for b, (s, n) in enumerate(unit_blocks(units)):
+def load_tokens(blocks, target, copies):
+    rows = blocks[0].shape[0]
+    return [
+        copies.start(block, target.at[pl.ds(k * rows, rows)]) for k, block in enumerate(blocks)
+    ]
+
+
+def load_chunk(chunk, ranks, na_in, oc_in, weights, na, oc, w, d, copies):
+    first = load_tokens(na_in, na, copies)
+    block_copies = []
+    for b, (s, n) in enumerate(chunk.blocks):
+        mine = []
         for half in range(2):
-            at = pl.ds(half * units + s, n)
-            begin(refs["w"].at[at], w.at[at], later if b else first)
+            for offset, count, row in chunk.in_parts(s, n, half):
+                target = w.at[pl.ds(half * chunk.units + s + offset, count)]
+                mine.append(copies.start(weights.at[pl.ds(row, count)], target))
         if b == 0:
-            for k in range(ranks):
-                begin(refs["oc"][k], oc.at[pl.ds(k * rows, rows)], first)
-            begin(refs["d"], d, first)
-            if back is not None:
-                begin(refs["back"], back, first)
-                begin(refs["mixed"], mixed, first)
-    for copy in first:
-        copy.wait()
-    return later
+            first += load_tokens(oc_in, oc, copies)
+        for column, row, at, width in chunk.down_parts(s, n):
+            source = weights.at[pl.ds(row, chunk.low), pl.ds(at, width)]
+            target = d.at[pl.ds(column, chunk.low), pl.ds(s, width)]
+            mine.append(copies.start(source, target))
+        block_copies.append(mine)
+    return first, block_copies
+
+
+def store_in(chunk, s, n, half, dw, at, weights_out, copies):
+    return [
+        copies.start(dw.at[pl.ds(at + offset, count)], weights_out.at[pl.ds(row, count)])
+        for offset, count, row in chunk.in_parts(s, n, half)
+    ]
+
+
+def store_down(chunk, s, n, dd, at, weights_out, copies):
+    return [
+        copies.start(
+            dd.at[pl.ds(column, chunk.low), pl.ds(at, width)],
+            weights_out.at[pl.ds(row, chunk.low), pl.ds(place, width)],
+        )
+        for column, row, place, width in chunk.down_parts(s, n)
+    ]
+
+
+def copy_count(chunk):
+    parts = sum(len(chunk.in_parts(s, n, 0)) for s, n in chunk.blocks)
+    return 2 * parts + len(chunk.blocks) * chunk.lines * chunk.folds
 
 
 def unit_block(units, s, n, tokens, na, oc, w, d, back, mixed, gt, ut, ht, at_row, add, final):
@@ -554,73 +674,81 @@
             mixed[at, :] = mixed_term
 
 
-def gradient_block(units, s, n, na, oc_t, gt, ut, ht, at_row, dw, dd):
+def gradient_block(n, na, oc_t, gt, ut, ht, at_row, dw, dw_gate, dw_up, dd, dd_at):
     at = pl.ds(at_row, n)
 
     @pl.loop(0, D // GRAD_TILE)
     def _(j):
         cols = pl.ds(pl.multiple_of(j * GRAD_TILE, GRAD_TILE), GRAD_TILE)
-        dw[pl.ds(s, n), cols] = bf16(dot_nn(gt[at, :], na[:, cols]))
-        dw[pl.ds(units + s, n), cols] = bf16(dot_nn(ut[at, :], na[:, cols]))
-        dd[cols, pl.ds(s, n)] = bf16(dot_nt(oc_t[cols, :], ht[at, :]))
-
-
-def first_chunk_kernel(units, ranks, *refs):
-    ins = {"na": refs[:ranks], "oc": refs[ranks : 2 * ranks]}
-    refs = refs[2 * ranks :]
-    ins["w"], ins["d"] = refs[:2]
-    back_out, mixed_out, dw_out, dd_out = refs[2:6]
-    na, oc, oc_t, w, d, dw, dd, back, mixed, gt, ut, ht, in_sem, out_sem = refs[6:]
+        dw[pl.ds(dw_gate, n), cols] = bf16(dot_nn(gt[at, :], na[:, cols]))
+        dw[pl.ds(dw_up, n), cols] = bf16(dot_nn(ut[at, :], na[:, cols]))
+        dd[cols, pl.ds(dd_at, n)] = bf16(dot_nt(oc_t[cols, :], ht[at, :]))
+
+
+def first_chunk_kernel(chunk, ranks, carried, *refs):
+    na_in = refs[:ranks]
+    oc_in = refs[ranks : 2 * ranks]
+    weights = refs[2 * ranks]
+    refs = refs[2 * ranks + 1 :]
+    if carried:
+        back_in, mixed_in = refs[:2]
+        refs = refs[2:]
+    back_out, mixed_out, weights_out = refs[:3]
+    na, oc, oc_t, w, d, dw, dd, back, mixed, gt, ut, ht, in_sem, out_sem = refs[3:]
     tokens = na.shape[0]
-    later = load_chunk(units, ranks, ins, na, oc, w, d, in_sem)
+    copies = Copies(in_sem)
+    first, block_copies = load_chunk(chunk, ranks, na_in, oc_in, weights, na, oc, w, d, copies)
+    if carried:
+        first.append(copies.start(back_in, back))
+        first.append(copies.start(mixed_in, mixed))
+    wait_all(first)
     transpose_tokens(oc, oc_t, tokens)
-    blocks = unit_blocks(units)
+    copies = Copies(out_sem)
     outs = []
-    for b, (s, n) in enumerate(blocks):
-        if b:
-            later[2 * b - 2].wait()
-            later[2 * b - 1].wait()
+    stored = []
+    for b, (s, n) in enumerate(chunk.blocks):
+        wait_all(block_copies[b])
+        add = carried or bool(b)
         unit_block(
-            units, s, n, tokens, na, oc, w, d, back, mixed, gt, ut, ht, 0, bool(b), False
+            chunk.units, s, n, tokens, na, oc, w, d, back, mixed, gt, ut, ht, 0, add, False
         )
-        if b == len(blocks) - 1:
-            outs.append(fetch(back, back_out, out_sem.at[0]))
-            outs.append(fetch(mixed, mixed_out, out_sem.at[1]))
-        gradient_block(units, s, n, na, oc_t, gt, ut, ht, 0, dw, dd)
-        for half in range(2):
-            at = pl.ds(half * units + s, n)
-            outs.append(fetch(dw.at[at], dw_out.at[at], out_sem.at[3 + 2 * b + half]))
-    outs.append(fetch(dd, dd_out, out_sem.at[2]))
-    for copy in outs:
-        copy.wait()
-
-
-def last_chunk_kernel(units, ranks, carried, *refs):
-    ins = {"na": refs[:ranks], "oc": refs[ranks : 2 * ranks]}
-    refs = refs[2 * ranks :]
-    ins["w"], ins["d"] = refs[:2]
-    refs = refs[2:]
+        if b == len(chunk.blocks) - 1:
+            outs.append(copies.start(back, back_out))
+            outs.append(copies.start(mixed, mixed_out))
+        wait_all(stored)
+        gradient_block(n, na, oc_t, gt, ut, ht, 0, dw, 0, UNIT_TILE, dd, 0)
+        stored = store_in(chunk, s, n, 0, dw, 0, weights_out, copies)
+        stored += store_in(chunk, s, n, 1, dw, UNIT_TILE, weights_out, copies)
+        stored += store_down(chunk, s, n, dd, 0, weights_out, copies)
+    wait_all(outs + stored)
+
+
+def last_chunk_kernel(chunk, ranks, carried, *refs):
+    na_in = refs[:ranks]
+    oc_in = refs[ranks : 2 * ranks]
+    weights = refs[2 * ranks]
+    refs = refs[2 * ranks + 1 :]
     if carried:
-        ins["back"], ins["mixed"] = refs[:2]
+        back_in, mixed_in = refs[:2]
         refs = refs[2:]
     back_out = refs[:ranks]
     mixed_out = refs[ranks : 2 * ranks]
-    gt_out, ut_out, ht_out = refs[2 * ranks : 2 * ranks + 3]
+    kept_out = refs[2 * ranks : 2 * ranks + 3]
     na, oc, w, d, back, mixed, gt, ut, ht, in_sem, out_sem = refs[2 * ranks + 3 :]
     tokens = na.shape[0]
     rows = tokens // ranks
+    copies = Copies(in_sem)
+    first, block_copies = load_chunk(chunk, ranks, na_in, oc_in, weights, na, oc, w, d, copies)
     if carried:
-        later = load_chunk(units, ranks, ins, na, oc, w, d, in_sem, back, mixed)
-    else:
-        later = load_chunk(units, ranks, ins, na, oc, w, d, in_sem)
-    blocks = unit_blocks(units)
+        first.append(copies.start(back_in, back))
+        first.append(copies.start(mixed_in, mixed))
+    wait_all(first)
+    copies = Copies(out_sem)
     outs = []
-    for b, (s, n) in enumerate(blocks):
-        if b:
-            later[2 * b - 2].wait()
-            later[2 * b - 1].wait()
+    for b, (s, n) in enumerate(chunk.blocks):
+        wait_all(block_copies[b])
         unit_block(
-            units,
+            chunk.units,
             s,
             n,
             tokens,
@@ -635,52 +763,45 @@
             ht,
             s,
             carried or bool(b),
-            b == len(blocks) - 1,
+            b == len(chunk.blocks) - 1,
         )
-        for i, (kept, target) in enumerate(((gt, gt_out), (ut, ut_out), (ht, ht_out))):
+        for kept, target in zip((gt, ut, ht), kept_out):
             at = pl.ds(s, n)
-            outs.append(fetch(kept.at[at], target.at[at], out_sem.at[2 * ranks + 3 * b + i]))
+            outs.append(copies.start(kept.at[at], target.at[at]))
     for k in range(ranks):
         at = pl.ds(k * rows, rows)
-        outs.append(fetch(na.at[at], back_out[k], out_sem.at[k]))
-        outs.append(fetch(oc.at[at], mixed_out[k], out_sem.at[ranks + k]))
-    for copy in outs:
-        copy.wait()
-
-
-def gradient_kernel(units, ranks, *refs):
+        outs.append(copies.start(na.at[at], back_out[k]))
+        outs.append(copies.start(oc.at[at], mixed_out[k]))
+    wait_all(outs)
+
+
+def gradient_kernel(chunk, ranks, *refs):
     na_in = refs[:ranks]
     oc_in = refs[ranks : 2 * ranks]
-    gt_in, ut_in, ht_in, dw_out, dd_out = refs[2 * ranks : 2 * ranks + 5]
-    na, oc, oc_t, gt, ut, ht, dw, dd, in_sem, out_sem = refs[2 * ranks + 5 :]
+    kept_in = refs[2 * ranks : 2 * ranks + 3]
+    weights_out, na, oc, oc_t, gt, ut, ht, dw, dd, in_sem, out_sem = refs[2 * ranks + 3 :]
     tokens = na.shape[0]
-    rows = tokens // ranks
-    copies = []
-    for k in range(ranks):
-        at = pl.ds(k * rows, rows)
-        copies.append(fetch(oc_in[k], oc.at[at], in_sem.at[k]))
-    for k in range(ranks):
-        at = pl.ds(k * rows, rows)
-        copies.append(fetch(na_in[k], na.at[at], in_sem.at[ranks + k]))
-    for i, (source, kept) in enumerate(((gt_in, gt), (ut_in, ut), (ht_in, ht))):
-        copies.append(fetch(source, kept, in_sem.at[2 * ranks + i]))
-    for copy in copies[:ranks]:
-        copy.wait()
+    copies = Copies(in_sem)
+    first = load_tokens(oc_in, oc, copies)
+    later = load_tokens(na_in, na, copies)
+    later += [copies.start(source, kept) for source, kept in zip(kept_in, (gt, ut, ht))]
+    wait_all(first)
     transpose_tokens(oc, oc_t, tokens)
-    for copy in copies[ranks:]:
-        copy.wait()
+    if chunk.wide > chunk.units:
+        spare = chunk.wide - chunk.units
+        dd[:, pl.ds(chunk.units, spare)] = jnp.zeros((D, spare), jnp.bfloat16)
+    wait_all(later)
+    copies = Copies(out_sem)
     outs = []
-    for b, (s, n) in enumerate(unit_blocks(units)):
-        gradient_block(units, s, n, na, oc_t, gt, ut, ht, s, dw, dd)
-        for half in range(2):
-            at = pl.ds(half * units + s, n)
-            outs.append(fetch(dw.at[at], dw_out.at[at], out_sem.at[1 + 2 * b + half]))
-    outs.append(fetch(dd, dd_out, out_sem.at[0]))
-    for copy in outs:
-        copy.wait()
-
-
-def hbm_call(kernel, args, outs, scratch, flops):
+    for s, n in chunk.blocks:
+        gradient_block(n, na, oc_t, gt, ut, ht, s, dw, s, chunk.units + s, dd, s)
+        outs += store_in(chunk, s, n, 0, dw, s, weights_out, copies)
+        outs += store_in(chunk, s, n, 1, dw, chunk.units + s, weights_out, copies)
+        outs += store_down(chunk, s, n, dd, s, weights_out, copies)
+    wait_all(outs)
+
+
+def hbm_call(kernel, args, outs, scratch, micros):
     moved = sum(math.prod(a.shape) * a.dtype.itemsize for a in args)
     moved += sum(math.prod(a.shape) * a.dtype.itemsize for a in outs)
     anywhere = pl.BlockSpec(memory_space=pl.ANY)
@@ -691,7 +812,9 @@
         out_specs=(anywhere,) * len(outs),
         scratch_shapes=scratch,
         compiler_params=pltpu.CompilerParams(vmem_limit_bytes=VMEM_LIMIT),
-        cost_estimate=pl.CostEstimate(flops=flops, bytes_accessed=moved, transcendentals=0),
+        cost_estimate=pl.CostEstimate(
+            flops=micros * FLOPS_PER_MICRO, bytes_accessed=moved, transcendentals=0
+        ),
     )(*args)
 
 
@@ -703,82 +826,79 @@
     return pltpu.VMEM(shape, jnp.float32)
 
 
-def first_chunk(na, oc, w, d):
+def first_chunk(chunk, na, oc, weights, carry):
     ranks = len(na)
     tokens = ranks * na[0].shape[0]
-    units = d.shape[1]
-    blocks = len(unit_blocks(units))
     scratch = [
         vmem_bf16(tokens, D),
         vmem_bf16(tokens, D),
         vmem_bf16(D, tokens),
-        vmem_bf16(2 * units, D),
-        vmem_bf16(D, units),
-        vmem_bf16(2 * units, D),
-        vmem_bf16(D, units),
+        vmem_bf16(2 * chunk.units, D),
+        vmem_bf16(D, chunk.wide),
+        vmem_bf16(2 * UNIT_TILE, D),
+        vmem_bf16(D, UNIT_TILE),
         vmem_f32(tokens, D),
         vmem_f32(tokens, D),
         vmem_bf16(UNIT_TILE, tokens),
         vmem_bf16(UNIT_TILE, tokens),
         vmem_bf16(UNIT_TILE, tokens),
-        pltpu.SemaphoreType.DMA((2 * ranks + 1 + 2 * blocks,)),
-        pltpu.SemaphoreType.DMA((3 + 2 * blocks,)),
+        pltpu.SemaphoreType.DMA((2 * ranks + 2 + copy_count(chunk),)),
+        pltpu.SemaphoreType.DMA((2 + copy_count(chunk),)),
     ]
-    outs = [
-        f32_like(tokens, D),
-        f32_like(tokens, D),
-        bf16_like(2 * units, D),
-        bf16_like(D, units),
-    ]
-    kernel = functools.partial(first_chunk_kernel, units, ranks)
-    return hbm_call(kernel, [*na, *oc, w, d], outs, scratch, 18 * tokens * D * units)
-
-
-def last_chunk(na, oc, w, d, carry):
+    outs = [f32_like(tokens, D), f32_like(tokens, D), bf16_like(chunk.rows, D)]
+    kernel = functools.partial(first_chunk_kernel, chunk, ranks, bool(carry))
+    return hbm_call(kernel, [*na, *oc, weights, *carry], outs, scratch, 68)
+
+
+def last_chunk(chunk, na, oc, weights, carry):
     ranks = len(na)
     rows = na[0].shape[0]
     tokens = ranks * rows
-    units = d.shape[1]
-    blocks = len(unit_blocks(units))
     scratch = [
         vmem_bf16(tokens, D),
         vmem_bf16(tokens, D),
-        vmem_bf16(2 * units, D),
-        vmem_bf16(D, units),
+        vmem_bf16(2 * chunk.units, D),
+        vmem_bf16(D, chunk.wide),
         vmem_f32(tokens, D),
         vmem_f32(tokens, D),
-        vmem_bf16(units, tokens),
-        vmem_bf16(units, tokens),
-        vmem_bf16(units, tokens),
-        pltpu.SemaphoreType.DMA((2 * ranks + 3 + 2 * blocks,)),
-        pltpu.SemaphoreType.DMA((2 * ranks + 3 * blocks,)),
+        vmem_bf16(chunk.units, tokens),
+        vmem_bf16(chunk.units, tokens),
+        vmem_bf16(chunk.units, tokens),
+        pltpu.SemaphoreType.DMA((2 * ranks + 2 + copy_count(chunk),)),
+        pltpu.SemaphoreType.DMA((2 * ranks + 3 * len(chunk.blocks),)),
     ]
-    outs = [bf16_like(rows, D)] * (2 * ranks) + [bf16_like(units, tokens)] * 3
-    kernel = functools.partial(last_chunk_kernel, units, ranks, bool(carry))
-    got = hbm_call(kernel, [*na, *oc, w, d, *carry], outs, scratch, 12 * tokens * D * units)
+    outs = [bf16_like(rows, D)] * (2 * ranks) + [bf16_like(chunk.units, tokens)] * 3
+    kernel = functools.partial(last_chunk_kernel, chunk, ranks, bool(carry))
+    got = hbm_call(
+        kernel, [*na, *oc, weights, *carry], outs, scratch, 35
+    )
     return got[:ranks], got[ranks : 2 * ranks], got[2 * ranks :]
 
 
-def chunk_gradients(na, oc, kept):
+def chunk_gradients(chunk, na, oc, kept):
     ranks = len(na)
     tokens = ranks * na[0].shape[0]
-    units = kept[0].shape[0]
-    blocks = len(unit_blocks(units))
     scratch = [
         vmem_bf16(tokens, D),
         vmem_bf16(tokens, D),
         vmem_bf16(D, tokens),
-        vmem_bf16(units, tokens),
-        vmem_bf16(units, tokens),
-        vmem_bf16(units, tokens),
-        vmem_bf16(2 * units, D),
-        vmem_bf16(D, units),
+        vmem_bf16(chunk.units, tokens),
+        vmem_bf16(chunk.units, tokens),
+        vmem_bf16(chunk.units, tokens),
+        vmem_bf16(2 * chunk.units, D),
+        vmem_bf16(D, chunk.wide),
         pltpu.SemaphoreType.DMA((2 * ranks + 3,)),
-        pltpu.SemaphoreType.DMA((1 + 2 * blocks,)),
+        pltpu.SemaphoreType.DMA((copy_count(chunk),)),
     ]
-    outs = [bf16_like(2 * units, D), bf16_like(D, units)]
-    kernel = functools.partial(gradient_kernel, units, ranks)
-    return hbm_call(kernel, [*na, *oc, *kept], outs, scratch, 6 * tokens * D * units)
+    kernel = functools.partial(gradient_kernel, chunk, ranks)
+    (terms,) = hbm_call(
+        kernel,
+        [*na, *oc, *kept],
+        [bf16_like(chunk.rows, D)],
+        scratch,
+        16,
+    )
+    return terms
 
 
 def sharded_pass(tokens, cotangent, lengths, half_qkv, half_out, half_in, half_down, half_small):
@@ -792,60 +912,54 @@
     info = jnp.stack([place, lax.rem(lax.axis_index("fsdp"), 2), lengths[0]])
 
     small_rows, small_columns = half_small.shape
-    small_size = small_rows * small_columns
     columns = half_qkv.shape[1]
-    small_part = jnp.pad(half_small.reshape(1, small_size), ((0, 15), (0, block - small_size)))
-    qkv_along = gather_line(jnp.concatenate([half_qkv.T, small_part]))
-    exchange = exchange_weights(half_in, half_down)
-    sent = next(exchange)
-    sent, qkv_along = lax.optimization_barrier((sent, qkv_along))
-    got = dp_exchange(sent)
-    qkv_own, qkv_other = gather_rest(qkv_along)
-    half_out, qkv_own[1] = lax.optimization_barrier((half_out, qkv_own[1]))
-    out_along = gather_line(half_out.T)
-    out_along, qkv_own[ranks - 1] = lax.optimization_barrier((out_along, qkv_own[ranks - 1]))
-    out_own, out_other = gather_rest(out_along)
-
-    small_pairs = []
-    for mine, theirs in zip(qkv_own, qkv_other):
-        mine, theirs = (
-            part.reshape(slices, columns + 16, block)[:, columns, :small_size]
-            for part in (mine, theirs)
-        )
-        even = jnp.where(is_even(), mine, theirs)
-        odd = jnp.where(is_even(), theirs, mine)
-        small_pairs.append(jnp.stack([even, odd], axis=1))
-    small_stack = jnp.stack(small_pairs)
+    line = jnp.concatenate([half_qkv.T, half_out.T])
+    line = scoped("matrix_line", line_gather, line)
+    qkv_along = line[:, :columns].reshape(-1, block)
+    out_along = line[:, columns:].reshape(-1, block)
+    half_small, qkv_along = lax.optimization_barrier((half_small, qkv_along))
+    small_line = scoped("small_gather", line_gather, half_small)
+    small_other = scoped("small_gather", core_swap, small_line)
+    small_line = jnp.stack(
+        [
+            jnp.where(is_even(), small_line, small_other),
+            jnp.where(is_even(), small_other, small_line),
+        ],
+        axis=1,
+    )
+    small_line = small_line.reshape(lines, small_rows, small_columns)
+    small_stack = jnp.stack(
+        [small_line]
+        + [scoped("small_gather", dp_send, small_line, k) for k in range(1, ranks)]
+    )
     small_vec = jnp.stack(
         [
             lax.dynamic_index_in_dim(small_stack, place ^ a, 0, keepdims=False)
             for a in range(ranks)
         ]
     )
-    small_vec = small_vec.reshape(ranks, lines, small_rows, small_columns)
     small_vec = small_vec.transpose(0, 2, 1, 3).reshape(-1).astype(jnp.float32)
     gain_attn, gain_mlp, biases = unpack_small(small_vec)
     gain_attn = gain_attn[None]
     gain_mlp = gain_mlp[None]
 
+    exchange = exchange_weights(half_in, half_down)
+    got = scoped("weights_exchange", dp_exchange, next(exchange))
+    got, out_along, qkv_along = lax.optimization_barrier((got, out_along, qkv_along))
+    qkv_own = scoped("qkv_gather", dp_gather, qkv_along)
+    qkv_other = [scoped("qkv_swap", core_swap, block) for block in qkv_own]
+    out_along, qkv_other = lax.optimization_barrier((out_along, qkv_other))
+    out_near = scoped("out_gather", gather_near, out_along)
+
     in_piece, down_piece = exchange.send(got)
-    in_chunks = []
-    down_chunks = []
+    chunks = [Chunk(size, lines) for size in CHUNKS]
+    gathered = []
     start = 0
-    for size in CHUNKS:
-        width = size // slices
-        down_chunks.append(
-            lax.all_gather(
-                down_piece[:, :, start : start + width].reshape(-1, size),
-                "fsdp",
-                axis=0,
-                tiled=True,
-            )
-        )
-        in_chunks.append(
-            lax.all_gather(in_piece[start : start + width], "fsdp", axis=0, tiled=True)
-        )
-        start += width
+    for chunk in chunks:
+        stop = start + chunk.real
+        packed = chunk.pack(in_piece[start:stop], down_piece[:, :, start:stop])
+        gathered.append(lax.all_gather(packed, "fsdp", axis=0, tiled=True))
+        start = stop
 
     query_places = place * rows + jnp.arange(rows, dtype=jnp.int32)
     cosine, sine = rope_tables(query_places.astype(jnp.float32))
@@ -855,18 +969,21 @@
         [info, inputs, gain_attn, biases[None], cosine, sine, *qkv_own, *qkv_other],
         [bf16_like(rows, D), bf16_like(rows, D), bf16_like(rows, 2 * KV_WIDTH)],
         [vmem_f32(rows, QKV)],
-        2 * rows * D * QKV,
-    )
-    kv_blocks = dp_gather(kv)
+        7,
+    )
+    kv, out_near = lax.optimization_barrier((kv, out_near))
+    out_own = scoped("out_gather", gather_far, out_near)
+    kv_blocks = scoped("kv_gather", dp_gather, kv)
+    out_other = scoped("out_swap", core_swap, jnp.stack(out_own))
 
     valid = query_places < lengths[0]
     out_cot = jnp.where(valid[:, None], cotangent[0], jnp.zeros_like(cotangent[0]))
     out_cot, *kv_blocks = lax.optimization_barrier((out_cot, *kv_blocks))
-    cot_blocks = dp_gather(out_cot)
+    cot_blocks = scoped("cot_gather", dp_gather, out_cot)
 
     attended, totals, middle, normed_again = call(
         functools.partial(attend_kernel, ranks, slices),
-        [info, inputs, gain_mlp, queries, *kv_blocks, *out_own, *out_other],
+        [info, inputs, gain_mlp, queries, *kv_blocks, *out_own, out_other],
         [bf16_like(rows, D), f32_like(16, rows), f32_like(rows, D), bf16_like(rows, D)],
         [
             vmem_f32(ranks * rows, rows),
@@ -874,49 +991,37 @@
             vmem_bf16(ranks * rows, KV_WIDTH),
             vmem_bf16(KV_WIDTH, ranks * rows),
         ],
-        2 * rows * D * D + 4 * rows * D * ranks * rows,
-    )
-    normed_blocks = dp_gather(normed_again)
-
+        24,
+    )
+    normed_blocks = scoped("normed_gather", dp_gather, normed_again)
+
+    *before, end = zip(chunks, gathered)
     carry = ()
-    in_terms = []
-    down_terms = []
-    for index, size in enumerate(CHUNKS):
-        in_mat = in_chunks[index]
-        down_mat = down_chunks[index]
-        if index < len(CHUNKS) - 1:
-            back, mixed, in_term, down_term = first_chunk(
-                normed_blocks, cot_blocks, in_mat, down_mat
-            )
-            carry = (back, mixed)
-        else:
-            back_blocks, mixed_blocks, kept = last_chunk(
-                normed_blocks, cot_blocks, in_mat, down_mat, carry
-            )
-            back_got = [dp_send(back_blocks[k], k) for k in range(1, ranks)]
-            in_term, down_term = chunk_gradients(normed_blocks, cot_blocks, kept)
-        in_terms.append(in_term)
-        down_terms.append(down_term)
-    in_terms[-1], down_terms[-1], back_blocks, back_got, mixed_blocks = lax.optimization_barrier(
-        (in_terms[-1], down_terms[-1], back_blocks, back_got, mixed_blocks)
-    )
-    mixed = middle + mixed_blocks[0].astype(jnp.float32)
-    for k in range(1, ranks):
-        mixed = mixed + dp_send(mixed_blocks[k], k).astype(jnp.float32)
-    in_parts = []
-    down_parts = []
-    for in_term, down_term, size in zip(in_terms, down_terms, CHUNKS):
-        down_sum = lax.psum_scatter(down_term, "fsdp", scatter_dimension=0, tiled=True)
-        in_sum = lax.psum_scatter(in_term, "fsdp", scatter_dimension=0, tiled=True)
-        down_sum = down_sum.reshape(-1, slices, size // slices)
-        in_part, down_part = exchange_gradients(in_sum, down_sum, half_down.shape[1])
-        in_parts.append(in_part)
-        down_parts.append(down_part)
-    in_grad = jnp.concatenate(in_parts, axis=1)
-    in_grad = in_grad.transpose(2, 0, 1).reshape(half_in.shape).astype(jnp.float32)
-    down_grad = jnp.concatenate(down_parts, axis=1)
-    down_grad = down_grad.transpose(2, 0, 1, 3).reshape(half_down.shape).astype(jnp.float32)
-
+    terms = []
+    for chunk, weights in before:
+        back, mixed, term = first_chunk(chunk, normed_blocks, cot_blocks, weights, carry)
+        carry = (back, mixed)
+        terms.append(term)
+    chunk, weights = end
+    back_blocks, mixed_blocks, kept = last_chunk(
+        chunk, normed_blocks, cot_blocks, weights, carry
+    )
+    back_got = [scoped("back_reduce", dp_send, back_blocks[k], k) for k in range(1, ranks)]
+    term = chunk_gradients(chunk, normed_blocks, cot_blocks, kept)
+    term, back_blocks, back_got, mixed_blocks = lax.optimization_barrier(
+        (term, back_blocks, back_got, mixed_blocks)
+    )
+    terms.append(term)
+    first_shard = lax.psum_scatter(terms[0], "fsdp", scatter_dimension=0, tiled=True)
+
+    def pack_chunk(chunk, shard):
+        return scoped("gradient_exchange", pack_gradients, *chunk.unpack(shard))
+
+    def exchange_chunk(sent):
+        got = scoped("gradient_exchange", dp_exchange, sent)
+        return unpack_gradients(got, half_in.shape[0], half_down.shape[1])
+
+    mixed_got = [scoped("mixed_reduce", dp_send, mixed_blocks[k], k) for k in range(1, ranks - 1)]
     middle_cot, middle_low, gain_mlp_grad, query_cot, *kv_cot = call(
         functools.partial(attend_back_kernel, ranks, slices),
         [
@@ -930,7 +1035,7 @@
             *back_got,
             *kv_blocks,
             *out_own,
-            *out_other,
+            out_other,
         ],
         [f32_like(rows, D), bf16_like(rows, D), f32_like(1, D), f32_like(rows, D)]
         + [bf16_like(rows, 2 * KV_WIDTH)] * ranks,
@@ -945,22 +1050,28 @@
             vmem_bf16(rows, D // 2),
             vmem_bf16(rows, D // 2),
         ],
-        2 * rows * D * D + 10 * rows * D * ranks * rows,
-    )
-    kv_got = [dp_send(kv_cot[k], k) for k in range(1, ranks)]
+        31,
+    )
 
     def outer(left, right):
         columns = right.shape[1]
-        terms = call(
+        return call(
             functools.partial(outer_kernel, ranks, slices),
             [info, left, right],
-            [bf16_like(columns // 2, block)] * (2 * ranks),
+            [bf16_like(ranks, columns // 2, block)] * 2,
             [vmem_bf16(columns, rows)],
-            2 * rows * D * columns,
+            0,
         )
-        return reduce_matrix(terms[:ranks], terms[ranks:])
-
-    out_grad = outer(attended, middle_low)
+
+    kv_cot, middle_low, mixed_got = lax.optimization_barrier((kv_cot, middle_low, mixed_got))
+    kv_got = [scoped("kv_reduce", dp_send, kv_cot[k], k) for k in range(1, ranks)]
+    out_own_term, out_other_term = outer(attended, middle_low)
+
+
+    kv_got, out_own_term, out_other_term = lax.optimization_barrier(
+        (kv_got, out_own_term, out_other_term)
+    )
+    out_swapped = scoped("out_core", core_swap, out_other_term)
     projected_low, bias_grad = call(
         functools.partial(project_back_kernel, ranks),
         [info, query_cot, cosine, sine, kv_cot[0], *kv_got],
@@ -968,22 +1079,82 @@
         [],
         0,
     )
-    qkv_grad = outer(normed, projected_low)
+    projected_low, out_swapped = lax.optimization_barrier((projected_low, out_swapped))
+    out_got = scoped("out_dp", reduce_over_dp, sum_blocks(out_own_term, out_swapped))
+    qkv_own_term, qkv_other_term = outer(normed, projected_low)
+
+    projected_low, qkv_own_term, qkv_other_term, first_shard, last_term = (
+        lax.optimization_barrier(
+            (projected_low, qkv_own_term, qkv_other_term, first_shard, terms[1])
+        )
+    )
+    last_shard = lax.psum_scatter(last_term, "fsdp", scatter_dimension=0, tiled=True)
+    qkv_swapped = scoped("qkv_core", core_swap, qkv_other_term)
     input_grad, gain_attn_grad = call(
         functools.partial(input_back_kernel, ranks, slices),
         [info, projected_low, inputs, gain_attn, middle_cot, *qkv_own, *qkv_other],
         [bf16_like(rows, D), f32_like(1, D)],
         [vmem_bf16(rows, QKV // 2), vmem_bf16(rows, QKV // 2), vmem_f32(rows, D)],
-        2 * rows * D * QKV,
-    )
+        0,
+    )
+
     small_term = group_small(gain_attn_grad[0], gain_mlp_grad[0], bias_grad[0])
-    small_sum = sum_everywhere(small_term)
-    small_grad = lax.dynamic_slice(
-        small_sum,
-        (place * small_rows, lax.axis_index("fsdp") * small_columns),
-        (small_rows, small_columns),
-    )
-    return (bf16(mixed), input_grad, qkv_grad, out_grad, in_grad, down_grad, small_sum, small_grad)
+    small_term = small_term.reshape(ranks, small_rows, slices, 2, small_columns)
+    small_term = small_term.transpose(3, 0, 2, 1, 4).reshape(2, ranks, slices, -1)
+    small_parity = lax.rem(lax.axis_index("fsdp"), 2)
+    small_own = lax.dynamic_index_in_dim(small_term, small_parity, 0, keepdims=False)
+    small_other = lax.dynamic_index_in_dim(small_term, 1 - small_parity, 0, keepdims=False)
+    small_sums = small_own + scoped("small_core", core_swap, small_other)
+
+    qkv_swapped, out_got, small_sums, first_shard = lax.optimization_barrier(
+        (qkv_swapped, out_got, small_sums, first_shard)
+    )
+    small_rest = ((0, 0), (0, 15), (0, block - small_sums.shape[2]))
+    qkv_sums = []
+    for k, total in enumerate(sum_blocks(qkv_own_term, qkv_swapped)):
+        extra = jnp.pad(dp_own(small_sums, k)[:, None], small_rest)
+        total = jnp.concatenate([total.reshape(slices, -1, block), extra], axis=1)
+        qkv_sums.append(total.reshape(-1, block))
+    qkv_got = scoped("qkv_dp", reduce_over_dp, qkv_sums)
+    out_shard = scoped("out_line", reduce_over_line, out_got)
+    squares = sum_of_squares(first_shard)
+    first_sent = pack_chunk(chunks[0], first_shard)
+
+    qkv_got, out_shard, squares, first_sent = lax.optimization_barrier(
+        (qkv_got, out_shard, squares, first_sent)
+    )
+    qkv_shard = scoped("qkv_line", reduce_over_line, qkv_got)
+    out_grad = total_shard(out_shard)
+    squares = squares + sum_of_squares(out_grad) + sum_of_squares(last_shard)
+
+    qkv_shard, squares, last_shard, first_sent = lax.optimization_barrier(
+        (qkv_shard, squares, last_shard, first_sent)
+    )
+    qkv_shard = sum(part.astype(jnp.float32) for part in qkv_shard)
+    squares = squares + sum_of_squares(qkv_shard)
+    squares = scoped("norm_sum", sum_over_dp, squares)
+    first_sent, last_shard, squares = lax.optimization_barrier((first_sent, last_shard, squares))
+    total_squares = scoped("norm_sum", sum_over_line, scoped("norm_sum", sum_over_core, squares))
+    qkv_grad = lax.optimization_barrier(qkv_shard[:columns].T)
+    small_grad = qkv_shard[columns, : small_rows * small_columns]
+    small_grad = small_grad.reshape(small_rows, small_columns)
+    in_first, down_first = exchange_chunk(first_sent)
+    in_last, down_last = exchange_chunk(pack_chunk(chunks[1], last_shard))
+    in_grad = jnp.concatenate([in_first, in_last], axis=1)
+    in_grad = in_grad.transpose(2, 0, 1).reshape(half_in.shape)
+    down_grad = jnp.concatenate([down_first, down_last], axis=1)
+    down_grad = down_grad.transpose(2, 0, 1, 3).reshape(half_down.shape)
+    in_grad, down_grad, mixed_last = lax.optimization_barrier(
+        (in_grad, down_grad, mixed_blocks[-1])
+    )
+    in_grad = in_grad.astype(jnp.float32)
+    down_grad = down_grad.astype(jnp.float32)
+    mixed_got.append(scoped("mixed_reduce", dp_send, mixed_last, ranks - 1))
+    mixed = middle + mixed_blocks[0].astype(jnp.float32)
+    for got in mixed_got:
+        mixed = mixed + got.astype(jnp.float32)
+    mixed = bf16(mixed)
+    return (mixed, input_grad, total_squares, qkv_grad, out_grad, in_grad, down_grad, small_grad)
 
 
 def per_device(
@@ -1016,11 +1187,7 @@
         bf16(down_weight),
         bf16(small_params),
     )
-    mixed, input_cot, qkv_grad, out_grad, in_grad, down_grad, small_sum, small_grad = results
-    local_squares = sum(
-        (jnp.sum(piece * piece) for piece in (qkv_grad, out_grad, in_grad, down_grad))
-    )
-    total_squares = sum_everywhere(local_squares) + jnp.sum(small_sum * small_sum)
+    mixed, input_cot, total_squares, qkv_grad, out_grad, in_grad, down_grad, small_grad = results
     grad_norm = jnp.sqrt(total_squares)
     clip_factor = CLIP_NORM / jnp.maximum(grad_norm, CLIP_NORM)
     outs = [mixed[None], input_cot[None], grad_norm]

time: 755 us -> 649 us (0.86)
  waiting for transfers between devices: 314 us -> 180 us
  local copies, waits for them, and re-layouts: 37.2 us -> 66.4 us
  other arithmetic: 56.9 us -> 67 us
  starting transfers between devices: 101 us -> 92.3 us
    ppermute x45 -> x50, waiting for transfers between devices: 286 us -> 127 us  [dp_send(): return lax.ppermute(block, 'dp', [(i, i ^ k) for i in range(count)])]
    ppermute x18 -> x15, waiting for transfers between devices: 23.8 us -> 46.6 us  [line_send(): return lax.ppermute(block, 'fsdp', [(i, i ^ 2 * r) for i in range(count)])]
    ppermute x18 -> x15, starting transfers between devices: 44.5 us -> 28 us  [line_send(): return lax.ppermute(block, 'fsdp', [(i, i ^ 2 * r) for i in range(count)])]
    ppermute x45 -> x50, starting transfers between devices: 52.7 us -> 61.2 us  [dp_send(): return lax.ppermute(block, 'dp', [(i, i ^ k) for i in range(count)])]
    unnamed x111 -> x130, local copies, waits for them, and re-layouts: 13.6 us -> 17.4 us
  transfers between devices with their start and end apart: 89 -> 79, of which waited for: 37 -> 35; matrix products, arithmetic and copies ran while one was open for 6% -> 15% of each run, Pallas kernels for 29% -> 33%
where the time goes in v3:
time: 649 us; the launch traced here: 643 us
  Pallas kernels  213 us (33%)
  waiting for transfers between devices  180 us (28%)
  starting transfers between devices  92.3 us (14%)
  other arithmetic  67 us (10%)
  local copies, waits for them, and re-layouts  66.4 us (10%)
  between operations  24.2 us (4%)
    ppermute x50, waiting for transfers between devices, dp_send(): return lax.ppermute(block, 'dp', [(i, i ^ k) for i in range(count)])  127 us
    pallas_call x3, Pallas kernels, hbm_call(): pl.pallas_call(kernel, out_shape=tuple(outs), in_specs=[anywhere] * len(a...  122 us
    pallas_call x7, Pallas kernels, call(): pl.pallas_call(kernel, out_shape=tuple(outs), in_specs=[pl.BlockSpec(memo...  91.7 us
    ppermute x50, starting transfers between devices, dp_send(): return lax.ppermute(block, 'dp', [(i, i ^ k) for i in range(count)])  61.2 us
    ppermute x15, waiting for transfers between devices, line_send(): return lax.ppermute(block, 'fsdp', [(i, i ^ 2 * r) for i in range(count)])  46.6 us
    ppermute x15, starting transfers between devices, line_send(): return lax.ppermute(block, 'fsdp', [(i, i ^ 2 * r) for i in range(count)])  28 us
    unnamed x130, local copies, waits for them, and re-layouts  17.4 us
    convert_element_type x5, other arithmetic, update(): return (weight_new, first_new, second_new, weight_new.astype(jnp.bfloat16))  15.5 us
  transfers between devices with their start and end apart: 79, of which 35 were waited for; matrix products, arithmetic and copies ran while one was open for 15% of the time, Pallas kernels for 33%

profile of v3, /device:TPU:0, one launch (start us, length us, event | category | flops | bytes accessed | tf_op | source)
XLA Modules:
  0.0 643.0 jit_solution(11569467600074272684)
XLA Ops:
  33.1 10.4 %collective-permute-done.1 = bf16[448,384]{0,1:T(8,128)(2,1)} collective-permute-done((bf16[448,384]{0,1:T(8,128)(2,1)}, bf16[448,384]{0,1:T(8,128)(2,1)}, u32[]{:S(2)}, u32[]{:S(2)}) %collective-permute-start.1) | collective-permute-done | bytes 344096 | tf_op jit(solution)/shard_map/matrix_line/ppermute | solution.py:153
  47.0 12.6 %collective-permute-done.11 = bf16[560,576]{1,0:T(8,128)(2,1)} collective-permute-done((bf16[560,576]{1,0:T(8,128)(2,1)}, bf16[560,576]{1,0:T(8,128)(2,1)}, u32[]{:S(2)}, u32[]{:S(2)}) %collective-permute-start.11) | collective-permute-done | bytes 645152 | tf_op jit(solution)/shard_map/weights_exchange/ppermute | solution.py:116
  82.2 5.5 collective-permute-done.13.refs_7_.refs_6_
  107.6 7.5 %shard_map.353 = (bf16[320,1536]{1,0:T(8,128)(2,1)}, bf16[320,1536]{1,0:T(8,128)(2,1)}, bf16[320,512]{1,0:T(8,128)(2,1)}) custom-call(s32[3]{0:T(128)} %pad_add_fusion.refs_0_, bf16[320,1536]{1,0:T(8,128)(2,1)} %bitcast.200, f32[1,1536]{1,0:T(1,128)} %broadcast_in_dim_reshape.7.refs_2_.refs_3_, f32[1,2048]{1,0:T(1,128)} %bitcast.212, ...), custom_call_target="tpu_custom_call" | custom-call | flops 8049999872 | bytes 9910284 | tf_op jit(solution)/shard_map/pallas_call | solution.py:489
  124.4 5.7 collective-permute-done.27
  138.6 7.6 %collective-permute-done.23.refs_5_.refs_11_ = bf16[320,512]{1,0:T(8,128)(2,1)S(1)} collective-permute-done((bf16[320,512]{1,0:T(8,128)(2,1)}, bf16[320,512]{1,0:T(8,128)(2,1)S(1)}, u32[]{:S(2)}, u32[]{:S(2)}) %collective-permute-start.23) | collective-permute-done | bytes 327712 | tf_op jit(solution)/shard_map/kv_gather/ppermute | solution.py:116
  156.3 24.0 %shard_map.354 = (bf16[320,1536]{1,0:T(8,128)(2,1)}, f32[16,320]{1,0:T(8,128)}, f32[320,1536]{1,0:T(8,128)}, bf16[320,1536]{1,0:T(8,128)(2,1)}) custom-call(s32[3]{0:T(128)} %pad_add_fusion.refs_0_, bf16[320,1536]{1,0:T(8,128)(2,1)} %bitcast.201, f32[1,1536]{1,0:T(1,128)} %broadcast_in_dim_reshape.6.refs_2_.refs_3_, ...), custom_call_target="tpu_custom_call" | custom-call | flops 27599998976 | bytes 11954188 | tf_op jit(solution)/shard_map/pallas_call | solution.py:489
  184.6 20.6 %collective-permute-done.30.refs_1_ = bf16[320,1536]{1,0:T(8,128)(2,1)S(1)} collective-permute-done((bf16[320,1536]{1,0:T(8,128)(2,1)}, bf16[320,1536]{1,0:T(8,128)(2,1)S(1)}, u32[]{:S(2)}, u32[]{:S(2)}) %collective-permute-start.30) | collective-permute-done | bytes 983072 | tf_op jit(solution)/shard_map/normed_gather/ppermute | solution.py:116
  207.7 9.2 %collective-permute-done.36 = bf16[160,1536]{1,0:T(8,128)(2,1)S(1)} collective-permute-done((bf16[160,1536]{1,0:T(8,128)(2,1)S(1)}, bf16[160,1536]{1,0:T(8,128)(2,1)S(1)}, u32[]{:S(2)}, u32[]{:S(2)}) %collective-permute-start.36) | collective-permute-done | bytes 491552 | tf_op jit(solution)/shard_map/cot_gather/ppermute | solution.py:116
  217.0 6.7 %collective-permute-done.32 = bf16[160,1536]{1,0:T(8,128)(2,1)S(1)} collective-permute-done((bf16[160,1536]{1,0:T(8,128)(2,1)S(1)}, bf16[160,1536]{1,0:T(8,128)(2,1)S(1)}, u32[]{:S(2)}, u32[]{:S(2)}) %collective-permute-start.32) | collective-permute-done | bytes 491552 | tf_op jit(solution)/shard_map/normed_gather/ppermute | solution.py:116
  224.7 68.5 %shard_map.355 = (f32[1280,1536]{1,0:T(8,128)}, f32[1280,1536]{1,0:T(8,128)}, bf16[4608,1536]{1,0:T(8,128)(2,1)}) custom-call(bf16[320,1536]{1,0:T(8,128)(2,1)} %get-tuple-element.157.refs_0_, bf16[320,1536]{1,0:T(8,128)(2,1)} %copy-done.42, bf16[320,1536]{1,0:T(8,128)(2,1)} %copy-done.43, bf16[320,1536]{1,0:T(8,128)(2,1)} %copy-done.45, ...), custom_call_target="tpu_custom_call" | custom-call | flops 78199996416 | bytes 51904512 | tf_op jit(solution)/shard_map/pallas_call | solution.py:808
  293.3 37.2 %shard_map.356 = (bf16[320,1536]{1,0:T(8,128)(2,1)}, bf16[320,1536]{1,0:T(8,128)(2,1)}, bf16[320,1536]{1,0:T(8,128)(2,1)}, bf16[320,1536]{1,0:T(8,128)(2,1)}, bf...) custom-call(bf16[320,1536]{1,0:T(8,128)(2,1)} %get-tuple-element.157, ...), custom_call_target="tpu_custom_call" | custom-call | flops 40249999360 | bytes 43548672 | tf_op jit(solution)/shard_map/pallas_call | solution.py:808
  334.0 16.2 %shard_map.357 = bf16[2176,1536]{1,0:T(8,128)(2,1)} custom-call(bf16[320,1536]{1,0:T(8,128)(2,1)} %get-tuple-element.157.refs_0_, bf16[320,1536]{1,0:T(8,128)(2,1)} %copy-done.42, bf16[320,1536]{1,0:T(8,128)(2,1)} %copy-done.43, bf16[320,1536]{1,0:T(8,128)(2,1)} %copy-done.45, bf16[320,1536]{1,0:T(8,128)(2,1)} %copy-done.32, bf16[320,1536]{1,0:T(8,128)(2,1)} %copy-done.40, ...), custom_call_target="tpu_custom_call" | custom-call | flops 18400000000 | bytes 19955712 | tf_op jit(solution)/shard_map/pallas_call | solution.py:808
  355.5 18.5 %collective-permute-done.40.refs_9_ = bf16[320,1536]{1,0:T(8,128)(2,1)} collective-permute-done((bf16[320,1536]{1,0:T(8,128)(2,1)}, bf16[320,1536]{1,0:T(8,128)(2,1)}, u32[]{:S(2)}, u32[]{:S(2)}) %collective-permute-start.40) | collective-permute-done | bytes 983072 | tf_op jit(solution)/shard_map/back_reduce/ppermute | solution.py:116
  375.2 31.5 %shard_map.358 = (f32[320,1536]{1,0:T(8,128)}, bf16[320,1536]{1,0:T(8,128)(2,1)}, f32[1,1536]{1,0:T(1,128)}, f32[320,1536]{1,0:T(8,128)}, bf16[320,512]{1,0:T(8,...) custom-call(s32[3]{0:T(128)} %pad_add_fusion.refs_0_, ...), custom_call_target="tpu_custom_call" | custom-call | flops 35649998848 | bytes 20152332 | tf_op jit(solution)/shard_map/pallas_call | solution.py:489
  410.3 7.1 %shard_map.359 = (bf16[4,768,384]{2,1,0:T(8,128)(2,1)}, bf16[4,768,384]{2,1,0:T(8,128)(2,1)}) custom-call(s32[3]{0:T(128)} %pad_add_fusion.refs_0_, bf16[320,1536]{1,0:T(8,128)(2,1)} %get-tuple-element.193.refs_1_, bf16[320,1536]{1,0:T(8,128)(2,1)} %get-tuple-element.194.refs_2_), custom_call_target="tpu_custom_call" | custom-call | tf_op jit(solution)/shard_map/pallas_call | solution.py:489
  423.9 8.7 %shard_map.361 = (bf16[4,1024,384]{2,1,0:T(8,128)(2,1)}, bf16[4,1024,384]{2,1,0:T(8,128)(2,1)}) custom-call(s32[3]{0:T(128)} %pad_add_fusion.refs_0_, bf16[320,1536]{1,0:T(8,128)(2,1)} %get-tuple-element.203.refs_1_, bf16[320,2048]{1,0:T(8,128)(2,1)} %get-tuple-element.212.refs_2_.refs_1_), custom_call_target="tpu_custom_call" | custom-call | tf_op jit(solution)/shard_map/pallas_call | solution.py:489
  449.3 9.0 %shard_map.362 = (bf16[320,1536]{1,0:T(8,128)(2,1)}, f32[1,1536]{1,0:T(1,128)}) custom-call(s32[3]{0:T(128)} %pad_add_fusion.refs_0_, bf16[320,2048]{1,0:T(8,128)(2,1)} %get-tuple-element.212.refs_2_.refs_1_, bf16[320,1536]{1,0:T(8,128)(2,1)} %bitcast.202, f32[1,1536]{1,0:T(1,128)} %broadcast_in_dim_reshape.7.refs_2_.refs_3_, ...), custom_call_target="tpu_custom_call" | custom-call | tf_op jit(solution)/shard_map/pallas_call | solution.py:489
  489.6 10.6 %collective-permute-done.55 = bf16[192,384]{1,0:T(8,128)(2,1)S(1)} collective-permute-done((bf16[192,384]{1,0:T(8,128)(2,1)S(1)}, bf16[192,384]{1,0:T(8,128)(2,1)S(1)}, u32[]{:S(2)}, u32[]{:S(2)}) %collective-permute-start.55) | collective-permute-done | bytes 147488 | tf_op jit(solution)/shard_map/out_line/ppermute | solution.py:153
  501.4 10.0 %collective-permute-done.57 = bf16[192,384]{1,0:T(8,128)(2,1)S(1)} collective-permute-done((bf16[192,384]{1,0:T(8,128)(2,1)S(1)}, bf16[192,384]{1,0:T(8,128)(2,1)S(1)}, u32[]{:S(2)}, u32[]{:S(2)}) %collective-permute-start.57) | collective-permute-done | bytes 147488 | tf_op jit(solution)/shard_map/out_line/ppermute | solution.py:153
  511.4 9.3 %collective-permute-done.53 = bf16[1088,384]{1,0:T(8,128)(2,1)S(1)} collective-permute-done((bf16[1088,384]{1,0:T(8,128)(2,1)S(1)}, bf16[1088,384]{1,0:T(8,128)(2,1)S(1)}, u32[]{:S(2)}, u32[]{:S(2)}) %collective-permute-start.53) | collective-permute-done | bytes 835616 | tf_op jit(solution)/shard_map/qkv_dp/ppermute | solution.py:116
  532.3 7.8 %collective-permute-done.59 = bf16[272,384]{1,0:T(8,128)(2,1)} collective-permute-done((bf16[272,384]{1,0:T(8,128)(2,1)}, bf16[272,384]{1,0:T(8,128)(2,1)}, u32[]{:S(2)}, u32[]{:S(2)}) %collective-permute-start.59) | collective-permute-done | bytes 208928 | tf_op jit(solution)/shard_map/qkv_line/ppermute | solution.py:153
  614.9 7.9 %fusion.49 = (bf16[384,2240]{0,1:T(8,128)(2,1)}, f32[384,2240]{0,1:T(8,128)}, f32[384,2240]{0,1:T(8,128)}, f32[384,2240]{0,1:T(8,128)}) fusion(f32[384,2240]{0,1:T(8,128)S(1)} %copy-done.1, f32[]{:T(128)S(6)} %div.70, bf16[384,2240]{0,1:T(8,128)(2,1)} %bitcast.168, f32[384,2240]{0,1:T(8,128)} %param.28, f32[384,2240]{0,1:T(8,128)} %param.29), kind=kLoop, calls=%fused_computation.200 | loop fusion | flops 14622720 | bytes 24084484 | tf_op jit(solution)/shard_map/convert_element_type | solution.py:111
  626.7 6.8 %collective-permute-done.70 = bf16[320,1536]{1,0:T(8,128)(2,1)S(1)} collective-permute-done((bf16[320,1536]{1,0:T(8,128)(2,1)}, bf16[320,1536]{1,0:T(8,128)(2,1)S(1)}, u32[]{:S(2)}, u32[]{:S(2)}) %collective-permute-start.70) | collective-permute-done | bytes 983072 | tf_op jit(solution)/shard_map/mixed_reduce/ppermute | solution.py:116
  (431 shorter events, 260.0 us)
Async XLA Ops:
  7.2 216.6 %all-gather.5.cloned.1.call-start = ((), (), s32[]{:S(2)}) async-start(), calls=%async_computation.3 | async-start | bytes 15925248 | tf_op jit(solution)/shard_map/all_gather | solution.py:961
  13.3 30.1 %collective-permute-start.1 = (bf16[448,384]{0,1:T(8,128)(2,1)}, bf16[448,384]{0,1:T(8,128)(2,1)}, u32[]{:S(2)}, u32[]{:S(2)}) collective-permute-start(bf16[448,384]{0,1:T(8,128)(2,1)} %get-tuple-element.414), channel_id=1, source_target_pairs={{0,4},{1,5},{2,6},{3,7},{4,0},{5,1},{6,2},{7,3},{8,12},{9,13},{10,... | collective-permute-start | bytes 1032200 | tf_op jit(solution)/shard_map/matrix_line/ppermute | solution.py:153
  27.2 32.4 %collective-permute-start.11 = (bf16[560,576]{1,0:T(8,128)(2,1)}, bf16[560,576]{1,0:T(8,128)(2,1)}, u32[]{:S(2)}, u32[]{:S(2)}) collective-permute-start(bf16[560,576]{1,0:T(8,128)(2,1)} %get-tuple-element.383), channel_id=1, source_target_pairs={{0,16},{8,24},{16,0},{24,8},{1,17},{9,25},{17,1},{25,9},{2,18},{10... | collective-permute-start | bytes 1935368 | tf_op jit(solution)/shard_map/weights_exchange/ppermute | solution.py:116
  30.4 29.1 %collective-permute-start.12 = (bf16[560,576]{1,0:T(8,128)(2,1)}, bf16[560,576]{1,0:T(8,128)(2,1)}, u32[]{:S(2)}, u32[]{:S(2)}) collective-permute-start(bf16[560,576]{1,0:T(8,128)(2,1)} %get-tuple-element.384), channel_id=1, source_target_pairs={{0,24},{8,16},{16,8},{24,0},{1,25},{9,17},{17,9},{25,1},{2,26},{10... | collective-permute-start | bytes 1935368 | tf_op jit(solution)/shard_map/weights_exchange/ppermute | solution.py:116
  69.3 224.0 %all-gather.3.cloned.1.call-start = ((), (), s32[]{:S(2)}) async-start(), calls=%async_computation.2 | async-start | bytes 7520256 | tf_op jit(solution)/shard_map/all_gather | solution.py:961
  150.1 287.5 %reduce-scatter.3.cloned.1.call-start = ((), (), s32[]{:S(2)}) async-start(), calls=%async_computation.4 | async-start | bytes 15925248 | tf_op jit(solution)/shard_map/reduce_scatter | solution.py:1015
  154.6 28.1 %collective-permute-start.34 = (bf16[320,1536]{1,0:T(8,128)(2,1)S(1)}, bf16[320,1536]{1,0:T(8,128)(2,1)S(1)}, u32[]{:S(2)}, u32[]{:S(2)}) collective-permute-start(bf16[320,1536]{1,0:T(8,128)(2,1)S(1)} %bitcast_select_fusion.refs_4_.refs_2_), channel_id=1, source_target_pairs={{0,8},{8,0},{16,24},{24,16},{1,9},{9,1},{17,25},{25,17},{2,10},{10... | collective-permute-start | bytes 2949128 | tf_op jit(solution)/shard_map/cot_gather/ppermute | solution.py:116
  155.2 28.4 %collective-permute-start.35 = (bf16[320,1536]{1,0:T(8,128)(2,1)S(1)}, bf16[320,1536]{1,0:T(8,128)(2,1)S(1)}, u32[]{:S(2)}, u32[]{:S(2)}) collective-permute-start(bf16[320,1536]{1,0:T(8,128)(2,1)S(1)} %bitcast_select_fusion.refs_4_.refs_2_), channel_id=1, source_target_pairs={{0,16},{8,24},{16,0},{24,8},{1,17},{9,25},{17,1},{25,9},{2,18},{10... | collective-permute-start | bytes 2949128 | tf_op jit(solution)/shard_map/cot_gather/ppermute | solution.py:116
  182.7 34.2 %collective-permute-start.36 = (bf16[160,1536]{1,0:T(8,128)(2,1)S(1)}, bf16[160,1536]{1,0:T(8,128)(2,1)S(1)}, u32[]{:S(2)}, u32[]{:S(2)}) collective-permute-start(bf16[160,1536]{1,0:T(8,128)(2,1)S(1)} %slice.247), channel_id=1, source_target_pairs={{0,16},{8,24},{16,0},{24,8},{1,17},{9,25},{17,1},{25,9},{2,18},{10... | collective-permute-start | bytes 1474568 | tf_op jit(solution)/shard_map/cot_gather/ppermute | solution.py:116
  183.6 33.3 %collective-permute-start.37 = (bf16[160,1536]{1,0:T(8,128)(2,1)S(1)}, bf16[160,1536]{1,0:T(8,128)(2,1)S(1)}, u32[]{:S(2)}, u32[]{:S(2)}) collective-permute-start(bf16[160,1536]{1,0:T(8,128)(2,1)S(1)} %slice.248), channel_id=1, source_target_pairs={{0,8},{8,0},{16,24},{24,16},{1,9},{9,1},{17,25},{25,17},{2,10},{10... | collective-permute-start | bytes 1474568 | tf_op jit(solution)/shard_map/cot_gather/ppermute | solution.py:116
  293.2 235.8 %reduce-scatter.5.cloned.1.call-start = ((), (), s32[]{:S(2)}) async-start(), calls=%async_computation.5 | async-start | bytes 7520256 | tf_op jit(solution)/shard_map/reduce_scatter | solution.py:1091
  332.2 41.8 %collective-permute-start.40 = (bf16[320,1536]{1,0:T(8,128)(2,1)}, bf16[320,1536]{1,0:T(8,128)(2,1)}, u32[]{:S(2)}, u32[]{:S(2)}) collective-permute-start(bf16[320,1536]{1,0:T(8,128)(2,1)} %get-tuple-element.168), channel_id=1, source_target_pairs={{0,24},{8,16},{16,8},{24,0},{1,25},{9,17},{17,9},{25,1},{2,26},{10... | collective-permute-start | bytes 2949128 | tf_op jit(solution)/shard_map/back_reduce/ppermute | solution.py:116
  374.1 32.7 %collective-permute-start.41 = (bf16[320,1536]{1,0:T(8,128)(2,1)S(1)}, bf16[320,1536]{1,0:T(8,128)(2,1)S(1)}, u32[]{:S(2)}, u32[]{:S(2)}) collective-permute-start(bf16[320,1536]{1,0:T(8,128)(2,1)S(1)} %copy-done.55), channel_id=1, source_target_pairs={{0,8},{8,0},{16,24},{24,16},{1,9},{9,1},{17,25},{25,17},{2,10},{10... | collective-permute-start | bytes 2949128 | tf_op jit(solution)/shard_map/mixed_reduce/ppermute | solution.py:116
  374.7 32.0 %collective-permute-start.42 = (bf16[320,1536]{1,0:T(8,128)(2,1)S(1)}, bf16[320,1536]{1,0:T(8,128)(2,1)S(1)}, u32[]{:S(2)}, u32[]{:S(2)}) collective-permute-start(bf16[320,1536]{1,0:T(8,128)(2,1)S(1)} %copy-done.54), channel_id=1, source_target_pairs={{0,16},{8,24},{16,0},{24,8},{1,17},{9,25},{17,1},{25,9},{2,18},{10... | collective-permute-start | bytes 2949128 | tf_op jit(solution)/shard_map/mixed_reduce/ppermute | solution.py:116
  437.6 35.5 %collective-permute-start.47 = (bf16[4,1024,384]{2,1,0:T(8,128)(2,1)}, bf16[4,1024,384]{2,1,0:T(8,128)(2,1)S(1)}, u32[]{:S(2)}, u32[]{:S(2)}) collective-permute-start(bf16[4,1024,384]{2,1,0:T(8,128)(2,1)} %get-tuple-element.209), channel_id=1, source_target_pairs={{0,1},{1,0},{2,3},{3,2},{4,5},{5,4},{6,7},{7,6},{8,9},{9,8},{10,11... | collective-permute-start | bytes 9437192 | tf_op jit(solution)/shard_map/qkv_core/ppermute | solution.py:121
  443.4 29.7 %collective-permute-start.48 = (bf16[768,384]{1,0:T(8,128)(2,1)}, bf16[768,384]{1,0:T(8,128)(2,1)}, u32[]{:S(2)}, u32[]{:S(2)}) collective-permute-start(bf16[768,384]{1,0:T(8,128)(2,1)} %get-tuple-element.375), channel_id=1, source_target_pairs={{0,8},{8,0},{16,24},{24,16},{1,9},{9,1},{17,25},{25,17},{2,10},{10... | collective-permute-start | bytes 1769480 | tf_op jit(solution)/shard_map/out_dp/ppermute | solution.py:116
  444.8 28.3 %collective-permute-start.49 = (bf16[768,384]{1,0:T(8,128)(2,1)}, bf16[768,384]{1,0:T(8,128)(2,1)}, u32[]{:S(2)}, u32[]{:S(2)}) collective-permute-start(bf16[768,384]{1,0:T(8,128)(2,1)} %get-tuple-element.374), channel_id=1, source_target_pairs={{0,16},{8,24},{16,0},{24,8},{1,17},{9,25},{17,1},{25,9},{2,18},{10... | collective-permute-start | bytes 1769480 | tf_op jit(solution)/shard_map/out_dp/ppermute | solution.py:116
  480.8 30.6 %collective-permute-start.54 = (bf16[1088,384]{1,0:T(8,128)(2,1)S(1)}, bf16[1088,384]{1,0:T(8,128)(2,1)S(1)}, u32[]{:S(2)}, u32[]{:S(2)}) collective-permute-start(bf16[1088,384]{1,0:T(8,128)(2,1)S(1)} %bitcast.203), channel_id=1, source_target_pairs={{0,24},{8,16},{16,8},{24,0},{1,25},{9,17},{17,9},{25,1},{2,26},{10... | collective-permute-start | bytes 2506760 | tf_op jit(solution)/shard_map/qkv_dp/ppermute | solution.py:116
  483.3 37.4 %collective-permute-start.53 = (bf16[1088,384]{1,0:T(8,128)(2,1)S(1)}, bf16[1088,384]{1,0:T(8,128)(2,1)S(1)}, u32[]{:S(2)}, u32[]{:S(2)}) collective-permute-start(bf16[1088,384]{1,0:T(8,128)(2,1)S(1)} %bitcast.204), channel_id=1, source_target_pairs={{0,16},{8,24},{16,0},{24,8},{1,17},{9,25},{17,1},{25,9},{2,18},{10... | collective-permute-start | bytes 2506760 | tf_op jit(solution)/shard_map/qkv_dp/ppermute | solution.py:116
  484.0 36.7 %collective-permute-start.52 = (bf16[1088,384]{1,0:T(8,128)(2,1)S(1)}, bf16[1088,384]{1,0:T(8,128)(2,1)S(1)}, u32[]{:S(2)}, u32[]{:S(2)}) collective-permute-start(bf16[1088,384]{1,0:T(8,128)(2,1)S(1)} %bitcast.205), channel_id=1, source_target_pairs={{0,8},{8,0},{16,24},{24,16},{1,9},{9,1},{17,25},{25,17},{2,10},{10... | collective-permute-start | bytes 2506760 | tf_op jit(solution)/shard_map/qkv_dp/ppermute | solution.py:116
  554.9 44.2 %collective-permute-start.64 = (bf16[384,576]{0,1:T(8,128)(2,1)}, bf16[384,576]{0,1:T(8,128)(2,1)}, u32[]{:S(2)}, u32[]{:S(2)}) collective-permute-start(bf16[384,576]{0,1:T(8,128)(2,1)} %get-tuple-element.392), channel_id=1, source_target_pairs={{0,8},{8,0},{16,24},{24,16},{1,9},{9,1},{17,25},{25,17},{2,10},{10... | collective-permute-start | bytes 1327112 | tf_op jit(solution)/shard_map/gradient_exchange/ppermute | solution.py:116
  556.0 43.2 %collective-permute-start.65 = (bf16[384,576]{0,1:T(8,128)(2,1)}, bf16[384,576]{0,1:T(8,128)(2,1)}, u32[]{:S(2)}, u32[]{:S(2)}) collective-permute-start(bf16[384,576]{0,1:T(8,128)(2,1)} %get-tuple-element.391), channel_id=1, source_target_pairs={{0,16},{8,24},{16,0},{24,8},{1,17},{9,25},{17,1},{25,9},{2,18},{10... | collective-permute-start | bytes 1327112 | tf_op jit(solution)/shard_map/gradient_exchange/ppermute | solution.py:116
  562.2 31.3 %collective-permute-start.67 = (bf16[176,576]{1,0:T(8,128)(2,1)}, bf16[176,576]{1,0:T(8,128)(2,1)}, u32[]{:S(2)}, u32[]{:S(2)}) collective-permute-start(bf16[176,576]{1,0:T(8,128)(2,1)} %bitcast.92), channel_id=1, source_target_pairs={{0,8},{8,0},{16,24},{24,16},{1,9},{9,1},{17,25},{25,17},{2,10},{10... | collective-permute-start | bytes 608264 | tf_op jit(solution)/shard_map/gradient_exchange/ppermute | solution.py:116
  565.3 30.9 %collective-permute-start.68 = (bf16[176,576]{1,0:T(8,128)(2,1)}, bf16[176,576]{1,0:T(8,128)(2,1)}, u32[]{:S(2)}, u32[]{:S(2)}) collective-permute-start(bf16[176,576]{1,0:T(8,128)(2,1)} %bitcast.94), channel_id=1, source_target_pairs={{0,16},{8,24},{16,0},{24,8},{1,17},{9,25},{17,1},{25,9},{2,18},{10... | collective-permute-start | bytes 608264 | tf_op jit(solution)/shard_map/gradient_exchange/ppermute | solution.py:116
  (117 other events, 1351.1 us)
Sparse Core Ops, SparseCore 0:
  69.4 129.8 all-gather.4
  201.5 66.2 all-gather.2
  293.4 144.1 reduce-scatter.2
  439.8 81.3 reduce-scatter.4

commit v4 on v3

--- a/solution.py
+++ b/solution.py
@@ -226,17 +226,6 @@
     yield in_piece, down_piece.reshape(width, ranks * slices, part)
 
 
-def pack_gradients(in_grad, down_grad):
-    ranks = lax.axis_size("dp")
-    part = in_grad.shape[0]
-    columns = down_grad.shape[0]
-    rows = in_grad.shape[1] // ranks
-    slices = down_grad.shape[1] // ranks
-    in_sent = in_grad.reshape(part, ranks, rows).transpose(1, 0, 2)
-    down_sent = down_grad.reshape(columns, ranks, slices, part).transpose(1, 3, 2, 0)
-    return jnp.concatenate([in_sent, down_sent.reshape(ranks, part, slices * columns)], axis=2)
-
-
 def unpack_gradients(got, rows, columns):
     ranks, part, width = got.shape
     return got[:, :, :rows], got[:, :, rows:].reshape(ranks, part, -1, columns)
@@ -316,7 +305,7 @@
         values[pl.ds(k * rows, rows), :] = kv[k][:, pl.ds(KV_WIDTH, KV_WIDTH)]
     values_t[...] = values[...].T
 
-    @pl.loop(0, HEADS)
+    @pl.loop(0, HEADS, unroll=2)
     def _(h):
         cols = pl.ds(pl.multiple_of(h * HEAD, HEAD), HEAD)
         kv_cols = pl.ds(pl.multiple_of((h // GROUP) * HEAD, HEAD), HEAD)
@@ -392,7 +381,7 @@
     key_sum[...] = jnp.zeros_like(key_sum)
     value_sum[...] = jnp.zeros_like(value_sum)
 
-    @pl.loop(0, HEADS)
+    @pl.loop(0, HEADS, unroll=2)
     def _(h):
         cols = pl.ds(pl.multiple_of(h * HEAD, HEAD), HEAD)
         kv_cols = pl.ds(pl.multiple_of((h // GROUP) * HEAD, HEAD), HEAD)
@@ -479,6 +468,40 @@
     scaled = cot * gain[...]
     back = scale * (scaled - n * jnp.mean(scaled * n, axis=-1, keepdims=True))
     input_grad[...] = bf16(middle_cot[...] + back)
+
+
+def finish_kernel(info, *refs):
+    *terms, grad, small, squares = refs
+    total = terms[0][...].astype(jnp.float32)
+    for term in terms[1:]:
+        total = total + term[...].astype(jnp.float32)
+    columns = grad.shape[1]
+    grad[...] = total[:columns].T
+    small[...] = total[columns : columns + 1]
+    squares[...] = jnp.sum(total * total, keepdims=True)
+
+
+def pack_kernel(chunk, ranks, info, shard, *refs):
+    outs = refs[:ranks]
+    squares, turned = refs[ranks:]
+    place = info[0]
+    block = D // ranks
+    each = chunk.slices // ranks
+    rows = shard[pl.ds(0, chunk.real), :].astype(jnp.float32)
+    total = jnp.sum(rows * rows, keepdims=True)
+    low = shard[pl.ds(chunk.deep, chunk.low), :].astype(jnp.float32)
+    for s in range(chunk.slices):
+        for i in range(chunk.folds):
+            start = i * chunk.wide + s * chunk.deep
+            part = low[:, start : start + chunk.real]
+            total = total + jnp.sum(part * part, keepdims=True)
+            at = (s % each) * chunk.columns + i * chunk.low
+            turned[s // each, :, pl.ds(at, chunk.low)] = part.T
+    squares[...] = total
+    for k in range(ranks):
+        cols = pl.ds(pl.multiple_of((place ^ k) * block, 128), block)
+        outs[k][:, pl.ds(0, block)] = shard[pl.ds(0, chunk.real), cols]
+        outs[k][:, pl.ds(block, each * chunk.columns)] = bf16(turned[place ^ k])
 
 
 def call(kernel, args, outs, scratch, micros):
@@ -723,7 +746,7 @@
     wait_all(outs + stored)
 
 
-def last_chunk_kernel(chunk, ranks, carried, *refs):
+def last_chunk_kernel(chunk, ranks, carried, start, *refs):
     na_in = refs[:ranks]
     oc_in = refs[ranks : 2 * ranks]
     weights = refs[2 * ranks]
@@ -740,8 +763,9 @@
     copies = Copies(in_sem)
     first, block_copies = load_chunk(chunk, ranks, na_in, oc_in, weights, na, oc, w, d, copies)
     if carried:
-        first.append(copies.start(back_in, back))
-        first.append(copies.start(mixed_in, mixed))
+        at = pl.ds(start * rows, tokens)
+        first.append(copies.start(back_in.at[at], back))
+        first.append(copies.start(mixed_in.at[at], mixed))
     wait_all(first)
     copies = Copies(out_sem)
     outs = []
@@ -778,13 +802,16 @@
 def gradient_kernel(chunk, ranks, *refs):
     na_in = refs[:ranks]
     oc_in = refs[ranks : 2 * ranks]
-    kept_in = refs[2 * ranks : 2 * ranks + 3]
-    weights_out, na, oc, oc_t, gt, ut, ht, dw, dd, in_sem, out_sem = refs[2 * ranks + 3 :]
+    kept_in = refs[2 * ranks : 2 * ranks + 6]
+    weights_out, na, oc, oc_t, gt, ut, ht, dw, dd, in_sem, out_sem = refs[2 * ranks + 6 :]
     tokens = na.shape[0]
     copies = Copies(in_sem)
     first = load_tokens(oc_in, oc, copies)
     later = load_tokens(na_in, na, copies)
-    later += [copies.start(source, kept) for source, kept in zip(kept_in, (gt, ut, ht))]
+    half = tokens // 2
+    for i, source in enumerate(kept_in):
+        kept = (gt, ut, ht)[i % 3].at[:, pl.ds(i // 3 * half, half)]
+        later.append(copies.start(source, kept))
     wait_all(first)
     transpose_tokens(oc, oc_t, tokens)
     if chunk.wide > chunk.units:
@@ -850,7 +877,7 @@
     return hbm_call(kernel, [*na, *oc, weights, *carry], outs, scratch, 68)
 
 
-def last_chunk(chunk, na, oc, weights, carry):
+def last_chunk(chunk, na, oc, weights, carry, start):
     ranks = len(na)
     rows = na[0].shape[0]
     tokens = ranks * rows
@@ -868,9 +895,9 @@
         pltpu.SemaphoreType.DMA((2 * ranks + 3 * len(chunk.blocks),)),
     ]
     outs = [bf16_like(rows, D)] * (2 * ranks) + [bf16_like(chunk.units, tokens)] * 3
-    kernel = functools.partial(last_chunk_kernel, chunk, ranks, bool(carry))
+    kernel = functools.partial(last_chunk_kernel, chunk, ranks, bool(carry), start)
     got = hbm_call(
-        kernel, [*na, *oc, weights, *carry], outs, scratch, 35
+        kernel, [*na, *oc, weights, *carry], outs, scratch, 20
     )
     return got[:ranks], got[ranks : 2 * ranks], got[2 * ranks :]
 
@@ -887,7 +914,7 @@
         vmem_bf16(chunk.units, tokens),
         vmem_bf16(2 * chunk.units, D),
         vmem_bf16(D, chunk.wide),
-        pltpu.SemaphoreType.DMA((2 * ranks + 3,)),
+        pltpu.SemaphoreType.DMA((2 * ranks + 6,)),
         pltpu.SemaphoreType.DMA((copy_count(chunk),)),
     ]
     kernel = functools.partial(gradient_kernel, chunk, ranks)
@@ -1003,10 +1030,19 @@
         carry = (back, mixed)
         terms.append(term)
     chunk, weights = end
-    back_blocks, mixed_blocks, kept = last_chunk(
-        chunk, normed_blocks, cot_blocks, weights, carry
-    )
-    back_got = [scoped("back_reduce", dp_send, back_blocks[k], k) for k in range(1, ranks)]
+    half = ranks // 2
+    far_back, far_mixed, far_kept = last_chunk(
+        chunk, normed_blocks[half:], cot_blocks[half:], weights, carry, half
+    )
+    far_got = [scoped("back_reduce", dp_send, far_back[k - half], k) for k in range(half, ranks)]
+    near_cot, far_back = lax.optimization_barrier((cot_blocks[:half], far_back))
+    near_back, near_mixed, near_kept = last_chunk(
+        chunk, normed_blocks[:half], near_cot, weights, carry, 0
+    )
+    back_got = [scoped("back_reduce", dp_send, near_back[k], k) for k in range(1, half)] + far_got
+    back_blocks = near_back
+    mixed_blocks = [*near_mixed, *far_mixed]
+    kept = [*near_kept, *far_kept]
     term = chunk_gradients(chunk, normed_blocks, cot_blocks, kept)
     term, back_blocks, back_got, mixed_blocks = lax.optimization_barrier(
         (term, back_blocks, back_got, mixed_blocks)
@@ -1015,11 +1051,29 @@
     first_shard = lax.psum_scatter(terms[0], "fsdp", scatter_dimension=0, tiled=True)
 
     def pack_chunk(chunk, shard):
-        return scoped("gradient_exchange", pack_gradients, *chunk.unpack(shard))
+        width = block + D // ranks // 2
+        *sent, squares = call(
+            functools.partial(pack_kernel, chunk, ranks),
+            [info, shard],
+            [bf16_like(chunk.real, width)] * ranks + [f32_like(1, 1)],
+            [vmem_f32(ranks, chunk.real, width - block)],
+            0,
+        )
+        return sent, squares[0, 0]
 
     def exchange_chunk(sent):
-        got = scoped("gradient_exchange", dp_exchange, sent)
-        return unpack_gradients(got, half_in.shape[0], half_down.shape[1])
+        got = sent[:1] + [scoped("gradient_exchange", dp_send, sent[k], k) for k in range(1, ranks)]
+        return got
+
+    def place_chunk(got):
+        stacked = jnp.stack(got)
+        ordered = jnp.stack(
+            [
+                lax.dynamic_index_in_dim(stacked, place ^ a, 0, keepdims=False)
+                for a in range(ranks)
+            ]
+        )
+        return unpack_gradients(ordered, half_in.shape[0], half_down.shape[1])
 
     mixed_got = [scoped("mixed_reduce", dp_send, mixed_blocks[k], k) for k in range(1, ranks - 1)]
     middle_cot, middle_low, gain_mlp_grad, query_cot, *kv_cot = call(
@@ -1079,16 +1133,15 @@
         [],
         0,
     )
-    projected_low, out_swapped = lax.optimization_barrier((projected_low, out_swapped))
-    out_got = scoped("out_dp", reduce_over_dp, sum_blocks(out_own_term, out_swapped))
+    out_sums = sum_blocks(out_own_term, out_swapped)
+    out_sums = [out_sums[0]] + [bf16(total) for total in out_sums[1:]]
+    projected_low, out_sums = lax.optimization_barrier((projected_low, out_sums))
+    out_got = scoped("out_dp", reduce_over_dp, out_sums)
     qkv_own_term, qkv_other_term = outer(normed, projected_low)
 
-    projected_low, qkv_own_term, qkv_other_term, first_shard, last_term = (
-        lax.optimization_barrier(
-            (projected_low, qkv_own_term, qkv_other_term, first_shard, terms[1])
-        )
-    )
-    last_shard = lax.psum_scatter(last_term, "fsdp", scatter_dimension=0, tiled=True)
+    qkv_own_term, qkv_other_term, projected_low = lax.optimization_barrier(
+        (qkv_own_term, qkv_other_term, projected_low)
+    )
     qkv_swapped = scoped("qkv_core", core_swap, qkv_other_term)
     input_grad, gain_attn_grad = call(
         functools.partial(input_back_kernel, ranks, slices),
@@ -1098,6 +1151,10 @@
         0,
     )
 
+    gain_attn_grad, first_shard, last_term, out_got[1:3] = lax.optimization_barrier(
+        (gain_attn_grad, first_shard, terms[1], out_got[1:3])
+    )
+    last_shard = lax.psum_scatter(last_term, "fsdp", scatter_dimension=0, tiled=True)
     small_term = group_small(gain_attn_grad[0], gain_mlp_grad[0], bias_grad[0])
     small_term = small_term.reshape(ranks, small_rows, slices, 2, small_columns)
     small_term = small_term.transpose(3, 0, 2, 1, 4).reshape(2, ranks, slices, -1)
@@ -1117,39 +1174,44 @@
         qkv_sums.append(total.reshape(-1, block))
     qkv_got = scoped("qkv_dp", reduce_over_dp, qkv_sums)
     out_shard = scoped("out_line", reduce_over_line, out_got)
-    squares = sum_of_squares(first_shard)
-    first_sent = pack_chunk(chunks[0], first_shard)
+    first_sent, squares = pack_chunk(chunks[0], first_shard)
 
     qkv_got, out_shard, squares, first_sent = lax.optimization_barrier(
         (qkv_got, out_shard, squares, first_sent)
     )
     qkv_shard = scoped("qkv_line", reduce_over_line, qkv_got)
     out_grad = total_shard(out_shard)
-    squares = squares + sum_of_squares(out_grad) + sum_of_squares(last_shard)
-
-    qkv_shard, squares, last_shard, first_sent = lax.optimization_barrier(
-        (qkv_shard, squares, last_shard, first_sent)
-    )
-    qkv_shard = sum(part.astype(jnp.float32) for part in qkv_shard)
-    squares = squares + sum_of_squares(qkv_shard)
-    squares = scoped("norm_sum", sum_over_dp, squares)
-    first_sent, last_shard, squares = lax.optimization_barrier((first_sent, last_shard, squares))
-    total_squares = scoped("norm_sum", sum_over_line, scoped("norm_sum", sum_over_core, squares))
-    qkv_grad = lax.optimization_barrier(qkv_shard[:columns].T)
-    small_grad = qkv_shard[columns, : small_rows * small_columns]
+    squares = squares + sum_of_squares(out_grad)
+    first_got = exchange_chunk(first_sent)
+    mixed_last, first_got = lax.optimization_barrier((mixed_blocks[-1], first_got))
+    mixed_got.append(scoped("mixed_reduce", dp_send, mixed_last, ranks - 1))
+
+    qkv_shard, squares, last_shard, first_got = lax.optimization_barrier(
+        (qkv_shard, squares, last_shard, first_got)
+    )
+    last_sent, last_squares = pack_chunk(chunks[1], last_shard)
+    last_got = exchange_chunk(last_sent)
+    qkv_grad, small_row, qkv_squares = call(
+        finish_kernel,
+        [info, *qkv_shard],
+        [f32_like(block, columns), f32_like(1, block), f32_like(1, 1)],
+        [],
+        0,
+    )
+    squares = squares + last_squares + qkv_squares[0, 0]
+    squares, last_got[1], mixed_got = lax.optimization_barrier((squares, last_got[1], mixed_got))
+    total_squares = scoped("norm_sum", sum_everywhere, squares)
+    small_grad = small_row[0, : small_rows * small_columns]
     small_grad = small_grad.reshape(small_rows, small_columns)
-    in_first, down_first = exchange_chunk(first_sent)
-    in_last, down_last = exchange_chunk(pack_chunk(chunks[1], last_shard))
+    in_first, down_first = place_chunk(first_got)
+    in_last, down_last = place_chunk(last_got)
     in_grad = jnp.concatenate([in_first, in_last], axis=1)
     in_grad = in_grad.transpose(2, 0, 1).reshape(half_in.shape)
     down_grad = jnp.concatenate([down_first, down_last], axis=1)
     down_grad = down_grad.transpose(2, 0, 1, 3).reshape(half_down.shape)
-    in_grad, down_grad, mixed_last = lax.optimization_barrier(
-        (in_grad, down_grad, mixed_blocks[-1])
-    )
+    in_grad, down_grad = lax.optimization_barrier((in_grad, down_grad))
     in_grad = in_grad.astype(jnp.float32)
     down_grad = down_grad.astype(jnp.float32)
-    mixed_got.append(scoped("mixed_reduce", dp_send, mixed_last, ranks - 1))
     mixed = middle + mixed_blocks[0].astype(jnp.float32)
     for got in mixed_got:
         mixed = mixed + got.astype(jnp.float32)

time: 649 us -> 616 us (0.949)
  local copies, waits for them, and re-layouts: 66.4 us -> 37.1 us
  Pallas kernels: 213 us -> 223 us
    ppermute x15, waiting for transfers between devices: 46.6 us -> 36.9 us  [line_send(): return lax.ppermute(block, 'fsdp', [(i, i ^ 2 * r) for i in range(count)])]
    dynamic_slice x5 -> x1, local copies, waits for them, and re-layouts: 6.5 us -> 0.01 us  [dp_own(): lax.dynamic_index_in_dim(array, lax.axis_index('dp') ^ k, 0, keepdims=False)]
    pallas_call x7 -> x10, Pallas kernels: 91.7 us -> 97.6 us  [call(): pl.pallas_call(kernel, out_shape=tuple(outs), in_specs=[pl.BlockSpec(memo...]
    unnamed x130 -> x129, local copies, waits for them, and re-layouts: 17.4 us -> 12 us
    pallas_call x3 -> x4, Pallas kernels: 122 us -> 125 us  [hbm_call(): pl.pallas_call(kernel, out_shape=tuple(outs), in_specs=[anywhere] * len(a...]
  transfers between devices with their start and end apart: 79 -> 79, of which waited for: 35 -> 36; matrix products, arithmetic and copies ran while one was open for 15% -> 10% of each run, Pallas kernels for 33% -> 36%
where the time goes in v4:
time: 616 us; the launch traced here: 611 us
  Pallas kernels  223 us (36%)
  waiting for transfers between devices  175 us (28%)
  starting transfers between devices  90 us (15%)
  other arithmetic  62.3 us (10%)
  local copies, waits for them, and re-layouts  37.1 us (6%)
  between operations  24 us (4%)
    ppermute x50, waiting for transfers between devices, dp_send(): return lax.ppermute(block, 'dp', [(i, i ^ k) for i in range(count)])  130 us
    pallas_call x4, Pallas kernels, hbm_call(): pl.pallas_call(kernel, out_shape=tuple(outs), in_specs=[anywhere] * len(a...  125 us
    pallas_call x10, Pallas kernels, call(): pl.pallas_call(kernel, out_shape=tuple(outs), in_specs=[pl.BlockSpec(memo...  97.6 us
    ppermute x50, starting transfers between devices, dp_send(): return lax.ppermute(block, 'dp', [(i, i ^ k) for i in range(count)])  63.3 us
    ppermute x15, waiting for transfers between devices, line_send(): return lax.ppermute(block, 'fsdp', [(i, i ^ 2 * r) for i in range(count)])  36.9 us
    ppermute x15, starting transfers between devices, line_send(): return lax.ppermute(block, 'fsdp', [(i, i ^ 2 * r) for i in range(count)])  23.2 us
    convert_element_type x5, other arithmetic, update(): return (weight_new, first_new, second_new, weight_new.astype(jnp.bfloat16))  15.1 us
  transfers between devices with their start and end apart: 79, of which 36 were waited for; matrix products, arithmetic and copies ran while one was open for 10% of the time, Pallas kernels for 36%

profile of v4, /device:TPU:0, one launch (start us, length us, event | category | flops | bytes accessed | tf_op | source)
XLA Modules:
  0.0 610.7 jit_solution(17181874976743731715)
XLA Ops:
  33.1 10.4 %collective-permute-done.1 = bf16[448,384]{0,1:T(8,128)(2,1)} collective-permute-done((bf16[448,384]{0,1:T(8,128)(2,1)}, bf16[448,384]{0,1:T(8,128)(2,1)}, u32[]{:S(2)}, u32[]{:S(2)}) %collective-permute-start.1) | collective-permute-done | bytes 344096 | tf_op jit(solution)/shard_map/matrix_line/ppermute | solution.py:153
  47.0 12.6 %collective-permute-done.11 = bf16[560,576]{1,0:T(8,128)(2,1)} collective-permute-done((bf16[560,576]{1,0:T(8,128)(2,1)}, bf16[560,576]{1,0:T(8,128)(2,1)}, u32[]{:S(2)}, u32[]{:S(2)}) %collective-permute-start.11) | collective-permute-done | bytes 645152 | tf_op jit(solution)/shard_map/weights_exchange/ppermute | solution.py:116
  107.7 7.5 %shard_map.353 = (bf16[320,1536]{1,0:T(8,128)(2,1)}, bf16[320,1536]{1,0:T(8,128)(2,1)}, bf16[320,512]{1,0:T(8,128)(2,1)}) custom-call(s32[3]{0:T(128)} %pad_add_fusion.refs_0_.info, bf16[320,1536]{1,0:T(8,128)(2,1)} %bitcast.174, f32[1,1536]{1,0:T(1,128)} %broadcast_in_dim_reshape.7.refs_2_.refs_3_, f32[1,2048]{1,0:T(1,128)} %bitcast.187, ...), custom_call_target="tpu_custom_call" | custom-call | flops 8049999872 | bytes 9910284 | tf_op jit(solution)/shard_map/pallas_call | solution.py:512
  124.4 5.7 collective-permute-done.27
  138.7 7.5 %collective-permute-done.23.refs_5_.refs_11_ = bf16[320,512]{1,0:T(8,128)(2,1)S(1)} collective-permute-done((bf16[320,512]{1,0:T(8,128)(2,1)}, bf16[320,512]{1,0:T(8,128)(2,1)S(1)}, u32[]{:S(2)}, u32[]{:S(2)}) %collective-permute-start.23) | collective-permute-done | bytes 327712 | tf_op jit(solution)/shard_map/kv_gather/ppermute | solution.py:116
  156.3 21.2 %shard_map.354 = (bf16[320,1536]{1,0:T(8,128)(2,1)}, f32[16,320]{1,0:T(8,128)}, f32[320,1536]{1,0:T(8,128)}, bf16[320,1536]{1,0:T(8,128)(2,1)}) custom-call(s32[3]{0:T(128)} %pad_add_fusion.refs_0_.info, bf16[320,1536]{1,0:T(8,128)(2,1)} %bitcast.175, f32[1,1536]{1,0:T(1,128)} %broadcast_in_dim_reshape.6.refs_2_.refs_3_, ...), custom_call_target="tpu_custom_call" | custom-call | flops 27599998976 | bytes 11954188 | tf_op jit(solution)/shard_map/pallas_call | solution.py:512
  181.8 20.6 %collective-permute-done.30.refs_1_ = bf16[320,1536]{1,0:T(8,128)(2,1)S(1)} collective-permute-done((bf16[320,1536]{1,0:T(8,128)(2,1)}, bf16[320,1536]{1,0:T(8,128)(2,1)S(1)}, u32[]{:S(2)}, u32[]{:S(2)}) %collective-permute-start.30) | collective-permute-done | bytes 983072 | tf_op jit(solution)/shard_map/normed_gather/ppermute | solution.py:116
  204.9 9.1 %collective-permute-done.36 = bf16[160,1536]{1,0:T(8,128)(2,1)S(1)} collective-permute-done((bf16[160,1536]{1,0:T(8,128)(2,1)S(1)}, bf16[160,1536]{1,0:T(8,128)(2,1)S(1)}, u32[]{:S(2)}, u32[]{:S(2)}) %collective-permute-start.36) | collective-permute-done | bytes 491552 | tf_op jit(solution)/shard_map/cot_gather/ppermute | solution.py:116
  214.1 6.7 %collective-permute-done.32 = bf16[160,1536]{1,0:T(8,128)(2,1)S(1)} collective-permute-done((bf16[160,1536]{1,0:T(8,128)(2,1)S(1)}, bf16[160,1536]{1,0:T(8,128)(2,1)S(1)}, u32[]{:S(2)}, u32[]{:S(2)}) %collective-permute-start.32) | collective-permute-done | bytes 491552 | tf_op jit(solution)/shard_map/normed_gather/ppermute | solution.py:116
  221.8 68.2 %shard_map.355 = (f32[1280,1536]{1,0:T(8,128)}, f32[1280,1536]{1,0:T(8,128)}, bf16[4608,1536]{1,0:T(8,128)(2,1)}) custom-call(bf16[320,1536]{1,0:T(8,128)(2,1)} %get-tuple-element.193.refs_0_, bf16[320,1536]{1,0:T(8,128)(2,1)} %copy-done.39, bf16[320,1536]{1,0:T(8,128)(2,1)} %copy-done.40, bf16[320,1536]{1,0:T(8,128)(2,1)} %copy-done.42, ...), custom_call_target="tpu_custom_call" | custom-call | flops 78199996416 | bytes 51904512 | tf_op jit(solution)/shard_map/pallas_call | solution.py:835
  290.6 20.5 %shard_map.356 = (bf16[320,1536]{1,0:T(8,128)(2,1)}, bf16[320,1536]{1,0:T(8,128)(2,1)}, bf16[320,1536]{1,0:T(8,128)(2,1)}, bf16[320,1536]{1,0:T(8,128)(2,1)}, bf...) custom-call(bf16[320,1536]{1,0:T(8,128)(2,1)} %copy-done.40, ...), custom_call_target="tpu_custom_call" | custom-call | flops 23000000512 | bytes 32980992 | tf_op jit(solution)/shard_map/pallas_call | solution.py:835
  313.0 20.3 %shard_map.357 = (bf16[320,1536]{1,0:T(8,128)(2,1)}, bf16[320,1536]{1,0:T(8,128)(2,1)}, bf16[320,1536]{1,0:T(8,128)(2,1)}, bf16[320,1536]{1,0:T(8,128)(2,1)}, bf...) custom-call(bf16[320,1536]{1,0:T(8,128)(2,1)} %get-tuple-element.193.refs_0_, ...), custom_call_target="tpu_custom_call" | custom-call | flops 23000000512 | bytes 32980992 | tf_op jit(solution)/shard_map/pallas_call | solution.py:835
  335.0 16.0 %shard_map.358 = bf16[2176,1536]{1,0:T(8,128)(2,1)} custom-call(bf16[320,1536]{1,0:T(8,128)(2,1)} %get-tuple-element.193.refs_0_, bf16[320,1536]{1,0:T(8,128)(2,1)} %copy-done.39, bf16[320,1536]{1,0:T(8,128)(2,1)} %copy-done.40, bf16[320,1536]{1,0:T(8,128)(2,1)} %copy-done.42, bf16[320,1536]{1,0:T(8,128)(2,1)} %copy-done.20, bf16[320,1536]{1,0:T(8,128)(2,1)} %copy-done.37, ...), custom_call_target="tpu_custom_call" | custom-call | flops 18400000000 | bytes 19955712 | tf_op jit(solution)/shard_map/pallas_call | solution.py:835
  356.7 30.6 %shard_map.359 = (f32[320,1536]{1,0:T(8,128)}, bf16[320,1536]{1,0:T(8,128)(2,1)}, f32[1,1536]{1,0:T(1,128)}, f32[320,1536]{1,0:T(8,128)}, bf16[320,512]{1,0:T(8,...) custom-call(s32[3]{0:T(128)} %pad_add_fusion.refs_0_.info, ...), custom_call_target="tpu_custom_call" | custom-call | flops 35649998848 | bytes 20152332 | tf_op jit(solution)/shard_map/pallas_call | solution.py:512
  390.9 7.2 %shard_map.360 = (bf16[4,768,384]{2,1,0:T(8,128)(2,1)}, bf16[4,768,384]{2,1,0:T(8,128)(2,1)}) custom-call(s32[3]{0:T(128)} %pad_add_fusion.refs_0_.info, bf16[320,1536]{1,0:T(8,128)(2,1)} %get-tuple-element.233.refs_1_, bf16[320,1536]{1,0:T(8,128)(2,1)} %get-tuple-element.234.refs_2_), custom_call_target="tpu_custom_call" | custom-call | tf_op jit(solution)/shard_map/pallas_call | solution.py:512
  411.8 8.7 %shard_map.362 = (bf16[4,1024,384]{2,1,0:T(8,128)(2,1)}, bf16[4,1024,384]{2,1,0:T(8,128)(2,1)}) custom-call(s32[3]{0:T(128)} %pad_add_fusion.refs_0_.info, bf16[320,1536]{1,0:T(8,128)(2,1)} %get-tuple-element.215.refs_1_, bf16[320,2048]{1,0:T(8,128)(2,1)} %get-tuple-element.249.refs_2_.refs_1_), custom_call_target="tpu_custom_call" | custom-call | tf_op jit(solution)/shard_map/pallas_call | solution.py:512
  420.5 8.9 %shard_map.363 = (bf16[320,1536]{1,0:T(8,128)(2,1)}, f32[1,1536]{1,0:T(1,128)}) custom-call(s32[3]{0:T(128)} %pad_add_fusion.refs_0_.info, bf16[320,2048]{1,0:T(8,128)(2,1)} %get-tuple-element.249.refs_2_.refs_1_, bf16[320,1536]{1,0:T(8,128)(2,1)} %bitcast.176, f32[1,1536]{1,0:T(1,128)} %broadcast_in_dim_reshape.7.refs_2_.refs_3_, ...), custom_call_target="tpu_custom_call" | custom-call | tf_op jit(solution)/shard_map/pallas_call | solution.py:512
  442.8 8.8 %collective-permute-done.50 = bf16[768,384]{1,0:T(8,128)(2,1)S(1)} collective-permute-done((bf16[768,384]{1,0:T(8,128)(2,1)S(1)}, bf16[768,384]{1,0:T(8,128)(2,1)S(1)}, u32[]{:S(2)}, u32[]{:S(2)}) %collective-permute-start.50) | collective-permute-done | bytes 589856 | tf_op jit(solution)/shard_map/out_dp/ppermute | solution.py:116
  470.0 6.8 %collective-permute-done.55 = bf16[192,384]{1,0:T(8,128)(2,1)S(1)} collective-permute-done((bf16[192,384]{1,0:T(8,128)(2,1)S(1)}, bf16[192,384]{1,0:T(8,128)(2,1)S(1)}, u32[]{:S(2)}, u32[]{:S(2)}) %collective-permute-start.55) | collective-permute-done | bytes 147488 | tf_op jit(solution)/shard_map/out_line/ppermute | solution.py:153
  478.2 9.7 %collective-permute-done.57 = bf16[192,384]{1,0:T(8,128)(2,1)S(1)} collective-permute-done((bf16[192,384]{1,0:T(8,128)(2,1)S(1)}, bf16[192,384]{1,0:T(8,128)(2,1)S(1)}, u32[]{:S(2)}, u32[]{:S(2)}) %collective-permute-start.57) | collective-permute-done | bytes 147488 | tf_op jit(solution)/shard_map/out_line/ppermute | solution.py:153
  487.9 7.8 %collective-permute-done.53 = bf16[1088,384]{1,0:T(8,128)(2,1)} collective-permute-done((bf16[1088,384]{1,0:T(8,128)(2,1)}, bf16[1088,384]{1,0:T(8,128)(2,1)}, u32[]{:S(2)}, u32[]{:S(2)}) %collective-permute-start.53) | collective-permute-done | bytes 835616 | tf_op jit(solution)/shard_map/qkv_dp/ppermute | solution.py:116
  503.7 6.1 collective-permute-done.61
  510.4 10.1 %collective-permute-done.62 = bf16[384,576]{1,0:T(8,128)(2,1)S(1)} collective-permute-done((bf16[384,576]{1,0:T(8,128)(2,1)S(1)}, bf16[384,576]{1,0:T(8,128)(2,1)S(1)}, u32[]{:S(2)}, u32[]{:S(2)}) %collective-permute-start.62) | collective-permute-done | bytes 442400 | tf_op jit(solution)/shard_map/gradient_exchange/ppermute | solution.py:116
  586.6 6.4 %fusion.42 = (bf16[2240,192]{0,1:T(8,128)(2,1)}, f32[2240,192]{0,1:T(8,128)}, f32[2240,192]{0,1:T(8,128)}, f32[2240,192]{0,1:T(8,128)}) fusion(f32[2240,192]{0,1:T(8,128)S(1)} %copy-done.2, f32[]{:T(128)S(6)} %div.70, bf16[2240,192]{0,1:T(8,128)(2,1)} %copy.102, f32[2240,192]{0,1:T(8,128)} %param.31, f32[2240,192]{0,1:T(8,128)} %param.32), kind=kLoop, calls=%fused_computation.174 | loop fusion | flops 7311360 | bytes 12042244 | tf_op jit(solution)/shard_map/convert_element_type | solution.py:111
  (404 shorter events, 249.5 us)
Async XLA Ops:
  7.2 213.7 %all-gather.5.cloned.1.call-start = ((), (), s32[]{:S(2)}) async-start(), calls=%async_computation.3 | async-start | bytes 15925248 | tf_op jit(solution)/shard_map/all_gather | solution.py:988
  13.3 30.1 %collective-permute-start.1 = (bf16[448,384]{0,1:T(8,128)(2,1)}, bf16[448,384]{0,1:T(8,128)(2,1)}, u32[]{:S(2)}, u32[]{:S(2)}) collective-permute-start(bf16[448,384]{0,1:T(8,128)(2,1)} %get-tuple-element.382), channel_id=1, source_target_pairs={{0,4},{1,5},{2,6},{3,7},{4,0},{5,1},{6,2},{7,3},{8,12},{9,13},{10,... | collective-permute-start | bytes 1032200 | tf_op jit(solution)/shard_map/matrix_line/ppermute | solution.py:153
  15.9 27.5 %collective-permute-start.2 = (bf16[448,384]{0,1:T(8,128)(2,1)}, bf16[448,384]{0,1:T(8,128)(2,1)}, u32[]{:S(2)}, u32[]{:S(2)}) collective-permute-start(bf16[448,384]{0,1:T(8,128)(2,1)} %get-tuple-element.382), channel_id=1, source_target_pairs={{0,6},{1,7},{2,4},{3,5},{4,2},{5,3},{6,0},{7,1},{8,14},{9,15},{10,... | collective-permute-start | bytes 1032200 | tf_op jit(solution)/shard_map/matrix_line/ppermute | solution.py:153
  27.2 32.4 %collective-permute-start.11 = (bf16[560,576]{1,0:T(8,128)(2,1)}, bf16[560,576]{1,0:T(8,128)(2,1)}, u32[]{:S(2)}, u32[]{:S(2)}) collective-permute-start(bf16[560,576]{1,0:T(8,128)(2,1)} %get-tuple-element.361), channel_id=1, source_target_pairs={{0,16},{8,24},{16,0},{24,8},{1,17},{9,25},{17,1},{25,9},{2,18},{10... | collective-permute-start | bytes 1935368 | tf_op jit(solution)/shard_map/weights_exchange/ppermute | solution.py:116
  30.4 29.1 %collective-permute-start.12 = (bf16[560,576]{1,0:T(8,128)(2,1)}, bf16[560,576]{1,0:T(8,128)(2,1)}, u32[]{:S(2)}, u32[]{:S(2)}) collective-permute-start(bf16[560,576]{1,0:T(8,128)(2,1)} %get-tuple-element.362), channel_id=1, source_target_pairs={{0,24},{8,16},{16,8},{24,0},{1,25},{9,17},{17,9},{25,1},{2,26},{10... | collective-permute-start | bytes 1935368 | tf_op jit(solution)/shard_map/weights_exchange/ppermute | solution.py:116
  69.3 221.3 %all-gather.3.cloned.1.call-start = ((), (), s32[]{:S(2)}) async-start(), calls=%async_computation.2 | async-start | bytes 7520256 | tf_op jit(solution)/shard_map/all_gather | solution.py:988
  150.1 284.5 %reduce-scatter.3.cloned.1.call-start = ((), (), s32[]{:S(2)}) async-start(), calls=%async_computation.4 | async-start | bytes 15925248 | tf_op jit(solution)/shard_map/reduce_scatter | solution.py:1051
  154.6 25.2 %collective-permute-start.34 = (bf16[320,1536]{1,0:T(8,128)(2,1)S(1)}, bf16[320,1536]{1,0:T(8,128)(2,1)S(1)}, u32[]{:S(2)}, u32[]{:S(2)}) collective-permute-start(bf16[320,1536]{1,0:T(8,128)(2,1)S(1)} %bitcast_select_fusion.refs_4_.refs_2_), channel_id=1, source_target_pairs={{0,8},{8,0},{16,24},{24,16},{1,9},{9,1},{17,25},{25,17},{2,10},{10... | collective-permute-start | bytes 2949128 | tf_op jit(solution)/shard_map/cot_gather/ppermute | solution.py:116
  155.2 25.5 %collective-permute-start.35 = (bf16[320,1536]{1,0:T(8,128)(2,1)S(1)}, bf16[320,1536]{1,0:T(8,128)(2,1)S(1)}, u32[]{:S(2)}, u32[]{:S(2)}) collective-permute-start(bf16[320,1536]{1,0:T(8,128)(2,1)S(1)} %bitcast_select_fusion.refs_4_.refs_2_), channel_id=1, source_target_pairs={{0,16},{8,24},{16,0},{24,8},{1,17},{9,25},{17,1},{25,9},{2,18},{10... | collective-permute-start | bytes 2949128 | tf_op jit(solution)/shard_map/cot_gather/ppermute | solution.py:116
  177.5 24.9 %collective-permute-start.30 = (bf16[320,1536]{1,0:T(8,128)(2,1)}, bf16[320,1536]{1,0:T(8,128)(2,1)S(1)}, u32[]{:S(2)}, u32[]{:S(2)}) collective-permute-start(bf16[320,1536]{1,0:T(8,128)(2,1)} %get-tuple-element.193.refs_0_), channel_id=1, source_target_pairs={{0,8},{8,0},{16,24},{24,16},{1,9},{9,1},{17,25},{25,17},{2,10},{10... | collective-permute-start | bytes 2949128 | tf_op jit(solution)/shard_map/normed_gather/ppermute | solution.py:116
  178.6 24.9 %collective-permute-start.31 = (bf16[320,1536]{1,0:T(8,128)(2,1)}, bf16[320,1536]{1,0:T(8,128)(2,1)S(1)}, u32[]{:S(2)}, u32[]{:S(2)}) collective-permute-start(bf16[320,1536]{1,0:T(8,128)(2,1)} %get-tuple-element.193.refs_0_), channel_id=1, source_target_pairs={{0,16},{8,24},{16,0},{24,8},{1,17},{9,25},{17,1},{25,9},{2,18},{10... | collective-permute-start | bytes 2949128 | tf_op jit(solution)/shard_map/normed_gather/ppermute | solution.py:116
  179.9 34.1 %collective-permute-start.36 = (bf16[160,1536]{1,0:T(8,128)(2,1)S(1)}, bf16[160,1536]{1,0:T(8,128)(2,1)S(1)}, u32[]{:S(2)}, u32[]{:S(2)}) collective-permute-start(bf16[160,1536]{1,0:T(8,128)(2,1)S(1)} %slice.220), channel_id=1, source_target_pairs={{0,16},{8,24},{16,0},{24,8},{1,17},{9,25},{17,1},{25,9},{2,18},{10... | collective-permute-start | bytes 1474568 | tf_op jit(solution)/shard_map/cot_gather/ppermute | solution.py:116
  180.7 33.3 %collective-permute-start.37 = (bf16[160,1536]{1,0:T(8,128)(2,1)S(1)}, bf16[160,1536]{1,0:T(8,128)(2,1)S(1)}, u32[]{:S(2)}, u32[]{:S(2)}) collective-permute-start(bf16[160,1536]{1,0:T(8,128)(2,1)S(1)} %slice.221), channel_id=1, source_target_pairs={{0,8},{8,0},{16,24},{24,16},{1,9},{9,1},{17,25},{25,17},{2,10},{10... | collective-permute-start | bytes 1474568 | tf_op jit(solution)/shard_map/cot_gather/ppermute | solution.py:116
  290.0 240.7 %reduce-scatter.5.cloned.1.call-start = ((), (), s32[]{:S(2)}) async-start(), calls=%async_computation.5 | async-start | bytes 7520256 | tf_op jit(solution)/shard_map/reduce_scatter | solution.py:1157
  311.1 42.2 %collective-permute-start.39 = (bf16[320,1536]{1,0:T(8,128)(2,1)}, bf16[320,1536]{1,0:T(8,128)(2,1)S(1)}, u32[]{:S(2)}, u32[]{:S(2)}) collective-permute-start(bf16[320,1536]{1,0:T(8,128)(2,1)} %get-tuple-element.198), channel_id=1, source_target_pairs={{0,16},{8,24},{16,0},{24,8},{1,17},{9,25},{17,1},{25,9},{2,18},{10... | collective-permute-start | bytes 2949128 | tf_op jit(solution)/shard_map/back_reduce/ppermute | solution.py:116
  312.0 41.4 %collective-permute-start.40 = (bf16[320,1536]{1,0:T(8,128)(2,1)}, bf16[320,1536]{1,0:T(8,128)(2,1)S(1)}, u32[]{:S(2)}, u32[]{:S(2)}) collective-permute-start(bf16[320,1536]{1,0:T(8,128)(2,1)} %get-tuple-element.199), channel_id=1, source_target_pairs={{0,24},{8,16},{16,8},{24,0},{1,25},{9,17},{17,9},{25,1},{2,26},{10... | collective-permute-start | bytes 2949128 | tf_op jit(solution)/shard_map/back_reduce/ppermute | solution.py:116
  354.4 33.0 %collective-permute-start.41 = (bf16[320,1536]{1,0:T(8,128)(2,1)}, bf16[320,1536]{1,0:T(8,128)(2,1)S(1)}, u32[]{:S(2)}, u32[]{:S(2)}) collective-permute-start(bf16[320,1536]{1,0:T(8,128)(2,1)} %get-tuple-element.227), channel_id=1, source_target_pairs={{0,8},{8,0},{16,24},{24,16},{1,9},{9,1},{17,25},{25,17},{2,10},{10... | collective-permute-start | bytes 2949128 | tf_op jit(solution)/shard_map/mixed_reduce/ppermute | solution.py:116
  355.4 32.0 %collective-permute-start.42 = (bf16[320,1536]{1,0:T(8,128)(2,1)S(1)}, bf16[320,1536]{1,0:T(8,128)(2,1)S(1)}, u32[]{:S(2)}, u32[]{:S(2)}) collective-permute-start(bf16[320,1536]{1,0:T(8,128)(2,1)S(1)} %copy-done.54), channel_id=1, source_target_pairs={{0,16},{8,24},{16,0},{24,8},{1,17},{9,25},{17,1},{25,9},{2,18},{10... | collective-permute-start | bytes 2949128 | tf_op jit(solution)/shard_map/mixed_reduce/ppermute | solution.py:116
  457.0 30.9 %collective-permute-start.54 = (bf16[1088,384]{1,0:T(8,128)(2,1)}, bf16[1088,384]{1,0:T(8,128)(2,1)}, u32[]{:S(2)}, u32[]{:S(2)}) collective-permute-start(bf16[1088,384]{1,0:T(8,128)(2,1)} %bitcast.66), channel_id=1, source_target_pairs={{0,24},{8,16},{16,8},{24,0},{1,25},{9,17},{17,9},{25,1},{2,26},{10... | collective-permute-start | bytes 2506760 | tf_op jit(solution)/shard_map/qkv_dp/ppermute | solution.py:116
  460.3 35.3 %collective-permute-start.53 = (bf16[1088,384]{1,0:T(8,128)(2,1)}, bf16[1088,384]{1,0:T(8,128)(2,1)}, u32[]{:S(2)}, u32[]{:S(2)}) collective-permute-start(bf16[1088,384]{1,0:T(8,128)(2,1)} %bitcast.63), channel_id=1, source_target_pairs={{0,16},{8,24},{16,0},{24,8},{1,17},{9,25},{17,1},{25,9},{2,18},{10... | collective-permute-start | bytes 2506760 | tf_op jit(solution)/shard_map/qkv_dp/ppermute | solution.py:116
  461.9 33.8 %collective-permute-start.52 = (bf16[1088,384]{1,0:T(8,128)(2,1)}, bf16[1088,384]{1,0:T(8,128)(2,1)}, u32[]{:S(2)}, u32[]{:S(2)}) collective-permute-start(bf16[1088,384]{1,0:T(8,128)(2,1)} %bitcast.60), channel_id=1, source_target_pairs={{0,8},{8,0},{16,24},{24,16},{1,9},{9,1},{17,25},{25,17},{2,10},{10... | collective-permute-start | bytes 2506760 | tf_op jit(solution)/shard_map/qkv_dp/ppermute | solution.py:116
  497.2 23.3 %collective-permute-start.62 = (bf16[384,576]{1,0:T(8,128)(2,1)S(1)}, bf16[384,576]{1,0:T(8,128)(2,1)S(1)}, u32[]{:S(2)}, u32[]{:S(2)}) collective-permute-start(bf16[384,576]{1,0:T(8,128)(2,1)S(1)} %copy-done.58), channel_id=1, source_target_pairs={{0,16},{8,24},{16,0},{24,8},{1,17},{9,25},{17,1},{25,9},{2,18},{10... | collective-permute-start | bytes 1327112 | tf_op jit(solution)/shard_map/gradient_exchange/ppermute | solution.py:116
  502.1 23.4 %collective-permute-start.58 = (bf16[272,384]{1,0:T(8,128)(2,1)}, bf16[272,384]{1,0:T(8,128)(2,1)S(1)}, u32[]{:S(2)}, u32[]{:S(2)}) collective-permute-start(bf16[272,384]{1,0:T(8,128)(2,1)} %get-tuple-element.369), channel_id=1, source_target_pairs={{0,2},{1,3},{2,0},{3,1},{4,6},{5,7},{6,4},{7,5},{8,10},{9,11},{10,... | collective-permute-start | bytes 626696 | tf_op jit(solution)/shard_map/qkv_line/ppermute | solution.py:153
  520.5 26.0 %collective-permute-start.65 = (bf16[320,1536]{1,0:T(8,128)(2,1)}, bf16[320,1536]{1,0:T(8,128)(2,1)}, u32[]{:S(2)}, u32[]{:S(2)}) collective-permute-start(bf16[320,1536]{1,0:T(8,128)(2,1)} %get-tuple-element.305), channel_id=1, source_target_pairs={{0,24},{8,16},{16,8},{24,0},{1,25},{9,17},{17,9},{25,1},{2,26},{10... | collective-permute-start | bytes 2949128 | tf_op jit(solution)/shard_map/mixed_reduce/ppermute | solution.py:116
  (116 other events, 1323.2 us)
Sparse Core Ops, SparseCore 0:
  69.4 129.8 all-gather.4
  201.5 66.2 all-gather.2
  290.2 144.3 reduce-scatter.2
  436.8 92.3 reduce-scatter.4

commit v5 on v4

--- a/solution.py
+++ b/solution.py
@@ -209,21 +209,6 @@
 
 def total_shard(shard):
     return sum(block.astype(jnp.float32) for block in shard).T
-
-
-def exchange_weights(half_in, half_down):
-    ranks = lax.axis_size("dp")
-    rows, columns = half_in.shape
-    part = columns // ranks
-    width = half_down.shape[1]
-    slices = half_down.shape[0] // (ranks * part)
-    in_sent = half_in.reshape(rows, ranks, part).transpose(1, 2, 0)
-    down_sent = half_down.reshape(slices, ranks, part, width).transpose(1, 2, 0, 3)
-    sent = jnp.concatenate([in_sent, down_sent.reshape(ranks, part, slices * width)], axis=2)
-    got = yield sent
-    in_piece = got[:, :, :rows].transpose(1, 0, 2).reshape(part, ranks * rows)
-    down_piece = got[:, :, rows:].reshape(ranks, part, slices, width).transpose(3, 0, 2, 1)
-    yield in_piece, down_piece.reshape(width, ranks * slices, part)
 
 
 def unpack_gradients(got, rows, columns):
@@ -481,6 +466,51 @@
     squares[...] = jnp.sum(total * total, keepdims=True)
 
 
+def send_kernel(ranks, info, w_in, w_down, *refs):
+    outs = refs[:ranks]
+    (turned,) = refs[ranks:]
+    place = info[0]
+    rows = w_in.shape[1]
+    part = w_in.shape[0] // ranks
+    columns = w_down.shape[0]
+    for p in range(ranks):
+        turned[p, :, pl.ds(0, rows)] = bf16(w_in[pl.ds(p * part, part), :])
+        for s in range(w_down.shape[1] // (ranks * part)):
+            source = w_down[:, pl.ds((s * ranks + p) * part, part)]
+            turned[p, :, pl.ds(rows + s * columns, columns)] = bf16(source.T)
+    for k in range(ranks):
+        outs[k][...] = turned[place ^ k]
+
+
+def place_kernel(chunks, ranks, info, *refs):
+    got = refs[:ranks]
+    outs = refs[ranks : ranks + len(chunks)]
+    stacked, *lows = refs[ranks + len(chunks) :]
+    place = info[0]
+    rows = D // ranks
+    for k in range(ranks):
+        stacked[k] = got[k][...]
+    for chunk, out, low in zip(chunks, outs, lows):
+        low[...] = jnp.zeros_like(low)
+        if chunk.deep > chunk.real:
+            out[...] = jnp.zeros_like(out)
+    for a in range(ranks):
+        start = 0
+        for chunk, out, low in zip(chunks, outs, lows):
+            each = chunk.slices // ranks
+            piece = stacked[place ^ a, pl.ds(start, chunk.real), :]
+            out[pl.ds(0, chunk.real), pl.ds(a * rows, rows)] = piece[:, :rows]
+            for s in range(each):
+                at = rows + s * chunk.columns
+                turned = piece[:, at : at + chunk.columns].astype(jnp.float32).T
+                for i in range(chunk.folds):
+                    lane = i * chunk.wide + (a * each + s) * chunk.deep
+                    low[:, pl.ds(lane, chunk.real)] = turned[i * chunk.low : (i + 1) * chunk.low]
+            start += chunk.real
+    for chunk, out, low in zip(chunks, outs, lows):
+        out[pl.ds(chunk.deep, chunk.low), :] = bf16(low[...])
+
+
 def pack_kernel(chunk, ranks, info, shard, *refs):
     outs = refs[:ranks]
     squares, turned = refs[ranks:]
@@ -546,27 +576,6 @@
         self.blocks = [
             (s, min(UNIT_TILE, self.units - s)) for s in range(0, self.units, UNIT_TILE)
         ]
-
-    def pack(self, in_piece, down_piece):
-        extra = self.deep - self.real
-        in_piece = jnp.pad(in_piece, ((0, extra), (0, 0)))
-        down_piece = jnp.pad(down_piece, ((0, 0), (0, 0), (0, extra)))
-        down_piece = down_piece.reshape(self.columns, self.units)
-        down_piece = jnp.pad(down_piece, ((0, 0), (0, self.wide - self.units)))
-        parts = [down_piece[i * self.low : (i + 1) * self.low] for i in range(self.folds)]
-        down_piece = jnp.concatenate(parts, axis=1)
-        down_piece = jnp.pad(down_piece, ((0, 0), (0, D - down_piece.shape[1])))
-        return jnp.concatenate([in_piece, down_piece])
-
-    def unpack(self, shard):
-        in_piece = shard[: self.real]
-        down_piece = shard[self.deep :]
-        parts = [
-            down_piece[:, i * self.wide : i * self.wide + self.units] for i in range(self.folds)
-        ]
-        down_piece = jnp.concatenate(parts)
-        down_piece = down_piece.reshape(self.columns, self.slices, self.deep)
-        return in_piece, down_piece[:, :, : self.real]
 
     def in_parts(self, s, n, half):
         parts = []
@@ -970,23 +979,33 @@
     gain_attn = gain_attn[None]
     gain_mlp = gain_mlp[None]
 
-    exchange = exchange_weights(half_in, half_down)
-    got = scoped("weights_exchange", dp_exchange, next(exchange))
+    part = half_in.shape[1] // ranks
+    width = block + D // ranks // 2
+    sent = call(
+        functools.partial(send_kernel, ranks),
+        [info, half_in.T, half_down.T],
+        [bf16_like(part, width)] * ranks,
+        [vmem_bf16(ranks, part, width)],
+        1,
+    )
+    got = [sent[0]] + [
+        scoped("weights_exchange", dp_send, sent[k], k) for k in range(1, ranks)
+    ]
     got, out_along, qkv_along = lax.optimization_barrier((got, out_along, qkv_along))
     qkv_own = scoped("qkv_gather", dp_gather, qkv_along)
     qkv_other = [scoped("qkv_swap", core_swap, block) for block in qkv_own]
     out_along, qkv_other = lax.optimization_barrier((out_along, qkv_other))
     out_near = scoped("out_gather", gather_near, out_along)
 
-    in_piece, down_piece = exchange.send(got)
     chunks = [Chunk(size, lines) for size in CHUNKS]
-    gathered = []
-    start = 0
-    for chunk in chunks:
-        stop = start + chunk.real
-        packed = chunk.pack(in_piece[start:stop], down_piece[:, :, start:stop])
-        gathered.append(lax.all_gather(packed, "fsdp", axis=0, tiled=True))
-        start = stop
+    packed = call(
+        functools.partial(place_kernel, chunks, ranks),
+        [info, *got],
+        [bf16_like(chunk.step, D) for chunk in chunks],
+        [vmem_bf16(ranks, part, width)] + [vmem_f32(chunk.low, D) for chunk in chunks],
+        1,
+    )
+    gathered = [lax.all_gather(array, "fsdp", axis=0, tiled=True) for array in packed]
 
     query_places = place * rows + jnp.arange(rows, dtype=jnp.int32)
     cosine, sine = rope_tables(query_places.astype(jnp.float32))
@@ -1245,8 +1264,8 @@
         lengths,
         bf16(qkv_weight),
         bf16(out_weight),
-        bf16(mlp_in_weight),
-        bf16(down_weight),
+        mlp_in_weight,
+        down_weight,
         bf16(small_params),
     )
     mixed, input_cot, total_squares, qkv_grad, out_grad, in_grad, down_grad, small_grad = results

time: 616 us -> 606 us (0.984)
  other arithmetic: 62.3 us -> 46.8 us
  local copies, waits for them, and re-layouts: 37.1 us -> 25.6 us
  Pallas kernels: 223 us -> 232 us
    pallas_call x10 -> x12, Pallas kernels: 97.6 us -> 107 us  [call(): pl.pallas_call(kernel, out_shape=tuple(outs), in_specs=[pl.BlockSpec(memo...]
    concatenate x3 -> x0, other arithmetic: 6.53 us -> none  [the longest x2 3.33 us: pack(): return jnp.concatenate([in_piece, down_piece])]
  transfers between devices with their start and end apart: 79 -> 79, of which waited for: 36 -> 39; matrix products, arithmetic and copies ran while one was open for 10% -> 7% of each run, Pallas kernels for 36% -> 38%
where the time goes in v5:
time: 606 us; the launch traced here: 597 us
  Pallas kernels  232 us (38%)
  waiting for transfers between devices  181 us (30%)
  starting transfers between devices  88 us (15%)
  other arithmetic  46.8 us (8%)
  local copies, waits for them, and re-layouts  25.6 us (4%)
  between operations  24.1 us (4%)
    ppermute x50, waiting for transfers between devices, dp_send(): return lax.ppermute(block, 'dp', [(i, i ^ k) for i in range(count)])  132 us
    pallas_call x4, Pallas kernels, hbm_call(): pl.pallas_call(kernel, out_shape=tuple(outs), in_specs=[anywhere] * len(a...  125 us
    pallas_call x12, Pallas kernels, call(): pl.pallas_call(kernel, out_shape=tuple(outs), in_specs=[pl.BlockSpec(memo...  107 us
    ppermute x50, starting transfers between devices, dp_send(): return lax.ppermute(block, 'dp', [(i, i ^ k) for i in range(count)])  62.2 us
    ppermute x15, waiting for transfers between devices, line_send(): return lax.ppermute(block, 'fsdp', [(i, i ^ 2 * r) for i in range(count)])  42 us
    ppermute x15, starting transfers between devices, line_send(): return lax.ppermute(block, 'fsdp', [(i, i ^ 2 * r) for i in range(count)])  23.4 us
    convert_element_type x5, other arithmetic, update(): return (weight_new, first_new, second_new, weight_new.astype(jnp.bfloat16))  15.1 us
  transfers between devices with their start and end apart: 79, of which 39 were waited for; matrix products, arithmetic and copies ran while one was open for 7% of the time, Pallas kernels for 38%

profile of v5, /device:TPU:0, one launch (start us, length us, event | category | flops | bytes accessed | tf_op | source)
XLA Modules:
  0.0 597.1 jit_solution(383830615788888063)
XLA Ops:
  31.9 10.4 %collective-permute-done.1 = bf16[448,384]{0,1:T(8,128)(2,1)S(1)} collective-permute-done((bf16[448,384]{0,1:T(8,128)(2,1)S(1)}, bf16[448,384]{0,1:T(8,128)(2,1)S(1)}, u32[]{:S(2)}, u32[]{:S(2)}) %collective-permute-start.1) | collective-permute-done | bytes 344096 | tf_op jit(solution)/shard_map/matrix_line/ppermute | solution.py:153
  43.8 11.6 %collective-permute-done.11.refs_2_ = bf16[560,576]{1,0:T(8,128)(2,1)} collective-permute-done((bf16[560,576]{1,0:T(8,128)(2,1)}, bf16[560,576]{1,0:T(8,128)(2,1)}, u32[]{:S(2)}, u32[]{:S(2)}) %collective-permute-start.11) | collective-permute-done | bytes 645152 | tf_op jit(solution)/shard_map/weights_exchange/ppermute | solution.py:116
  95.9 7.6 %shard_map.354 = (bf16[320,1536]{1,0:T(8,128)(2,1)}, bf16[320,1536]{1,0:T(8,128)(2,1)}, bf16[320,512]{1,0:T(8,128)(2,1)}) custom-call(s32[3]{0:T(128)} %pad_add_fusion.info.refs_0_, bf16[320,1536]{1,0:T(8,128)(2,1)} %bitcast.144, f32[1,1536]{1,0:T(1,128)} %broadcast_in_dim_reshape.7.refs_2_.refs_3_, f32[1,2048]{1,0:T(1,128)} %bitcast.160, ...), custom_call_target="tpu_custom_call" | custom-call | flops 8049999872 | bytes 9910284 | tf_op jit(solution)/shard_map/pallas_call | solution.py:542
  111.6 5.9 collective-permute-done.27
  122.1 9.0 %collective-permute-done.23.refs_5_.refs_11_ = bf16[320,512]{1,0:T(8,128)(2,1)S(1)} collective-permute-done((bf16[320,512]{1,0:T(8,128)(2,1)S(1)}, bf16[320,512]{1,0:T(8,128)(2,1)S(1)}, u32[]{:S(2)}, u32[]{:S(2)}) %collective-permute-start.23) | collective-permute-done | bytes 327712 | tf_op jit(solution)/shard_map/kv_gather/ppermute | solution.py:116
  141.6 21.3 %shard_map.355 = (bf16[320,1536]{1,0:T(8,128)(2,1)}, f32[16,320]{1,0:T(8,128)}, f32[320,1536]{1,0:T(8,128)}, bf16[320,1536]{1,0:T(8,128)(2,1)}) custom-call(s32[3]{0:T(128)} %pad_add_fusion.info.refs_0_, bf16[320,1536]{1,0:T(8,128)(2,1)} %bitcast.145, f32[1,1536]{1,0:T(1,128)} %broadcast_in_dim_reshape.6.refs_2_.refs_3_, ...), custom_call_target="tpu_custom_call" | custom-call | flops 27599998976 | bytes 11954188 | tf_op jit(solution)/shard_map/pallas_call | solution.py:542
  168.2 19.6 %collective-permute-done.30.refs_1_ = bf16[320,1536]{1,0:T(8,128)(2,1)S(1)} collective-permute-done((bf16[320,1536]{1,0:T(8,128)(2,1)}, bf16[320,1536]{1,0:T(8,128)(2,1)S(1)}, u32[]{:S(2)}, u32[]{:S(2)}) %collective-permute-start.30) | collective-permute-done | bytes 983072 | tf_op jit(solution)/shard_map/normed_gather/ppermute | solution.py:116
  189.9 9.8 %collective-permute-done.36 = bf16[160,1536]{1,0:T(8,128)(2,1)S(1)} collective-permute-done((bf16[160,1536]{1,0:T(8,128)(2,1)S(1)}, bf16[160,1536]{1,0:T(8,128)(2,1)S(1)}, u32[]{:S(2)}, u32[]{:S(2)}) %collective-permute-start.36) | collective-permute-done | bytes 491552 | tf_op jit(solution)/shard_map/cot_gather/ppermute | solution.py:116
  199.9 7.2 %collective-permute-done.32 = bf16[160,1536]{1,0:T(8,128)(2,1)S(1)} collective-permute-done((bf16[160,1536]{1,0:T(8,128)(2,1)S(1)}, bf16[160,1536]{1,0:T(8,128)(2,1)S(1)}, u32[]{:S(2)}, u32[]{:S(2)}) %collective-permute-start.32) | collective-permute-done | bytes 491552 | tf_op jit(solution)/shard_map/normed_gather/ppermute | solution.py:116
  208.1 68.4 %shard_map.357 = (f32[1280,1536]{1,0:T(8,128)}, f32[1280,1536]{1,0:T(8,128)}, bf16[4608,1536]{1,0:T(8,128)(2,1)}) custom-call(bf16[320,1536]{1,0:T(8,128)(2,1)} %get-tuple-element.206.refs_0_, bf16[320,1536]{1,0:T(8,128)(2,1)} %copy-done.36, bf16[320,1536]{1,0:T(8,128)(2,1)} %copy-done.37, bf16[320,1536]{1,0:T(8,128)(2,1)} %copy-done.39, ...), custom_call_target="tpu_custom_call" | custom-call | flops 78199996416 | bytes 51904512 | tf_op jit(solution)/shard_map/pallas_call | solution.py:844
  276.8 20.5 %shard_map.358 = (bf16[320,1536]{1,0:T(8,128)(2,1)}, bf16[320,1536]{1,0:T(8,128)(2,1)}, bf16[320,1536]{1,0:T(8,128)(2,1)}, bf16[320,1536]{1,0:T(8,128)(2,1)}, bf...) custom-call(bf16[320,1536]{1,0:T(8,128)(2,1)} %copy-done.37, ...), custom_call_target="tpu_custom_call" | custom-call | flops 23000000512 | bytes 32980992 | tf_op jit(solution)/shard_map/pallas_call | solution.py:844
  299.0 20.5 %shard_map.359 = (bf16[320,1536]{1,0:T(8,128)(2,1)}, bf16[320,1536]{1,0:T(8,128)(2,1)}, bf16[320,1536]{1,0:T(8,128)(2,1)}, bf16[320,1536]{1,0:T(8,128)(2,1)}, bf...) custom-call(bf16[320,1536]{1,0:T(8,128)(2,1)} %get-tuple-element.206.refs_0_, ...), custom_call_target="tpu_custom_call" | custom-call | flops 23000000512 | bytes 32980992 | tf_op jit(solution)/shard_map/pallas_call | solution.py:844
  321.4 16.1 %shard_map.360 = bf16[2176,1536]{1,0:T(8,128)(2,1)} custom-call(bf16[320,1536]{1,0:T(8,128)(2,1)} %get-tuple-element.206.refs_0_, bf16[320,1536]{1,0:T(8,128)(2,1)} %copy-done.36, bf16[320,1536]{1,0:T(8,128)(2,1)} %copy-done.37, bf16[320,1536]{1,0:T(8,128)(2,1)} %copy-done.39, bf16[320,1536]{1,0:T(8,128)(2,1)} %bitcast_select_fusion.refs_4_.refs_2_, ...), custom_call_target="tpu_custom_call" | custom-call | flops 18400000000 | bytes 19955712 | tf_op jit(solution)/shard_map/pallas_call | solution.py:844
  342.8 30.4 %shard_map.361 = (f32[320,1536]{1,0:T(8,128)}, bf16[320,1536]{1,0:T(8,128)(2,1)}, f32[1,1536]{1,0:T(1,128)}, f32[320,1536]{1,0:T(8,128)}, bf16[320,512]{1,0:T(8,...) custom-call(s32[3]{0:T(128)} %pad_add_fusion.info.refs_0_, ...), custom_call_target="tpu_custom_call" | custom-call | flops 35649998848 | bytes 20152332 | tf_op jit(solution)/shard_map/pallas_call | solution.py:542
  376.8 7.1 %shard_map.362 = (bf16[4,768,384]{2,1,0:T(8,128)(2,1)}, bf16[4,768,384]{2,1,0:T(8,128)(2,1)}) custom-call(s32[3]{0:T(128)} %pad_add_fusion.info.refs_0_, bf16[320,1536]{1,0:T(8,128)(2,1)} %get-tuple-element.251.refs_1_, bf16[320,1536]{1,0:T(8,128)(2,1)} %get-tuple-element.252.refs_2_), custom_call_target="tpu_custom_call" | custom-call | tf_op jit(solution)/shard_map/pallas_call | solution.py:542
  398.3 8.7 %shard_map.364 = (bf16[4,1024,384]{2,1,0:T(8,128)(2,1)}, bf16[4,1024,384]{2,1,0:T(8,128)(2,1)}) custom-call(s32[3]{0:T(128)} %pad_add_fusion.info.refs_0_, bf16[320,1536]{1,0:T(8,128)(2,1)} %get-tuple-element.233.refs_1_, bf16[320,2048]{1,0:T(8,128)(2,1)} %get-tuple-element.267.refs_2_.refs_1_), custom_call_target="tpu_custom_call" | custom-call | tf_op jit(solution)/shard_map/pallas_call | solution.py:542
  406.9 8.9 %shard_map.365 = (bf16[320,1536]{1,0:T(8,128)(2,1)}, f32[1,1536]{1,0:T(1,128)}) custom-call(s32[3]{0:T(128)} %pad_add_fusion.info.refs_0_, bf16[320,2048]{1,0:T(8,128)(2,1)} %get-tuple-element.267.refs_2_.refs_1_, bf16[320,1536]{1,0:T(8,128)(2,1)} %bitcast.146, f32[1,1536]{1,0:T(1,128)} %broadcast_in_dim_reshape.7.refs_2_.refs_3_, ...), custom_call_target="tpu_custom_call" | custom-call | tf_op jit(solution)/shard_map/pallas_call | solution.py:542
  429.0 8.9 %collective-permute-done.50 = bf16[768,384]{1,0:T(8,128)(2,1)S(1)} collective-permute-done((bf16[768,384]{1,0:T(8,128)(2,1)S(1)}, bf16[768,384]{1,0:T(8,128)(2,1)S(1)}, u32[]{:S(2)}, u32[]{:S(2)}) %collective-permute-start.50) | collective-permute-done | bytes 589856 | tf_op jit(solution)/shard_map/out_dp/ppermute | solution.py:116
  456.3 6.8 %collective-permute-done.55 = bf16[192,384]{1,0:T(8,128)(2,1)S(1)} collective-permute-done((bf16[192,384]{1,0:T(8,128)(2,1)S(1)}, bf16[192,384]{1,0:T(8,128)(2,1)S(1)}, u32[]{:S(2)}, u32[]{:S(2)}) %collective-permute-start.55) | collective-permute-done | bytes 147488 | tf_op jit(solution)/shard_map/out_line/ppermute | solution.py:153
  464.4 9.7 %collective-permute-done.57 = bf16[192,384]{1,0:T(8,128)(2,1)S(1)} collective-permute-done((bf16[192,384]{1,0:T(8,128)(2,1)S(1)}, bf16[192,384]{1,0:T(8,128)(2,1)S(1)}, u32[]{:S(2)}, u32[]{:S(2)}) %collective-permute-start.57) | collective-permute-done | bytes 147488 | tf_op jit(solution)/shard_map/out_line/ppermute | solution.py:153
  474.1 7.8 %collective-permute-done.53 = bf16[1088,384]{1,0:T(8,128)(2,1)} collective-permute-done((bf16[1088,384]{1,0:T(8,128)(2,1)}, bf16[1088,384]{1,0:T(8,128)(2,1)}, u32[]{:S(2)}, u32[]{:S(2)}) %collective-permute-start.53) | collective-permute-done | bytes 835616 | tf_op jit(solution)/shard_map/qkv_dp/ppermute | solution.py:116
  490.0 6.0 %collective-permute-done.61 = bf16[384,576]{1,0:T(8,128)(2,1)S(1)} collective-permute-done((bf16[384,576]{1,0:T(8,128)(2,1)S(1)}, bf16[384,576]{1,0:T(8,128)(2,1)S(1)}, u32[]{:S(2)}, u32[]{:S(2)}) %collective-permute-start.61) | collective-permute-done | bytes 442400 | tf_op jit(solution)/shard_map/gradient_exchange/ppermute | solution.py:116
  496.7 10.1 %collective-permute-done.62 = bf16[384,576]{1,0:T(8,128)(2,1)S(1)} collective-permute-done((bf16[384,576]{1,0:T(8,128)(2,1)S(1)}, bf16[384,576]{1,0:T(8,128)(2,1)S(1)}, u32[]{:S(2)}, u32[]{:S(2)}) %collective-permute-start.62) | collective-permute-done | bytes 442400 | tf_op jit(solution)/shard_map/gradient_exchange/ppermute | solution.py:116
  572.8 6.4 %fusion.35 = (bf16[2240,192]{0,1:T(8,128)(2,1)}, f32[2240,192]{0,1:T(8,128)}, f32[2240,192]{0,1:T(8,128)}, f32[2240,192]{0,1:T(8,128)}) fusion(f32[2240,192]{0,1:T(8,128)S(1)} %copy-done.1, f32[]{:T(128)S(6)} %div.70, bf16[2240,192]{0,1:T(8,128)(2,1)} %copy.84, f32[2240,192]{0,1:T(8,128)} %param.31, f32[2240,192]{0,1:T(8,128)} %param.32), kind=kLoop, calls=%fused_computation.145 | loop fusion | flops 7311360 | bytes 12042244 | tf_op jit(solution)/shard_map/convert_element_type | solution.py:111
  (383 shorter events, 234.5 us)
Async XLA Ops:
  7.2 200.0 %all-gather.5.cloned.1.call-start = ((), (), s32[]{:S(2)}) async-start(), calls=%async_computation.3 | async-start | bytes 15925248 | tf_op jit(solution)/shard_map/all_gather | solution.py:1008
  12.5 29.8 %collective-permute-start.1 = (bf16[448,384]{0,1:T(8,128)(2,1)S(1)}, bf16[448,384]{0,1:T(8,128)(2,1)S(1)}, u32[]{:S(2)}, u32[]{:S(2)}) collective-permute-start(bf16[448,384]{0,1:T(8,128)(2,1)S(1)} %get-tuple-element.392), channel_id=1, source_target_pairs={{0,4},{1,5},{2,6},{3,7},{4,0},{5,1},{6,2},{7,3},{8,12},{9,13},{10,... | collective-permute-start | bytes 1032200 | tf_op jit(solution)/shard_map/matrix_line/ppermute | solution.py:153
  15.1 27.2 %collective-permute-start.2 = (bf16[448,384]{0,1:T(8,128)(2,1)S(1)}, bf16[448,384]{0,1:T(8,128)(2,1)S(1)}, u32[]{:S(2)}, u32[]{:S(2)}) collective-permute-start(bf16[448,384]{0,1:T(8,128)(2,1)S(1)} %get-tuple-element.392), channel_id=1, source_target_pairs={{0,6},{1,7},{2,4},{3,5},{4,2},{5,3},{6,0},{7,1},{8,14},{9,15},{10,... | collective-permute-start | bytes 1032200 | tf_op jit(solution)/shard_map/matrix_line/ppermute | solution.py:153
  23.0 32.4 %collective-permute-start.11 = (bf16[560,576]{1,0:T(8,128)(2,1)}, bf16[560,576]{1,0:T(8,128)(2,1)}, u32[]{:S(2)}, u32[]{:S(2)}) collective-permute-start(bf16[560,576]{1,0:T(8,128)(2,1)} %get-tuple-element.185), channel_id=1, source_target_pairs={{0,16},{8,24},{16,0},{24,8},{1,17},{9,25},{17,1},{25,9},{2,18},{10... | collective-permute-start | bytes 1935368 | tf_op jit(solution)/shard_map/weights_exchange/ppermute | solution.py:116
  29.3 26.1 %collective-permute-start.12 = (bf16[560,576]{1,0:T(8,128)(2,1)}, bf16[560,576]{1,0:T(8,128)(2,1)}, u32[]{:S(2)}, u32[]{:S(2)}) collective-permute-start(bf16[560,576]{1,0:T(8,128)(2,1)} %get-tuple-element.186), channel_id=1, source_target_pairs={{0,24},{8,16},{16,8},{24,0},{1,25},{9,17},{17,9},{25,1},{2,26},{10... | collective-permute-start | bytes 1935368 | tf_op jit(solution)/shard_map/weights_exchange/ppermute | solution.py:116
  59.5 217.2 %all-gather.3.cloned.1.call-start = ((), (), s32[]{:S(2)}) async-start(), calls=%async_computation.2 | async-start | bytes 7520256 | tf_op jit(solution)/shard_map/all_gather | solution.py:1008
  135.6 285.3 %reduce-scatter.3.cloned.1.call-start = ((), (), s32[]{:S(2)}) async-start(), calls=%async_computation.4 | async-start | bytes 15925248 | tf_op jit(solution)/shard_map/reduce_scatter | solution.py:1070
  139.2 25.4 %collective-permute-start.34 = (bf16[320,1536]{1,0:T(8,128)(2,1)}, bf16[320,1536]{1,0:T(8,128)(2,1)S(1)}, u32[]{:S(2)}, u32[]{:S(2)}) collective-permute-start(bf16[320,1536]{1,0:T(8,128)(2,1)} %bitcast_select_fusion.refs_4_.refs_2_), channel_id=1, source_target_pairs={{0,8},{8,0},{16,24},{24,16},{1,9},{9,1},{17,25},{25,17},{2,10},{10... | collective-permute-start | bytes 2949128 | tf_op jit(solution)/shard_map/cot_gather/ppermute | solution.py:116
  140.0 26.4 %collective-permute-start.35 = (bf16[320,1536]{1,0:T(8,128)(2,1)}, bf16[320,1536]{1,0:T(8,128)(2,1)}, u32[]{:S(2)}, u32[]{:S(2)}) collective-permute-start(bf16[320,1536]{1,0:T(8,128)(2,1)} %bitcast_select_fusion.refs_4_.refs_2_), channel_id=1, source_target_pairs={{0,16},{8,24},{16,0},{24,8},{1,17},{9,25},{17,1},{25,9},{2,18},{10... | collective-permute-start | bytes 2949128 | tf_op jit(solution)/shard_map/cot_gather/ppermute | solution.py:116
  162.9 24.9 %collective-permute-start.30 = (bf16[320,1536]{1,0:T(8,128)(2,1)}, bf16[320,1536]{1,0:T(8,128)(2,1)S(1)}, u32[]{:S(2)}, u32[]{:S(2)}) collective-permute-start(bf16[320,1536]{1,0:T(8,128)(2,1)} %get-tuple-element.206.refs_0_), channel_id=1, source_target_pairs={{0,8},{8,0},{16,24},{24,16},{1,9},{9,1},{17,25},{25,17},{2,10},{10... | collective-permute-start | bytes 2949128 | tf_op jit(solution)/shard_map/normed_gather/ppermute | solution.py:116
  164.3 24.9 %collective-permute-start.31 = (bf16[320,1536]{1,0:T(8,128)(2,1)}, bf16[320,1536]{1,0:T(8,128)(2,1)S(1)}, u32[]{:S(2)}, u32[]{:S(2)}) collective-permute-start(bf16[320,1536]{1,0:T(8,128)(2,1)} %get-tuple-element.206.refs_0_), channel_id=1, source_target_pairs={{0,16},{8,24},{16,0},{24,8},{1,17},{9,25},{17,1},{25,9},{2,18},{10... | collective-permute-start | bytes 2949128 | tf_op jit(solution)/shard_map/normed_gather/ppermute | solution.py:116
  164.7 35.1 %collective-permute-start.36 = (bf16[160,1536]{1,0:T(8,128)(2,1)S(1)}, bf16[160,1536]{1,0:T(8,128)(2,1)S(1)}, u32[]{:S(2)}, u32[]{:S(2)}) collective-permute-start(bf16[160,1536]{1,0:T(8,128)(2,1)S(1)} %slice.180), channel_id=1, source_target_pairs={{0,16},{8,24},{16,0},{24,8},{1,17},{9,25},{17,1},{25,9},{2,18},{10... | collective-permute-start | bytes 1474568 | tf_op jit(solution)/shard_map/cot_gather/ppermute | solution.py:116
  167.5 32.3 %collective-permute-start.37 = (bf16[160,1536]{1,0:T(8,128)(2,1)S(1)}, bf16[160,1536]{1,0:T(8,128)(2,1)S(1)}, u32[]{:S(2)}, u32[]{:S(2)}) collective-permute-start(bf16[160,1536]{1,0:T(8,128)(2,1)S(1)} %slice.181), channel_id=1, source_target_pairs={{0,8},{8,0},{16,24},{24,16},{1,9},{9,1},{17,25},{25,17},{2,10},{10... | collective-permute-start | bytes 1474568 | tf_op jit(solution)/shard_map/cot_gather/ppermute | solution.py:116
  276.5 240.5 %reduce-scatter.5.cloned.1.call-start = ((), (), s32[]{:S(2)}) async-start(), calls=%async_computation.5 | async-start | bytes 7520256 | tf_op jit(solution)/shard_map/reduce_scatter | solution.py:1176
  297.2 42.8 %collective-permute-start.39 = (bf16[320,1536]{1,0:T(8,128)(2,1)}, bf16[320,1536]{1,0:T(8,128)(2,1)S(1)}, u32[]{:S(2)}, u32[]{:S(2)}) collective-permute-start(bf16[320,1536]{1,0:T(8,128)(2,1)} %get-tuple-element.216), channel_id=1, source_target_pairs={{0,16},{8,24},{16,0},{24,8},{1,17},{9,25},{17,1},{25,9},{2,18},{10... | collective-permute-start | bytes 2949128 | tf_op jit(solution)/shard_map/back_reduce/ppermute | solution.py:116
  297.3 42.8 %collective-permute-start.40 = (bf16[320,1536]{1,0:T(8,128)(2,1)}, bf16[320,1536]{1,0:T(8,128)(2,1)S(1)}, u32[]{:S(2)}, u32[]{:S(2)}) collective-permute-start(bf16[320,1536]{1,0:T(8,128)(2,1)} %get-tuple-element.217), channel_id=1, source_target_pairs={{0,24},{8,16},{16,8},{24,0},{1,25},{9,17},{17,9},{25,1},{2,26},{10... | collective-permute-start | bytes 2949128 | tf_op jit(solution)/shard_map/back_reduce/ppermute | solution.py:116
  341.1 32.1 %collective-permute-start.41 = (bf16[320,1536]{1,0:T(8,128)(2,1)}, bf16[320,1536]{1,0:T(8,128)(2,1)S(1)}, u32[]{:S(2)}, u32[]{:S(2)}) collective-permute-start(bf16[320,1536]{1,0:T(8,128)(2,1)} %get-tuple-element.245), channel_id=1, source_target_pairs={{0,8},{8,0},{16,24},{24,16},{1,9},{9,1},{17,25},{25,17},{2,10},{10... | collective-permute-start | bytes 2949128 | tf_op jit(solution)/shard_map/mixed_reduce/ppermute | solution.py:116
  342.3 30.9 %collective-permute-start.42 = (bf16[320,1536]{1,0:T(8,128)(2,1)S(1)}, bf16[320,1536]{1,0:T(8,128)(2,1)S(1)}, u32[]{:S(2)}, u32[]{:S(2)}) collective-permute-start(bf16[320,1536]{1,0:T(8,128)(2,1)S(1)} %copy-done.52), channel_id=1, source_target_pairs={{0,16},{8,24},{16,0},{24,8},{1,17},{9,25},{17,1},{25,9},{2,18},{10... | collective-permute-start | bytes 2949128 | tf_op jit(solution)/shard_map/mixed_reduce/ppermute | solution.py:116
  443.2 30.9 %collective-permute-start.54 = (bf16[1088,384]{1,0:T(8,128)(2,1)}, bf16[1088,384]{1,0:T(8,128)(2,1)}, u32[]{:S(2)}, u32[]{:S(2)}) collective-permute-start(bf16[1088,384]{1,0:T(8,128)(2,1)} %bitcast.51), channel_id=1, source_target_pairs={{0,24},{8,16},{16,8},{24,0},{1,25},{9,17},{17,9},{25,1},{2,26},{10... | collective-permute-start | bytes 2506760 | tf_op jit(solution)/shard_map/qkv_dp/ppermute | solution.py:116
  446.6 35.3 %collective-permute-start.53 = (bf16[1088,384]{1,0:T(8,128)(2,1)}, bf16[1088,384]{1,0:T(8,128)(2,1)}, u32[]{:S(2)}, u32[]{:S(2)}) collective-permute-start(bf16[1088,384]{1,0:T(8,128)(2,1)} %bitcast.48), channel_id=1, source_target_pairs={{0,16},{8,24},{16,0},{24,8},{1,17},{9,25},{17,1},{25,9},{2,18},{10... | collective-permute-start | bytes 2506760 | tf_op jit(solution)/shard_map/qkv_dp/ppermute | solution.py:116
  448.1 33.8 %collective-permute-start.52 = (bf16[1088,384]{1,0:T(8,128)(2,1)}, bf16[1088,384]{1,0:T(8,128)(2,1)}, u32[]{:S(2)}, u32[]{:S(2)}) collective-permute-start(bf16[1088,384]{1,0:T(8,128)(2,1)} %bitcast.45), channel_id=1, source_target_pairs={{0,8},{8,0},{16,24},{24,16},{1,9},{9,1},{17,25},{25,17},{2,10},{10... | collective-permute-start | bytes 2506760 | tf_op jit(solution)/shard_map/qkv_dp/ppermute | solution.py:116
  483.4 23.4 %collective-permute-start.62 = (bf16[384,576]{1,0:T(8,128)(2,1)S(1)}, bf16[384,576]{1,0:T(8,128)(2,1)S(1)}, u32[]{:S(2)}, u32[]{:S(2)}) collective-permute-start(bf16[384,576]{1,0:T(8,128)(2,1)S(1)} %copy-done.56), channel_id=1, source_target_pairs={{0,16},{8,24},{16,0},{24,8},{1,17},{9,25},{17,1},{25,9},{2,18},{10... | collective-permute-start | bytes 1327112 | tf_op jit(solution)/shard_map/gradient_exchange/ppermute | solution.py:116
  488.3 23.4 %collective-permute-start.58 = (bf16[272,384]{1,0:T(8,128)(2,1)}, bf16[272,384]{1,0:T(8,128)(2,1)S(1)}, u32[]{:S(2)}, u32[]{:S(2)}) collective-permute-start(bf16[272,384]{1,0:T(8,128)(2,1)} %get-tuple-element.379), channel_id=1, source_target_pairs={{0,2},{1,3},{2,0},{3,1},{4,6},{5,7},{6,4},{7,5},{8,10},{9,11},{10,... | collective-permute-start | bytes 626696 | tf_op jit(solution)/shard_map/qkv_line/ppermute | solution.py:153
  506.7 26.0 %collective-permute-start.65 = (bf16[320,1536]{1,0:T(8,128)(2,1)}, bf16[320,1536]{1,0:T(8,128)(2,1)}, u32[]{:S(2)}, u32[]{:S(2)}) collective-permute-start(bf16[320,1536]{1,0:T(8,128)(2,1)} %get-tuple-element.323), channel_id=1, source_target_pairs={{0,24},{8,16},{16,8},{24,0},{1,25},{9,17},{17,9},{25,1},{2,26},{10... | collective-permute-start | bytes 2949128 | tf_op jit(solution)/shard_map/mixed_reduce/ppermute | solution.py:116
  (114 other events, 1332.4 us)
Sparse Core Ops, SparseCore 0:
  59.7 129.8 all-gather.4
  191.8 66.2 all-gather.2
  276.6 144.1 reduce-scatter.2
  423.0 92.3 reduce-scatter.4

commit v6 on v5

--- a/solution.py
+++ b/solution.py
@@ -1017,9 +1017,11 @@
         [vmem_f32(rows, QKV)],
         7,
     )
+    kv_near = scoped("kv_gather", gather_near, kv)
     kv, out_near = lax.optimization_barrier((kv, out_near))
+    kv_near, out_near = lax.optimization_barrier((kv_near, out_near))
     out_own = scoped("out_gather", gather_far, out_near)
-    kv_blocks = scoped("kv_gather", dp_gather, kv)
+    kv_blocks = scoped("kv_gather", gather_far, kv_near)
     out_other = scoped("out_swap", core_swap, jnp.stack(out_own))
 
     valid = query_places < lengths[0]

time: 606 us -> 603 us (level)
  transfers between devices with their start and end apart: 79 -> 79, of which waited for: 39 -> 41; matrix products, arithmetic and copies ran while one was open for 7% -> 8% of each run, Pallas kernels for 38% -> 38%
where the time goes in v6:
time: 603 us; the launch traced here: 594 us
  Pallas kernels  232 us (38%)
  waiting for transfers between devices  180 us (30%)
  starting transfers between devices  87.7 us (15%)
  other arithmetic  46.8 us (8%)
  local copies, waits for them, and re-layouts  24.2 us (4%)
  between operations  24 us (4%)
    ppermute x50, waiting for transfers between devices, dp_send(): return lax.ppermute(block, 'dp', [(i, i ^ k) for i in range(count)])  131 us
    pallas_call x4, Pallas kernels, hbm_call(): pl.pallas_call(kernel, out_shape=tuple(outs), in_specs=[anywhere] * len(a...  125 us
    pallas_call x12, Pallas kernels, call(): pl.pallas_call(kernel, out_shape=tuple(outs), in_specs=[pl.BlockSpec(memo...  107 us
    ppermute x50, starting transfers between devices, dp_send(): return lax.ppermute(block, 'dp', [(i, i ^ k) for i in range(count)])  61.8 us
    ppermute x15, waiting for transfers between devices, line_send(): return lax.ppermute(block, 'fsdp', [(i, i ^ 2 * r) for i in range(count)])  42.2 us
    ppermute x15, starting transfers between devices, line_send(): return lax.ppermute(block, 'fsdp', [(i, i ^ 2 * r) for i in range(count)])  23.4 us
    convert_element_type x5, other arithmetic, update(): return (weight_new, first_new, second_new, weight_new.astype(jnp.bfloat16))  15.1 us
  transfers between devices with their start and end apart: 79, of which 41 were waited for; matrix products, arithmetic and copies ran while one was open for 8% of the time, Pallas kernels for 38%

profile of v6, /device:TPU:0, one launch (start us, length us, event | category | flops | bytes accessed | tf_op | source)
XLA Modules:
  0.0 594.4 jit_solution(7313663603216472513)
XLA Ops:
  31.9 10.4 %collective-permute-done.1 = bf16[448,384]{0,1:T(8,128)(2,1)S(1)} collective-permute-done((bf16[448,384]{0,1:T(8,128)(2,1)S(1)}, bf16[448,384]{0,1:T(8,128)(2,1)S(1)}, u32[]{:S(2)}, u32[]{:S(2)}) %collective-permute-start.1) | collective-permute-done | bytes 344096 | tf_op jit(solution)/shard_map/matrix_line/ppermute | solution.py:153
  43.8 11.6 %collective-permute-done.11.refs_2_ = bf16[560,576]{1,0:T(8,128)(2,1)} collective-permute-done((bf16[560,576]{1,0:T(8,128)(2,1)}, bf16[560,576]{1,0:T(8,128)(2,1)}, u32[]{:S(2)}, u32[]{:S(2)}) %collective-permute-start.11) | collective-permute-done | bytes 645152 | tf_op jit(solution)/shard_map/weights_exchange/ppermute | solution.py:116
  95.9 7.6 %shard_map.354 = (bf16[320,1536]{1,0:T(8,128)(2,1)}, bf16[320,1536]{1,0:T(8,128)(2,1)}, bf16[320,512]{1,0:T(8,128)(2,1)}) custom-call(s32[3]{0:T(128)} %pad_add_fusion.info.refs_0_, bf16[320,1536]{1,0:T(8,128)(2,1)} %bitcast.144, f32[1,1536]{1,0:T(1,128)} %broadcast_in_dim_reshape.7.refs_2_.refs_3_, f32[1,2048]{1,0:T(1,128)} %bitcast.160, ...), custom_call_target="tpu_custom_call" | custom-call | flops 8049999872 | bytes 9910284 | tf_op jit(solution)/shard_map/pallas_call | solution.py:542
  118.6 5.9 collective-permute-done.27
  137.8 21.2 %shard_map.355 = (bf16[320,1536]{1,0:T(8,128)(2,1)}, f32[16,320]{1,0:T(8,128)}, f32[320,1536]{1,0:T(8,128)}, bf16[320,1536]{1,0:T(8,128)(2,1)}) custom-call(s32[3]{0:T(128)} %pad_add_fusion.info.refs_0_, bf16[320,1536]{1,0:T(8,128)(2,1)} %bitcast.145, f32[1,1536]{1,0:T(1,128)} %broadcast_in_dim_reshape.6.refs_2_.refs_3_, ...), custom_call_target="tpu_custom_call" | custom-call | flops 27599998976 | bytes 11954188 | tf_op jit(solution)/shard_map/pallas_call | solution.py:542
  164.3 19.6 %collective-permute-done.30.refs_1_ = bf16[320,1536]{1,0:T(8,128)(2,1)S(1)} collective-permute-done((bf16[320,1536]{1,0:T(8,128)(2,1)}, bf16[320,1536]{1,0:T(8,128)(2,1)S(1)}, u32[]{:S(2)}, u32[]{:S(2)}) %collective-permute-start.30) | collective-permute-done | bytes 983072 | tf_op jit(solution)/shard_map/normed_gather/ppermute | solution.py:116
  186.0 9.8 %collective-permute-done.36 = bf16[160,1536]{1,0:T(8,128)(2,1)S(1)} collective-permute-done((bf16[160,1536]{1,0:T(8,128)(2,1)S(1)}, bf16[160,1536]{1,0:T(8,128)(2,1)S(1)}, u32[]{:S(2)}, u32[]{:S(2)}) %collective-permute-start.36) | collective-permute-done | bytes 491552 | tf_op jit(solution)/shard_map/cot_gather/ppermute | solution.py:116
  195.9 8.0 %collective-permute-done.32 = bf16[160,1536]{1,0:T(8,128)(2,1)S(1)} collective-permute-done((bf16[160,1536]{1,0:T(8,128)(2,1)S(1)}, bf16[160,1536]{1,0:T(8,128)(2,1)S(1)}, u32[]{:S(2)}, u32[]{:S(2)}) %collective-permute-start.32) | collective-permute-done | bytes 491552 | tf_op jit(solution)/shard_map/normed_gather/ppermute | solution.py:116
  205.0 68.4 %shard_map.357 = (f32[1280,1536]{1,0:T(8,128)}, f32[1280,1536]{1,0:T(8,128)}, bf16[4608,1536]{1,0:T(8,128)(2,1)}) custom-call(bf16[320,1536]{1,0:T(8,128)(2,1)} %get-tuple-element.216.refs_0_, bf16[320,1536]{1,0:T(8,128)(2,1)} %copy-done.36, bf16[320,1536]{1,0:T(8,128)(2,1)} %copy-done.37, bf16[320,1536]{1,0:T(8,128)(2,1)} %copy-done.39, ...), custom_call_target="tpu_custom_call" | custom-call | flops 78199996416 | bytes 51904512 | tf_op jit(solution)/shard_map/pallas_call | solution.py:844
  273.7 20.4 %shard_map.358 = (bf16[320,1536]{1,0:T(8,128)(2,1)}, bf16[320,1536]{1,0:T(8,128)(2,1)}, bf16[320,1536]{1,0:T(8,128)(2,1)}, bf16[320,1536]{1,0:T(8,128)(2,1)}, bf...) custom-call(bf16[320,1536]{1,0:T(8,128)(2,1)} %copy-done.37, ...), custom_call_target="tpu_custom_call" | custom-call | flops 23000000512 | bytes 32980992 | tf_op jit(solution)/shard_map/pallas_call | solution.py:844
  295.9 20.6 %shard_map.359 = (bf16[320,1536]{1,0:T(8,128)(2,1)}, bf16[320,1536]{1,0:T(8,128)(2,1)}, bf16[320,1536]{1,0:T(8,128)(2,1)}, bf16[320,1536]{1,0:T(8,128)(2,1)}, bf...) custom-call(bf16[320,1536]{1,0:T(8,128)(2,1)} %get-tuple-element.216.refs_0_, ...), custom_call_target="tpu_custom_call" | custom-call | flops 23000000512 | bytes 32980992 | tf_op jit(solution)/shard_map/pallas_call | solution.py:844
  318.3 16.0 %shard_map.360 = bf16[2176,1536]{1,0:T(8,128)(2,1)} custom-call(bf16[320,1536]{1,0:T(8,128)(2,1)} %get-tuple-element.216.refs_0_, bf16[320,1536]{1,0:T(8,128)(2,1)} %copy-done.36, bf16[320,1536]{1,0:T(8,128)(2,1)} %copy-done.37, bf16[320,1536]{1,0:T(8,128)(2,1)} %copy-done.39, bf16[320,1536]{1,0:T(8,128)(2,1)} %bitcast_select_fusion.refs_4_.refs_2_, ...), custom_call_target="tpu_custom_call" | custom-call | flops 18400000000 | bytes 19955712 | tf_op jit(solution)/shard_map/pallas_call | solution.py:844
  340.8 30.4 %shard_map.361 = (f32[320,1536]{1,0:T(8,128)}, bf16[320,1536]{1,0:T(8,128)(2,1)}, f32[1,1536]{1,0:T(1,128)}, f32[320,1536]{1,0:T(8,128)}, bf16[320,512]{1,0:T(8,...) custom-call(s32[3]{0:T(128)} %pad_add_fusion.info.refs_0_, ...), custom_call_target="tpu_custom_call" | custom-call | flops 35649998848 | bytes 20152332 | tf_op jit(solution)/shard_map/pallas_call | solution.py:542
  374.8 7.2 %shard_map.362 = (bf16[4,768,384]{2,1,0:T(8,128)(2,1)}, bf16[4,768,384]{2,1,0:T(8,128)(2,1)}) custom-call(s32[3]{0:T(128)} %pad_add_fusion.info.refs_0_, bf16[320,1536]{1,0:T(8,128)(2,1)} %get-tuple-element.261.refs_1_, bf16[320,1536]{1,0:T(8,128)(2,1)} %get-tuple-element.262.refs_2_), custom_call_target="tpu_custom_call" | custom-call | tf_op jit(solution)/shard_map/pallas_call | solution.py:542
  395.7 8.7 %shard_map.364 = (bf16[4,1024,384]{2,1,0:T(8,128)(2,1)}, bf16[4,1024,384]{2,1,0:T(8,128)(2,1)}) custom-call(s32[3]{0:T(128)} %pad_add_fusion.info.refs_0_, bf16[320,1536]{1,0:T(8,128)(2,1)} %get-tuple-element.243.refs_1_, bf16[320,2048]{1,0:T(8,128)(2,1)} %get-tuple-element.277.refs_2_.refs_1_), custom_call_target="tpu_custom_call" | custom-call | tf_op jit(solution)/shard_map/pallas_call | solution.py:542
  404.3 8.9 %shard_map.365 = (bf16[320,1536]{1,0:T(8,128)(2,1)}, f32[1,1536]{1,0:T(1,128)}) custom-call(s32[3]{0:T(128)} %pad_add_fusion.info.refs_0_, bf16[320,2048]{1,0:T(8,128)(2,1)} %get-tuple-element.277.refs_2_.refs_1_, bf16[320,1536]{1,0:T(8,128)(2,1)} %bitcast.146, f32[1,1536]{1,0:T(1,128)} %broadcast_in_dim_reshape.7.refs_2_.refs_3_, ...), custom_call_target="tpu_custom_call" | custom-call | tf_op jit(solution)/shard_map/pallas_call | solution.py:542
  426.0 8.8 %collective-permute-done.50 = bf16[768,384]{1,0:T(8,128)(2,1)S(1)} collective-permute-done((bf16[768,384]{1,0:T(8,128)(2,1)S(1)}, bf16[768,384]{1,0:T(8,128)(2,1)S(1)}, u32[]{:S(2)}, u32[]{:S(2)}) %collective-permute-start.50) | collective-permute-done | bytes 589856 | tf_op jit(solution)/shard_map/out_dp/ppermute | solution.py:116
  453.3 6.8 %collective-permute-done.55 = bf16[192,384]{1,0:T(8,128)(2,1)S(1)} collective-permute-done((bf16[192,384]{1,0:T(8,128)(2,1)S(1)}, bf16[192,384]{1,0:T(8,128)(2,1)S(1)}, u32[]{:S(2)}, u32[]{:S(2)}) %collective-permute-start.55) | collective-permute-done | bytes 147488 | tf_op jit(solution)/shard_map/out_line/ppermute | solution.py:153
  461.4 9.7 %collective-permute-done.57 = bf16[192,384]{1,0:T(8,128)(2,1)S(1)} collective-permute-done((bf16[192,384]{1,0:T(8,128)(2,1)S(1)}, bf16[192,384]{1,0:T(8,128)(2,1)S(1)}, u32[]{:S(2)}, u32[]{:S(2)}) %collective-permute-start.57) | collective-permute-done | bytes 147488 | tf_op jit(solution)/shard_map/out_line/ppermute | solution.py:153
  471.1 7.8 %collective-permute-done.53 = bf16[1088,384]{1,0:T(8,128)(2,1)} collective-permute-done((bf16[1088,384]{1,0:T(8,128)(2,1)}, bf16[1088,384]{1,0:T(8,128)(2,1)}, u32[]{:S(2)}, u32[]{:S(2)}) %collective-permute-start.53) | collective-permute-done | bytes 835616 | tf_op jit(solution)/shard_map/qkv_dp/ppermute | solution.py:116
  487.0 6.0 %collective-permute-done.61 = bf16[384,576]{1,0:T(8,128)(2,1)S(1)} collective-permute-done((bf16[384,576]{1,0:T(8,128)(2,1)S(1)}, bf16[384,576]{1,0:T(8,128)(2,1)S(1)}, u32[]{:S(2)}, u32[]{:S(2)}) %collective-permute-start.61) | collective-permute-done | bytes 442400 | tf_op jit(solution)/shard_map/gradient_exchange/ppermute | solution.py:116
  493.7 10.0 %collective-permute-done.62 = bf16[384,576]{1,0:T(8,128)(2,1)S(1)} collective-permute-done((bf16[384,576]{1,0:T(8,128)(2,1)S(1)}, bf16[384,576]{1,0:T(8,128)(2,1)S(1)}, u32[]{:S(2)}, u32[]{:S(2)}) %collective-permute-start.62) | collective-permute-done | bytes 442400 | tf_op jit(solution)/shard_map/gradient_exchange/ppermute | solution.py:116
  570.1 6.4 %fusion.35 = (bf16[2240,192]{0,1:T(8,128)(2,1)}, f32[2240,192]{0,1:T(8,128)}, f32[2240,192]{0,1:T(8,128)}, f32[2240,192]{0,1:T(8,128)}) fusion(f32[2240,192]{0,1:T(8,128)S(1)} %copy-done.1, f32[]{:T(128)S(6)} %div.70, bf16[2240,192]{0,1:T(8,128)(2,1)} %copy.84, f32[2240,192]{0,1:T(8,128)} %param.31, f32[2240,192]{0,1:T(8,128)} %param.32), kind=kLoop, calls=%fused_computation.145 | loop fusion | flops 7311360 | bytes 12042244 | tf_op jit(solution)/shard_map/convert_element_type | solution.py:111
  577.6 5.7 fusion.37
  (381 shorter events, 234.5 us)
Async XLA Ops:
  7.2 196.9 %all-gather.5.cloned.1.call-start = ((), (), s32[]{:S(2)}) async-start(), calls=%async_computation.3 | async-start | bytes 15925248 | tf_op jit(solution)/shard_map/all_gather | solution.py:1008
  12.5 29.8 %collective-permute-start.1 = (bf16[448,384]{0,1:T(8,128)(2,1)S(1)}, bf16[448,384]{0,1:T(8,128)(2,1)S(1)}, u32[]{:S(2)}, u32[]{:S(2)}) collective-permute-start(bf16[448,384]{0,1:T(8,128)(2,1)S(1)} %get-tuple-element.402), channel_id=1, source_target_pairs={{0,4},{1,5},{2,6},{3,7},{4,0},{5,1},{6,2},{7,3},{8,12},{9,13},{10,... | collective-permute-start | bytes 1032200 | tf_op jit(solution)/shard_map/matrix_line/ppermute | solution.py:153
  15.1 27.2 %collective-permute-start.2 = (bf16[448,384]{0,1:T(8,128)(2,1)S(1)}, bf16[448,384]{0,1:T(8,128)(2,1)S(1)}, u32[]{:S(2)}, u32[]{:S(2)}) collective-permute-start(bf16[448,384]{0,1:T(8,128)(2,1)S(1)} %get-tuple-element.402), channel_id=1, source_target_pairs={{0,6},{1,7},{2,4},{3,5},{4,2},{5,3},{6,0},{7,1},{8,14},{9,15},{10,... | collective-permute-start | bytes 1032200 | tf_op jit(solution)/shard_map/matrix_line/ppermute | solution.py:153
  23.0 32.4 %collective-permute-start.11 = (bf16[560,576]{1,0:T(8,128)(2,1)}, bf16[560,576]{1,0:T(8,128)(2,1)}, u32[]{:S(2)}, u32[]{:S(2)}) collective-permute-start(bf16[560,576]{1,0:T(8,128)(2,1)} %get-tuple-element.190), channel_id=1, source_target_pairs={{0,16},{8,24},{16,0},{24,8},{1,17},{9,25},{17,1},{25,9},{2,18},{10... | collective-permute-start | bytes 1935368 | tf_op jit(solution)/shard_map/weights_exchange/ppermute | solution.py:116
  29.3 26.1 %collective-permute-start.12 = (bf16[560,576]{1,0:T(8,128)(2,1)}, bf16[560,576]{1,0:T(8,128)(2,1)}, u32[]{:S(2)}, u32[]{:S(2)}) collective-permute-start(bf16[560,576]{1,0:T(8,128)(2,1)} %get-tuple-element.191), channel_id=1, source_target_pairs={{0,24},{8,16},{16,8},{24,0},{1,25},{9,17},{17,9},{25,1},{2,26},{10... | collective-permute-start | bytes 1935368 | tf_op jit(solution)/shard_map/weights_exchange/ppermute | solution.py:116
  59.5 214.2 %all-gather.3.cloned.1.call-start = ((), (), s32[]{:S(2)}) async-start(), calls=%async_computation.2 | async-start | bytes 7520256 | tf_op jit(solution)/shard_map/all_gather | solution.py:1008
  131.1 286.8 %reduce-scatter.3.cloned.1.call-start = ((), (), s32[]{:S(2)}) async-start(), calls=%async_computation.4 | async-start | bytes 15925248 | tf_op jit(solution)/shard_map/reduce_scatter | solution.py:1072
  135.4 25.2 %collective-permute-start.34 = (bf16[320,1536]{1,0:T(8,128)(2,1)}, bf16[320,1536]{1,0:T(8,128)(2,1)S(1)}, u32[]{:S(2)}, u32[]{:S(2)}) collective-permute-start(bf16[320,1536]{1,0:T(8,128)(2,1)} %bitcast_select_fusion.refs_4_.refs_2_), channel_id=1, source_target_pairs={{0,8},{8,0},{16,24},{24,16},{1,9},{9,1},{17,25},{25,17},{2,10},{10... | collective-permute-start | bytes 2949128 | tf_op jit(solution)/shard_map/cot_gather/ppermute | solution.py:116
  136.2 26.3 %collective-permute-start.35 = (bf16[320,1536]{1,0:T(8,128)(2,1)}, bf16[320,1536]{1,0:T(8,128)(2,1)}, u32[]{:S(2)}, u32[]{:S(2)}) collective-permute-start(bf16[320,1536]{1,0:T(8,128)(2,1)} %bitcast_select_fusion.refs_4_.refs_2_), channel_id=1, source_target_pairs={{0,16},{8,24},{16,0},{24,8},{1,17},{9,25},{17,1},{25,9},{2,18},{10... | collective-permute-start | bytes 2949128 | tf_op jit(solution)/shard_map/cot_gather/ppermute | solution.py:116
  159.0 24.9 %collective-permute-start.30 = (bf16[320,1536]{1,0:T(8,128)(2,1)}, bf16[320,1536]{1,0:T(8,128)(2,1)S(1)}, u32[]{:S(2)}, u32[]{:S(2)}) collective-permute-start(bf16[320,1536]{1,0:T(8,128)(2,1)} %get-tuple-element.216.refs_0_), channel_id=1, source_target_pairs={{0,8},{8,0},{16,24},{24,16},{1,9},{9,1},{17,25},{25,17},{2,10},{10... | collective-permute-start | bytes 2949128 | tf_op jit(solution)/shard_map/normed_gather/ppermute | solution.py:116
  160.4 24.9 %collective-permute-start.31 = (bf16[320,1536]{1,0:T(8,128)(2,1)}, bf16[320,1536]{1,0:T(8,128)(2,1)S(1)}, u32[]{:S(2)}, u32[]{:S(2)}) collective-permute-start(bf16[320,1536]{1,0:T(8,128)(2,1)} %get-tuple-element.216.refs_0_), channel_id=1, source_target_pairs={{0,16},{8,24},{16,0},{24,8},{1,17},{9,25},{17,1},{25,9},{2,18},{10... | collective-permute-start | bytes 2949128 | tf_op jit(solution)/shard_map/normed_gather/ppermute | solution.py:116
  160.7 35.1 %collective-permute-start.36 = (bf16[160,1536]{1,0:T(8,128)(2,1)S(1)}, bf16[160,1536]{1,0:T(8,128)(2,1)S(1)}, u32[]{:S(2)}, u32[]{:S(2)}) collective-permute-start(bf16[160,1536]{1,0:T(8,128)(2,1)S(1)} %slice.178), channel_id=1, source_target_pairs={{0,16},{8,24},{16,0},{24,8},{1,17},{9,25},{17,1},{25,9},{2,18},{10... | collective-permute-start | bytes 1474568 | tf_op jit(solution)/shard_map/cot_gather/ppermute | solution.py:116
  163.6 32.2 %collective-permute-start.37 = (bf16[160,1536]{1,0:T(8,128)(2,1)S(1)}, bf16[160,1536]{1,0:T(8,128)(2,1)S(1)}, u32[]{:S(2)}, u32[]{:S(2)}) collective-permute-start(bf16[160,1536]{1,0:T(8,128)(2,1)S(1)} %slice.179), channel_id=1, source_target_pairs={{0,8},{8,0},{16,24},{24,16},{1,9},{9,1},{17,25},{25,17},{2,10},{10... | collective-permute-start | bytes 1474568 | tf_op jit(solution)/shard_map/cot_gather/ppermute | solution.py:116
  273.5 240.5 %reduce-scatter.5.cloned.1.call-start = ((), (), s32[]{:S(2)}) async-start(), calls=%async_computation.5 | async-start | bytes 7520256 | tf_op jit(solution)/shard_map/reduce_scatter | solution.py:1178
  294.1 43.8 %collective-permute-start.39 = (bf16[320,1536]{1,0:T(8,128)(2,1)}, bf16[320,1536]{1,0:T(8,128)(2,1)S(1)}, u32[]{:S(2)}, u32[]{:S(2)}) collective-permute-start(bf16[320,1536]{1,0:T(8,128)(2,1)} %get-tuple-element.226), channel_id=1, source_target_pairs={{0,16},{8,24},{16,0},{24,8},{1,17},{9,25},{17,1},{25,9},{2,18},{10... | collective-permute-start | bytes 2949128 | tf_op jit(solution)/shard_map/back_reduce/ppermute | solution.py:116
  294.3 43.6 %collective-permute-start.40 = (bf16[320,1536]{1,0:T(8,128)(2,1)}, bf16[320,1536]{1,0:T(8,128)(2,1)S(1)}, u32[]{:S(2)}, u32[]{:S(2)}) collective-permute-start(bf16[320,1536]{1,0:T(8,128)(2,1)} %get-tuple-element.227), channel_id=1, source_target_pairs={{0,24},{8,16},{16,8},{24,0},{1,25},{9,17},{17,9},{25,1},{2,26},{10... | collective-permute-start | bytes 2949128 | tf_op jit(solution)/shard_map/back_reduce/ppermute | solution.py:116
  338.9 32.3 %collective-permute-start.41 = (bf16[320,1536]{1,0:T(8,128)(2,1)}, bf16[320,1536]{1,0:T(8,128)(2,1)S(1)}, u32[]{:S(2)}, u32[]{:S(2)}) collective-permute-start(bf16[320,1536]{1,0:T(8,128)(2,1)} %get-tuple-element.255), channel_id=1, source_target_pairs={{0,8},{8,0},{16,24},{24,16},{1,9},{9,1},{17,25},{25,17},{2,10},{10... | collective-permute-start | bytes 2949128 | tf_op jit(solution)/shard_map/mixed_reduce/ppermute | solution.py:116
  340.1 31.1 %collective-permute-start.42 = (bf16[320,1536]{1,0:T(8,128)(2,1)S(1)}, bf16[320,1536]{1,0:T(8,128)(2,1)S(1)}, u32[]{:S(2)}, u32[]{:S(2)}) collective-permute-start(bf16[320,1536]{1,0:T(8,128)(2,1)S(1)} %copy-done.52), channel_id=1, source_target_pairs={{0,16},{8,24},{16,0},{24,8},{1,17},{9,25},{17,1},{25,9},{2,18},{10... | collective-permute-start | bytes 2949128 | tf_op jit(solution)/shard_map/mixed_reduce/ppermute | solution.py:116
  440.2 30.9 %collective-permute-start.54 = (bf16[1088,384]{1,0:T(8,128)(2,1)}, bf16[1088,384]{1,0:T(8,128)(2,1)}, u32[]{:S(2)}, u32[]{:S(2)}) collective-permute-start(bf16[1088,384]{1,0:T(8,128)(2,1)} %bitcast.51), channel_id=1, source_target_pairs={{0,24},{8,16},{16,8},{24,0},{1,25},{9,17},{17,9},{25,1},{2,26},{10... | collective-permute-start | bytes 2506760 | tf_op jit(solution)/shard_map/qkv_dp/ppermute | solution.py:116
  443.6 35.3 %collective-permute-start.53 = (bf16[1088,384]{1,0:T(8,128)(2,1)}, bf16[1088,384]{1,0:T(8,128)(2,1)}, u32[]{:S(2)}, u32[]{:S(2)}) collective-permute-start(bf16[1088,384]{1,0:T(8,128)(2,1)} %bitcast.48), channel_id=1, source_target_pairs={{0,16},{8,24},{16,0},{24,8},{1,17},{9,25},{17,1},{25,9},{2,18},{10... | collective-permute-start | bytes 2506760 | tf_op jit(solution)/shard_map/qkv_dp/ppermute | solution.py:116
  445.1 33.8 %collective-permute-start.52 = (bf16[1088,384]{1,0:T(8,128)(2,1)}, bf16[1088,384]{1,0:T(8,128)(2,1)}, u32[]{:S(2)}, u32[]{:S(2)}) collective-permute-start(bf16[1088,384]{1,0:T(8,128)(2,1)} %bitcast.45), channel_id=1, source_target_pairs={{0,8},{8,0},{16,24},{24,16},{1,9},{9,1},{17,25},{25,17},{2,10},{10... | collective-permute-start | bytes 2506760 | tf_op jit(solution)/shard_map/qkv_dp/ppermute | solution.py:116
  480.4 23.3 %collective-permute-start.62 = (bf16[384,576]{1,0:T(8,128)(2,1)S(1)}, bf16[384,576]{1,0:T(8,128)(2,1)S(1)}, u32[]{:S(2)}, u32[]{:S(2)}) collective-permute-start(bf16[384,576]{1,0:T(8,128)(2,1)S(1)} %copy-done.56), channel_id=1, source_target_pairs={{0,16},{8,24},{16,0},{24,8},{1,17},{9,25},{17,1},{25,9},{2,18},{10... | collective-permute-start | bytes 1327112 | tf_op jit(solution)/shard_map/gradient_exchange/ppermute | solution.py:116
  485.4 23.4 %collective-permute-start.58 = (bf16[272,384]{1,0:T(8,128)(2,1)}, bf16[272,384]{1,0:T(8,128)(2,1)S(1)}, u32[]{:S(2)}, u32[]{:S(2)}) collective-permute-start(bf16[272,384]{1,0:T(8,128)(2,1)} %get-tuple-element.389), channel_id=1, source_target_pairs={{0,2},{1,3},{2,0},{3,1},{4,6},{5,7},{6,4},{7,5},{8,10},{9,11},{10,... | collective-permute-start | bytes 626696 | tf_op jit(solution)/shard_map/qkv_line/ppermute | solution.py:153
  503.8 26.0 %collective-permute-start.65 = (bf16[320,1536]{1,0:T(8,128)(2,1)}, bf16[320,1536]{1,0:T(8,128)(2,1)}, u32[]{:S(2)}, u32[]{:S(2)}) collective-permute-start(bf16[320,1536]{1,0:T(8,128)(2,1)} %get-tuple-element.333), channel_id=1, source_target_pairs={{0,24},{8,16},{16,8},{24,0},{1,25},{9,17},{17,9},{25,1},{2,26},{10... | collective-permute-start | bytes 2949128 | tf_op jit(solution)/shard_map/mixed_reduce/ppermute | solution.py:116
  (113 other events, 1349.1 us)
Sparse Core Ops, SparseCore 0:
  59.7 129.8 all-gather.4
  191.8 66.2 all-gather.2
  273.6 144.2 reduce-scatter.2
  420.0 92.3 reduce-scatter.4
